TPU v7x, 128 devices: a whole 4x4x4 slice. The times are simulated.
128 devices in a mesh: struct: 4 (over x), fluid: 32 (over z, y, core).
Axes of the slice: x: 4, y: 4, z: 4, core: 2. Of those that a mesh axis runs over, the one named last changes fastest.
Arguments:
- shell_motion: float32 [3, 1048576], P(None, ('struct', 'fluid')), may hold values from -6 to 6
- owner: int32 [1048576, 1], P(('struct', 'fluid')), may hold values from 0 to 127; in each aligned block of 8192 rows (0 to 8191, 8192 to 16383, ...) at most 128 rows name the same one
- stencil_slot: int32 [4, 8, 256, 128], P(None, 'struct', 'fluid'), may hold values from 0 to 16383
- stencil_weight: float32 [4, 8, 256, 128], P(None, 'struct', 'fluid'), may hold values from 0 to 0.5
- prev_motion: float32 [3, 8, 256, 256], P(None, 'struct', 'fluid'), may hold values from -6 to 6
- node_offset: float32 [3, 8, 256, 256], P(None, 'struct', 'fluid'), may hold values from -0.07 to 0.07
- cell_split: int32 [8, 256, 256], P('struct', 'fluid'), may hold values from 0 to 3
Outputs:
- mesh_motion: float32 [3, 8, 256, 256], P(None, 'struct', 'fluid')
Inputs may be any that keep to these rules, and one draw needn't show every extreme that they name: Among the 8192 shell nodes of one device, no owner is named by more than 128 of them, a bound that some block reaches.
All inputs are finite; a program needn't handle non-finite values.
Results may differ from a plain program's by a relative error of at most 0.0003.
Values sent between devices are 32-bit elements; how exact they have to be, the bound alone decides.
No kernel may reach another device: no remote copies, remote signals or barrier semaphores. Data moves between devices by JAX's collectives and lax.ppermute only.
A program may use at most 64 MiB of HBM per device.

v0:
```python
from functools import reduce

import jax
import jax.numpy as jnp
from jax import lax
from jax.sharding import PartitionSpec as P

SWEEPS = 4


LAMBDA_RATIO = 1.0
RELAX_FACTOR = 0.5
STEP_ORDERS = ((0, 1, 2), (0, 2, 1), (1, 0, 2), (1, 2, 0), (2, 0, 1), (2, 1, 0))
CORNER_LIST = tuple(
    ((shift_x, shift_y, shift_z) for shift_x in (0, 1) for shift_y in (0, 1) for shift_z in (0, 1))
)


def from_behind(block, axis, distance):
    devices = range(lax.axis_size(axis))
    route = [((i - distance) % len(devices), i) for i in devices]
    return lax.ppermute(block, axis, route)


def cross_product(left_vec, right_vec):
    return jnp.stack(
        [
            left_vec[1] * right_vec[2] - left_vec[2] * right_vec[1],
            left_vec[2] * right_vec[0] - left_vec[0] * right_vec[2],
            left_vec[0] * right_vec[1] - left_vec[1] * right_vec[0],
        ]
    )


def select_flip(flip_y, flip_z, unflipped, flipped_z, flipped_y, flipped_both):
    return jnp.where(
        flip_y, jnp.where(flip_z, flipped_both, flipped_y), jnp.where(flip_z, flipped_z, unflipped)
    )


def reflect_corners(corners, flip_y, flip_z):
    result = {}
    for corner in CORNER_LIST:
        shift_x, shift_y, shift_z = corner
        result[corner] = select_flip(
            flip_y,
            flip_z,
            corners[corner],
            corners[shift_x, shift_y, 1 - shift_z],
            corners[shift_x, 1 - shift_y, shift_z],
            corners[shift_x, 1 - shift_y, 1 - shift_z],
        )
    return result


def flip_masks(split_codes):
    flip_y = split_codes // 2 == 1
    flip_z = split_codes % 2 == 1
    sign_y = jnp.where(flip_y, -1.0, 1.0).astype(jnp.float32)
    sign_z = jnp.where(flip_z, -1.0, 1.0).astype(jnp.float32)
    return (flip_y, flip_z, sign_y, sign_z)


def lattice_edge(vertex, sign_y, sign_z):
    return jnp.stack(
        [jnp.full_like(sign_y, float(vertex[0])), sign_y * vertex[1], sign_z * vertex[2]]
    )


def element_gradients(offsets, step_order, sign_y, sign_z):
    position = [0, 0, 0]
    vertex_path = [(0, 0, 0)]
    for axis_id in step_order:
        position[axis_id] = 1
        vertex_path.append(tuple(position))
    anchor = offsets[vertex_path[0]]
    edge_list = [
        lattice_edge(vertex, sign_y, sign_z) + offsets[vertex] - anchor
        for vertex in vertex_path[1:]
    ]
    across_one = cross_product(edge_list[1], edge_list[2])
    across_two = cross_product(edge_list[2], edge_list[0])
    across_three = cross_product(edge_list[0], edge_list[1])
    volume_six = jnp.sum(edge_list[0] * across_one, axis=0)
    grad_one = across_one / volume_six
    grad_two = across_two / volume_six
    grad_three = across_three / volume_six
    grad_zero = -(grad_one + grad_two + grad_three)
    return (vertex_path, [grad_zero, grad_one, grad_two, grad_three])


def element_forces(offsets, displace, sign_y, sign_z):
    forces = {corner: jnp.zeros_like(displace[corner]) for corner in CORNER_LIST}
    for step_order in STEP_ORDERS:
        vertex_path, gradient_list = element_gradients(offsets, step_order, sign_y, sign_z)
        tensor = displace[vertex_path[0]][:, None] * gradient_list[0][None, :]
        for vertex in range(1, 4):
            tensor = (
                tensor + displace[vertex_path[vertex]][:, None] * gradient_list[vertex][None, :]
            )
        trace_sum = tensor[0, 0] + tensor[1, 1] + tensor[2, 2]
        symmetric = tensor + jnp.swapaxes(tensor, 0, 1)
        for vertex in range(4):
            gradient = gradient_list[vertex]
            nodal_force = LAMBDA_RATIO * trace_sum * gradient + jnp.sum(
                symmetric * gradient[None, :], axis=1
            )
            forces[vertex_path[vertex]] = forces[vertex_path[vertex]] + nodal_force
    return forces


def element_diagonal(offsets, sign_y, sign_z):
    result = {corner: jnp.zeros_like(offsets[corner]) for corner in CORNER_LIST}
    for step_order in STEP_ORDERS:
        vertex_path, gradient_list = element_gradients(offsets, step_order, sign_y, sign_z)
        for vertex in range(4):
            gradient = gradient_list[vertex]
            entry = (LAMBDA_RATIO + 1.0) * gradient * gradient + jnp.sum(
                gradient * gradient, axis=0
            )
            result[vertex_path[vertex]] = result[vertex_path[vertex]] + entry
    return result


def cell_corners(extended, count_y, count_z):
    return {
        corner: jnp.roll(
            extended[:, corner[1] : corner[1] + count_y, corner[2] : corner[2] + count_z, :],
            -corner[0],
            axis=3,
        )
        for corner in CORNER_LIST
    }


def corner_diagonal(offset_ext, masks, count_y, count_z):
    flip_y, flip_z, sign_y, sign_z = masks
    offsets = reflect_corners(cell_corners(offset_ext, count_y, count_z), flip_y, flip_z)
    return reflect_corners(element_diagonal(offsets, sign_y, sign_z), flip_y, flip_z)


def corner_forces(offset_ext, motion_ext, masks, count_y, count_z):
    flip_y, flip_z, sign_y, sign_z = masks
    offsets = reflect_corners(cell_corners(offset_ext, count_y, count_z), flip_y, flip_z)
    displace = reflect_corners(cell_corners(motion_ext, count_y, count_z), flip_y, flip_z)
    return reflect_corners(element_forces(offsets, displace, sign_y, sign_z), flip_y, flip_z)


def spread_sum(per_corner):
    pieces = [
        jnp.roll(
            jnp.pad(
                per_corner[corner],
                ((0, 0), (corner[1], 1 - corner[1]), (corner[2], 1 - corner[2]), (0, 0)),
            ),
            corner[0],
            axis=3,
        )
        for corner in CORNER_LIST
    ]
    return reduce(jnp.add, pieces)


def upper_ghosts(nodal_field):
    top_plane = from_behind(nodal_field[:, :, :1, :], "fluid", -1)
    widened = jnp.concatenate([nodal_field, top_plane], axis=2)
    row_part = from_behind(widened[:, :1], "struct", -1)
    return jnp.concatenate([widened, row_part], axis=1)


def fold_back(spread):
    count_y = spread.shape[1] - 1
    count_z = spread.shape[2] - 1
    row_part = from_behind(spread[:, count_y:], "struct", 1)
    folded = jnp.concatenate([spread[:, :1] + row_part, spread[:, 1:count_y]], axis=1)
    top_plane = from_behind(folded[:, :, count_z:], "fluid", 1)
    return jnp.concatenate([folded[:, :, :1] + top_plane, folded[:, :, 1:count_z]], axis=2)


def shards(shell_motion, owner, stencil_slot, stencil_weight, prev_motion, node_offset, cell_split):
    struct_count = lax.axis_size("struct")
    fluid_count = lax.axis_size("fluid")
    devices = struct_count * fluid_count
    capacity = 2 * shell_motion.shape[1] // devices
    targets = jnp.arange(devices, dtype=jnp.int32)
    owner_rows = owner[:, 0]
    onehot = (owner_rows[:, None] == targets[None, :]).astype(jnp.int32)
    before = jnp.cumsum(onehot, axis=0) - onehot
    slot_rank = jnp.sum(before * onehot, axis=1)
    slot_place = owner_rows * capacity + slot_rank
    packed = jnp.zeros((3, devices * capacity), jnp.float32).at[:, slot_place].set(shell_motion)
    received = lax.all_to_all(
        packed.reshape(3, devices, capacity),
        ("struct", "fluid"),
        split_axis=1,
        concat_axis=1,
        tiled=True,
    )
    received = received.reshape(3, devices * capacity)
    stencil_count, count_y, count_z, wall_width = stencil_slot.shape
    gathered = jnp.take(received, stencil_slot.reshape(-1), axis=1).reshape(
        3, stencil_count, count_y, count_z, wall_width
    )
    wall_values = jnp.sum(stencil_weight[None] * gathered, axis=1)
    motion = jnp.concatenate([wall_values, prev_motion[:, :, :, wall_width:]], axis=3)
    is_wall = (jnp.arange(motion.shape[3], dtype=jnp.int32) < wall_width)[None, None, None, :]
    masks = flip_masks(cell_split)
    offset_ext = upper_ghosts(node_offset)
    diagonal = fold_back(spread_sum(corner_diagonal(offset_ext, masks, count_y, count_z)))
    for sweep_index in range(SWEEPS):
        forces = fold_back(
            spread_sum(corner_forces(offset_ext, upper_ghosts(motion), masks, count_y, count_z))
        )
        motion = jnp.where(is_wall, motion, motion - RELAX_FACTOR * forces / diagonal)
    return motion


def solution(mesh):
    return jax.shard_map(
        shards,
        mesh=mesh,
        in_specs=(
            P(None, ("struct", "fluid")),
            P(("struct", "fluid"), None),
            P(None, "struct", "fluid", None),
            P(None, "struct", "fluid", None),
            P(None, "struct", "fluid", None),
            P(None, "struct", "fluid", None),
            P("struct", "fluid", None),
        ),
        out_specs=P(None, "struct", "fluid", None),
        check_vma=False,
    )
```

profile of v0, /device:TPU:0, one launch (start us, length us, event | category | flops | bytes accessed | tf_op | source)
XLA Modules:
  0.0 191.9 jit_solution(16414757542172310630)
XLA Ops:
  0.8 6.0 %collective-permute-start.2 = (f32[3,2,1,256]{3,2,1,0:T(1,128)S(1)}, f32[3,2,1,256]{3,2,1,0:T(1,128)S(1)}, u32[]{:S(2)}, u32[]{:S(2)}) collective-permute-start(f32[3,2,1,256]{3,2,1,0:T(1,128)S(1)} %slice.619), channel_id=1, source_target_pairs={{1,0},{2,1},{3,2},{4,3},{5,4},{6,5},{7,6},{8,7},{9,8},{10,9},{11,1... | collective-permute-start | bytes 18440 | tf_op jit(solution)/shard_map/ppermute | solution.py:22
  10.9 2.6 %broadcast_add_fusion = s32[128,64,128]{0,1,2:T(8,128)S(1)} fusion(s32[128,64,128]{0,1,2:T(8,128)} %copy-done, s32[128,64]{0,1:T(8,128)S(1)} %slice.845), kind=kLoop, calls=%fused_computation.12 | loop fusion | flops 1048576 | bytes 8421376 | tf_op jit(solution)/shard_map/reduce_window_sum
  13.5 2.4 %copy.1354 = s32[128,64,128]{0,2,1:T(8,128)S(1)} copy(s32[128,64,128]{0,1,2:T(8,128)S(1)} %broadcast_add_fusion) | data formatting | bytes 8388608 | tf_op jit(solution)/shard_map/reduce_window_sum
  16.0 2.8 %fusion.1 = s32[8192]{0:T(1024)S(1)} fusion(s32[128,64,128]{0,2,1:T(8,128)S(1)} %copy.1354, s32[8192]{0:T(1024)S(1)} %bitcast.86), kind=kLoop, calls=%fused_computation.4 | loop fusion | flops 5234688 | bytes 4259840 | tf_op jit(solution)/shard_map/reduce_sum | solution.py:189
  18.9 2.7 %copy.1355 = f32[8192,3]{1,0:T(8,128)} copy(f32[8192,3]{0,1:T(4,128)S(1)} %bitcast.88) | data formatting | bytes 196608 | tf_op args[0]
  21.5 24.5 %scatter_custom_fusion = f32[3,16384]{0,1:T(8,128)} fusion(s32[8192]{0:T(1024)S(1)} %bitcast.91, f32[8192,3]{1,0:T(8,128)} %copy.1355, f32[]{:T(128)} %constant.58.clone.1), kind=kCustom, calls=%fused_computation.10 | custom fusion | bytes 197120 | tf_op jit(solution)/shard_map/scatter | solution.py:191
  46.1 6.0 %copy.1356 = f32[3,128,128]{2,0,1:T(4,128)} copy(f32[3,128,128]{0,2,1:T(8,128)} %bitcast.81) | data formatting | bytes 393216 | tf_op jit(solution)/shard_map/reshape | solution.py:193
  52.0 5.2 %all-to-all-start = ((f32[3,128,128]{2,0,1:T(4,128)}), f32[3,128,128]{2,0,1:T(4,128)S(1)}, u32[]{:S(2)}, u32[]{:S(2)}) async-start(f32[3,128,128]{2,0,1:T(4,128)} %copy.1356), calls=%async_computation | async-start | bytes 524288 | tf_op jit(solution)/shard_map/all_to_all | solution.py:192
  57.6 2.2 %collective-permute-start.3 = (f32[3,1,9,256]{3,1,2,0:T(1,128)S(1)}, f32[3,1,9,256]{3,1,2,0:T(1,128)S(1)}, u32[]{:S(2)}, u32[]{:S(2)}) collective-permute-start(f32[3,1,9,256]{3,1,2,0:T(1,128)S(1)} %copy.1361), channel_id=1, source_target_pairs={{32,0},{64,32},{96,64},{0,96},{33,1},{65,33},{97,65},{1,97},{34,2}... | collective-permute-start | bytes 82952 | tf_op jit(solution)/shard_map/ppermute | solution.py:22
  62.5 5.5 %all-to-all-done = f32[3,128,128]{2,0,1:T(4,128)S(1)} async-done(((f32[3,128,128]{2,0,1:T(4,128)}), f32[3,128,128]{2,0,1:T(4,128)S(1)}, u32[]{:S(2)}, u32[]{:S(2)}) %all-to-all-start) | async-done | bytes 196640 | tf_op jit(solution)/shard_map/all_to_all | solution.py:192
  68.0 4.9 %copy.1357 = f32[3,128,128]{0,2,1:T(8,128)} copy(f32[3,128,128]{2,0,1:T(4,128)S(1)} %all-to-all-done) | data formatting | bytes 393216 | tf_op jit(solution)/shard_map/all_to_all | solution.py:192
  72.9 31.1 %gather_fusion = f32[8192,3]{1,0:T(8,128)} fusion(f32[3,16384]{0,1:T(8,128)} %bitcast.82, s32[8192]{0:T(1024)S(1)} %broadcast_clamp_fusion), kind=kCustom, calls=%fused_computation | custom fusion | bytes 229376 | tf_op jit(solution)/shard_map/jit(_take)/gather | solution.py:201
  104.0 6.1 %multiply_reduce_fusion = f32[3,2,8,128]{0,3,2,1:T(8,128)S(1)} fusion(f32[3,4,2,8,128]{0,4,3,2,1:T(8,128)} %bitcast.83, f32[4,2,8,128]{3,2,1,0:T(8,128)S(1)} %copy-done.5, pred[4,2,8,128]{3,2,1,0:T(8,128)(4,1)S(1)} %compare_and_fusion), kind=kLoop, calls=%fused_computation.5 | loop fusion | flops 67584 | bytes 163840 | tf_op jit(solution)/shard_map/reduce_sum | solution.py:204
  122.6 2.9 %collective-permute-done.6 = f32[3,1,9,256]{3,1,2,0:T(1,128)S(1)} collective-permute-done((f32[3,1,9,256]{3,1,2,0:T(1,128)S(1)}, f32[3,1,9,256]{3,1,2,0:T(1,128)S(1)}, u32[]{:S(2)}, u32[]{:S(2)}) %collective-permute-start.6) | collective-permute-done | bytes 27680 | tf_op jit(solution)/shard_map/ppermute | solution.py:22
  126.7 5.3 %collective-permute-done.7 = f32[3,2,1,256]{3,1,2,0:T(2,128)S(1)} collective-permute-done((f32[3,2,1,256]{3,1,2,0:T(2,128)S(1)}, f32[3,2,1,256]{3,1,2,0:T(2,128)S(1)}, u32[]{:S(2)}, u32[]{:S(2)}) %collective-permute-start.7) | collective-permute-done | bytes 6176 | tf_op jit(solution)/shard_map/ppermute | solution.py:22
  136.2 2.4 %collective-permute-done.9 = f32[3,1,9,256]{3,1,2,0:T(1,128)S(1)} collective-permute-done((f32[3,1,9,256]{3,1,2,0:T(1,128)S(1)}, f32[3,1,9,256]{3,1,2,0:T(1,128)S(1)}, u32[]{:S(2)}, u32[]{:S(2)}) %collective-permute-start.9) | collective-permute-done | bytes 27680 | tf_op jit(solution)/shard_map/ppermute | solution.py:22
  141.0 4.8 %collective-permute-done.10 = f32[3,1,9,256]{3,1,2,0:T(1,128)S(1)} collective-permute-done((f32[3,1,9,256]{3,1,2,0:T(1,128)S(1)}, f32[3,1,9,256]{3,1,2,0:T(1,128)S(1)}, u32[]{:S(2)}, u32[]{:S(2)}) %collective-permute-start.10) | collective-permute-done | bytes 27680 | tf_op jit(solution)/shard_map/ppermute | solution.py:22
  146.1 6.3 %collective-permute-done.11 = f32[3,2,1,256]{3,1,2,0:T(2,128)S(1)} collective-permute-done((f32[3,2,1,256]{3,1,2,0:T(2,128)S(1)}, f32[3,2,1,256]{3,1,2,0:T(2,128)S(1)}, u32[]{:S(2)}, u32[]{:S(2)}) %collective-permute-start.11) | collective-permute-done | bytes 6176 | tf_op jit(solution)/shard_map/ppermute | solution.py:22
  155.5 2.4 %collective-permute-done.13 = f32[3,1,9,256]{3,1,2,0:T(1,128)S(1)} collective-permute-done((f32[3,1,9,256]{3,1,2,0:T(1,128)S(1)}, f32[3,1,9,256]{3,1,2,0:T(1,128)S(1)}, u32[]{:S(2)}, u32[]{:S(2)}) %collective-permute-start.13) | collective-permute-done | bytes 27680 | tf_op jit(solution)/shard_map/ppermute | solution.py:22
  160.1 5.1 %collective-permute-done.14 = f32[3,1,9,256]{3,1,2,0:T(1,128)S(1)} collective-permute-done((f32[3,1,9,256]{3,1,2,0:T(1,128)S(1)}, f32[3,1,9,256]{3,1,2,0:T(1,128)S(1)}, u32[]{:S(2)}, u32[]{:S(2)}) %collective-permute-start.14) | collective-permute-done | bytes 27680 | tf_op jit(solution)/shard_map/ppermute | solution.py:22
  165.6 6.3 %collective-permute-done.15 = f32[3,2,1,256]{3,1,2,0:T(2,128)S(1)} collective-permute-done((f32[3,2,1,256]{3,1,2,0:T(2,128)S(1)}, f32[3,2,1,256]{3,1,2,0:T(2,128)S(1)}, u32[]{:S(2)}, u32[]{:S(2)}) %collective-permute-start.15) | collective-permute-done | bytes 6176 | tf_op jit(solution)/shard_map/ppermute | solution.py:22
  175.0 2.4 %collective-permute-done.17 = f32[3,1,9,256]{3,1,2,0:T(1,128)S(1)} collective-permute-done((f32[3,1,9,256]{3,1,2,0:T(1,128)S(1)}, f32[3,1,9,256]{3,1,2,0:T(1,128)S(1)}, u32[]{:S(2)}, u32[]{:S(2)}) %collective-permute-start.17) | collective-permute-done | bytes 27680 | tf_op jit(solution)/shard_map/ppermute | solution.py:22
  179.6 5.1 %collective-permute-done.18 = f32[3,1,9,256]{3,1,2,0:T(1,128)S(1)} collective-permute-done((f32[3,1,9,256]{3,1,2,0:T(1,128)S(1)}, f32[3,1,9,256]{3,1,2,0:T(1,128)S(1)}, u32[]{:S(2)}, u32[]{:S(2)}) %collective-permute-start.18) | collective-permute-done | bytes 27680 | tf_op jit(solution)/shard_map/ppermute | solution.py:22
  184.9 6.3 %collective-permute-done.19 = f32[3,2,1,256]{3,1,2,0:T(2,128)S(1)} collective-permute-done((f32[3,2,1,256]{3,1,2,0:T(2,128)S(1)}, f32[3,2,1,256]{3,1,2,0:T(2,128)S(1)}, u32[]{:S(2)}, u32[]{:S(2)}) %collective-permute-start.19) | collective-permute-done | bytes 6176 | tf_op jit(solution)/shard_map/ppermute | solution.py:22
  (331 shorter events, 38.7 us)
Async XLA Ops:
  0.8 56.7 %collective-permute-start.2 = (f32[3,2,1,256]{3,2,1,0:T(1,128)S(1)}, f32[3,2,1,256]{3,2,1,0:T(1,128)S(1)}, u32[]{:S(2)}, u32[]{:S(2)}) collective-permute-start(f32[3,2,1,256]{3,2,1,0:T(1,128)S(1)} %slice.619), channel_id=1, source_target_pairs={{1,0},{2,1},{3,2},{4,3},{5,4},{6,5},{7,6},{8,7},{9,8},{10,9},{11,1... | collective-permute-start | bytes 18440 | tf_op jit(solution)/shard_map/ppermute | solution.py:22
  46.1 11.4 %copy-start.1 = (f32[3,2,8,256]{3,2,1,0:T(8,128)S(1)}, f32[3,2,8,256]{3,2,1,0:T(8,128)}, u32[]{:S(2)}) copy-start(f32[3,2,8,256]{3,2,1,0:T(8,128)} %param.12) | copy-start | bytes 147460
  46.1 13.9 %copy-start.7 = (f32[3,2,8,256]{3,2,1,0:T(8,128)S(1)}, f32[3,2,8,256]{3,2,1,0:T(8,128)}, u32[]{:S(2)}) copy-start(f32[3,2,8,256]{3,2,1,0:T(8,128)} %param.11) | copy-start | bytes 147460
  52.0 16.0 %all-to-all-start = ((f32[3,128,128]{2,0,1:T(4,128)}), f32[3,128,128]{2,0,1:T(4,128)S(1)}, u32[]{:S(2)}, u32[]{:S(2)}) async-start(f32[3,128,128]{2,0,1:T(4,128)} %copy.1356), calls=%async_computation | async-start | bytes 524288 | tf_op jit(solution)/shard_map/all_to_all | solution.py:192
  57.6 4.4 %collective-permute-start.3 = (f32[3,1,9,256]{3,1,2,0:T(1,128)S(1)}, f32[3,1,9,256]{3,1,2,0:T(1,128)S(1)}, u32[]{:S(2)}, u32[]{:S(2)}) collective-permute-start(f32[3,1,9,256]{3,1,2,0:T(1,128)S(1)} %copy.1361), channel_id=1, source_target_pairs={{32,0},{64,32},{96,64},{0,96},{33,1},{65,33},{97,65},{1,97},{34,2}... | collective-permute-start | bytes 82952 | tf_op jit(solution)/shard_map/ppermute | solution.py:22
  62.5 41.5 %copy-start.5 = (f32[4,2,8,128]{3,2,1,0:T(8,128)S(1)}, f32[4,2,8,128]{3,2,1,0:T(8,128)}, u32[]{:S(2)}) copy-start(f32[4,2,8,128]{3,2,1,0:T(8,128)} %param.10) | copy-start | bytes 98308
  110.5 2.3 %collective-permute-start = (f32[3,2,1,256]{3,2,1,0:T(1,128)S(1)}, f32[3,2,1,256]{3,2,1,0:T(1,128)S(1)}, u32[]{:S(2)}, u32[]{:S(2)}) collective-permute-start(f32[3,2,1,256]{3,2,1,0:T(1,128)S(1)} %fusion.199), channel_id=1, source_target_pairs={{1,0},{2,1},{3,2},{4,3},{5,4},{6,5},{7,6},{8,7},{9,8},{10,9},{11,1... | collective-permute-start | bytes 18440 | tf_op jit(solution)/shard_map/ppermute | solution.py:22
  112.8 3.9 %collective-permute-start.1 = (f32[3,1,9,256]{3,1,2,0:T(1,128)S(1)}, f32[3,1,9,256]{3,1,2,0:T(1,128)S(1)}, u32[]{:S(2)}, u32[]{:S(2)}) collective-permute-start(f32[3,1,9,256]{3,1,2,0:T(1,128)S(1)} %copy.1359), channel_id=1, source_target_pairs={{32,0},{64,32},{96,64},{0,96},{33,1},{65,33},{97,65},{1,97},{34,2}... | collective-permute-start | bytes 82952 | tf_op jit(solution)/shard_map/ppermute | solution.py:22
  120.3 5.1 %collective-permute-start.6 = (f32[3,1,9,256]{3,1,2,0:T(1,128)S(1)}, f32[3,1,9,256]{3,1,2,0:T(1,128)S(1)}, u32[]{:S(2)}, u32[]{:S(2)}) collective-permute-start(f32[3,1,9,256]{3,1,2,0:T(1,128)S(1)} %copy.1370), channel_id=1, source_target_pairs={{96,0},{0,32},{32,64},{64,96},{97,1},{1,33},{33,65},{65,97},{98,2}... | collective-permute-start | bytes 82952 | tf_op jit(solution)/shard_map/ppermute | solution.py:22
  121.3 5.1 %collective-permute-start.4 = (f32[3,1,9,256]{3,1,2,0:T(1,128)S(1)}, f32[3,1,9,256]{3,1,2,0:T(1,128)S(1)}, u32[]{:S(2)}, u32[]{:S(2)}) collective-permute-start(f32[3,1,9,256]{3,1,2,0:T(1,128)S(1)} %copy.1364), channel_id=1, source_target_pairs={{96,0},{0,32},{32,64},{64,96},{97,1},{1,33},{33,65},{65,97},{98,2}... | collective-permute-start | bytes 82952 | tf_op jit(solution)/shard_map/ppermute | solution.py:22
  125.6 6.4 %collective-permute-start.7 = (f32[3,2,1,256]{3,1,2,0:T(2,128)S(1)}, f32[3,2,1,256]{3,1,2,0:T(2,128)S(1)}, u32[]{:S(2)}, u32[]{:S(2)}) collective-permute-start(f32[3,2,1,256]{3,1,2,0:T(2,128)S(1)} %pad_maximum_fusion.52), channel_id=1, source_target_pairs={{31,0},{0,1},{1,2},{2,3},{3,4},{4,5},{5,6},{6,7},{7,8},{8,9},{9,10... | collective-permute-start | bytes 18440 | tf_op jit(solution)/shard_map/ppermute | solution.py:22
  126.6 6.4 %collective-permute-start.5 = (f32[3,2,1,256]{3,1,2,0:T(2,128)S(1)}, f32[3,2,1,256]{3,1,2,0:T(2,128)S(1)}, u32[]{:S(2)}, u32[]{:S(2)}) collective-permute-start(f32[3,2,1,256]{3,1,2,0:T(2,128)S(1)} %pad_maximum_fusion.53), channel_id=1, source_target_pairs={{31,0},{0,1},{1,2},{2,3},{3,4},{4,5},{5,6},{6,7},{7,8},{8,9},{9,10... | collective-permute-start | bytes 18440 | tf_op jit(solution)/shard_map/ppermute | solution.py:22
  133.2 1.4 collective-permute-start.8
  134.6 3.9 %collective-permute-start.9 = (f32[3,1,9,256]{3,1,2,0:T(1,128)S(1)}, f32[3,1,9,256]{3,1,2,0:T(1,128)S(1)}, u32[]{:S(2)}, u32[]{:S(2)}) collective-permute-start(f32[3,1,9,256]{3,1,2,0:T(1,128)S(1)} %copy.1376), channel_id=1, source_target_pairs={{32,0},{64,32},{96,64},{0,96},{33,1},{65,33},{97,65},{1,97},{34,2}... | collective-permute-start | bytes 82952 | tf_op jit(solution)/shard_map/ppermute | solution.py:22
  140.7 5.1 %collective-permute-start.10 = (f32[3,1,9,256]{3,1,2,0:T(1,128)S(1)}, f32[3,1,9,256]{3,1,2,0:T(1,128)S(1)}, u32[]{:S(2)}, u32[]{:S(2)}) collective-permute-start(f32[3,1,9,256]{3,1,2,0:T(1,128)S(1)} %copy.1378), channel_id=1, source_target_pairs={{96,0},{0,32},{32,64},{64,96},{97,1},{1,33},{33,65},{65,97},{98,2}... | collective-permute-start | bytes 82952 | tf_op jit(solution)/shard_map/ppermute | solution.py:22
  146.0 6.4 %collective-permute-start.11 = (f32[3,2,1,256]{3,1,2,0:T(2,128)S(1)}, f32[3,2,1,256]{3,1,2,0:T(2,128)S(1)}, u32[]{:S(2)}, u32[]{:S(2)}) collective-permute-start(f32[3,2,1,256]{3,1,2,0:T(2,128)S(1)} %pad_maximum_fusion.51), channel_id=1, source_target_pairs={{31,0},{0,1},{1,2},{2,3},{3,4},{4,5},{5,6},{6,7},{7,8},{8,9},{9,10... | collective-permute-start | bytes 18440 | tf_op jit(solution)/shard_map/ppermute | solution.py:22
  152.5 1.4 collective-permute-start.12
  153.9 3.9 %collective-permute-start.13 = (f32[3,1,9,256]{3,1,2,0:T(1,128)S(1)}, f32[3,1,9,256]{3,1,2,0:T(1,128)S(1)}, u32[]{:S(2)}, u32[]{:S(2)}) collective-permute-start(f32[3,1,9,256]{3,1,2,0:T(1,128)S(1)} %copy.1384), channel_id=1, source_target_pairs={{32,0},{64,32},{96,64},{0,96},{33,1},{65,33},{97,65},{1,97},{34,2}... | collective-permute-start | bytes 82952 | tf_op jit(solution)/shard_map/ppermute | solution.py:22
  160.0 5.1 %collective-permute-start.14 = (f32[3,1,9,256]{3,1,2,0:T(1,128)S(1)}, f32[3,1,9,256]{3,1,2,0:T(1,128)S(1)}, u32[]{:S(2)}, u32[]{:S(2)}) collective-permute-start(f32[3,1,9,256]{3,1,2,0:T(1,128)S(1)} %copy.1386), channel_id=1, source_target_pairs={{96,0},{0,32},{32,64},{64,96},{97,1},{1,33},{33,65},{65,97},{98,2}... | collective-permute-start | bytes 82952 | tf_op jit(solution)/shard_map/ppermute | solution.py:22
  165.3 6.7 %collective-permute-start.15 = (f32[3,2,1,256]{3,1,2,0:T(2,128)S(1)}, f32[3,2,1,256]{3,1,2,0:T(2,128)S(1)}, u32[]{:S(2)}, u32[]{:S(2)}) collective-permute-start(f32[3,2,1,256]{3,1,2,0:T(2,128)S(1)} %pad_maximum_fusion.50), channel_id=1, source_target_pairs={{31,0},{0,1},{1,2},{2,3},{3,4},{4,5},{5,6},{6,7},{7,8},{8,9},{9,10... | collective-permute-start | bytes 18440 | tf_op jit(solution)/shard_map/ppermute | solution.py:22
  172.0 1.4 collective-permute-start.16
  173.5 3.9 %collective-permute-start.17 = (f32[3,1,9,256]{3,1,2,0:T(1,128)S(1)}, f32[3,1,9,256]{3,1,2,0:T(1,128)S(1)}, u32[]{:S(2)}, u32[]{:S(2)}) collective-permute-start(f32[3,1,9,256]{3,1,2,0:T(1,128)S(1)} %copy.1392), channel_id=1, source_target_pairs={{32,0},{64,32},{96,64},{0,96},{33,1},{65,33},{97,65},{1,97},{34,2}... | collective-permute-start | bytes 82952 | tf_op jit(solution)/shard_map/ppermute | solution.py:22
  179.5 5.1 %collective-permute-start.18 = (f32[3,1,9,256]{3,1,2,0:T(1,128)S(1)}, f32[3,1,9,256]{3,1,2,0:T(1,128)S(1)}, u32[]{:S(2)}, u32[]{:S(2)}) collective-permute-start(f32[3,1,9,256]{3,1,2,0:T(1,128)S(1)} %copy.1394), channel_id=1, source_target_pairs={{96,0},{0,32},{32,64},{64,96},{97,1},{1,33},{33,65},{65,97},{98,2}... | collective-permute-start | bytes 82952 | tf_op jit(solution)/shard_map/ppermute | solution.py:22
  184.8 6.4 %collective-permute-start.19 = (f32[3,2,1,256]{3,1,2,0:T(2,128)S(1)}, f32[3,2,1,256]{3,1,2,0:T(2,128)S(1)}, u32[]{:S(2)}, u32[]{:S(2)}) collective-permute-start(f32[3,2,1,256]{3,1,2,0:T(2,128)S(1)} %pad_maximum_fusion.49), channel_id=1, source_target_pairs={{31,0},{0,1},{1,2},{2,3},{3,4},{4,5},{5,6},{6,7},{7,8},{8,9},{9,10... | collective-permute-start | bytes 18440 | tf_op jit(solution)/shard_map/ppermute | solution.py:22
  (5 other events, 29.8 us)
where the time goes:
time: 192 us
  local copies, waits for them, and re-layouts  78.6 us (41%)
  waiting for transfers between devices  66 us (34%)
  starting transfers between devices  23.5 us (12%)
  other arithmetic  21.9 us (11%)
    ppermute x20, waiting for transfers between devices, from_behind(): return lax.ppermute(block, axis, route)  60.4 us
    gather x1, local copies, waits for them, and re-layouts, shards(): jnp.take(received, stencil_slot.reshape(-1), axis=1)  31.1 us
    scatter x1, local copies, waits for them, and re-layouts, shards(): jnp.zeros((3, devices * capacity), jnp.float32).at[:, slot_place]  24.5 us
    ppermute x20, starting transfers between devices, from_behind(): return lax.ppermute(block, axis, route)  18.3 us
    reduce_sum x1, other arithmetic, shards(): wall_values = jnp.sum(stencil_weight[None] * gathered, axis=1)  6.12 us
    reshape x1, local copies, waits for them, and re-layouts, shards(): packed.reshape(3, devices, capacity)  5.95 us
    all_to_all x1, waiting for transfers between devices, shards(): lax.all_to_all(packed.reshape(3, devices, capacity), ('struct', 'fluid'),...  5.54 us
    all_to_all x1, starting transfers between devices, shards(): lax.all_to_all(packed.reshape(3, devices, capacity), ('struct', 'fluid'),...  5.25 us
  transfers between devices with their start and end apart: 21, of which 20 were waited for; matrix products, arithmetic and copies ran while one was open for 24% of the time, Pallas kernels for 0%

commit v1 on v0

v1 whole, which is shorter than its diff:
```python
import jax
import jax.numpy as jnp
from jax import lax
from jax.experimental import pallas as pl
from jax.experimental.pallas import tpu as pltpu
from jax.sharding import PartitionSpec as P

SWEEPS = 4
RELAX_FACTOR = 0.5
STEP_ORDERS = ((0, 1, 2), (0, 2, 1), (1, 0, 2), (1, 2, 0), (2, 0, 1), (2, 1, 0))
BITS = (0, 1)
CORNERS = tuple((a, b, c) for a in BITS for b in BITS for c in BITS)
STEPS = tuple(
    (x, y, z) for z in (-1, 0, 1) for y in (-1, 0, 1) for x in (-1, 0, 1) if (x, y, z) != (0, 0, 0)
)
SLOT_OF = {step: k for k, step in enumerate(STEPS)}
SELF = len(STEPS)
ENTRY = ((0, 3, 4), (3, 1, 5), (4, 5, 2))
BOTH = ("struct", "fluid")
DEPTH = SWEEPS
F32, BF16, I32 = jnp.float32, jnp.bfloat16, jnp.int32
VMEM = pl.BlockSpec(memory_space=pltpu.VMEM)


def params(mebibytes):
    return pltpu.CompilerParams(vmem_limit_bytes=mebibytes * 2**20)


def pack_kernel(owner_ref, value_ref, out_ref, left_ref, right_ref):
    count = owner_ref.shape[1]
    width = 256
    rows = lax.broadcasted_iota(I32, (width, width + 128), 0)
    columns = lax.broadcasted_iota(I32, (width, width + 128), 1)
    earlier = jnp.where((rows < columns) | (columns >= width), 1.0, 0.0).astype(BF16)
    owners = lax.broadcasted_iota(I32, (128, width), 0)
    pairs = lax.broadcasted_iota(I32, (64, width), 0)
    places = lax.broadcasted_iota(I32, (256, width), 0)
    base = jnp.zeros((128, 128), F32)
    for k in range(count // width):
        part = pl.ds(k * width, width)
        own = owner_ref[:, part]
        hit = owners == own
        before = jnp.dot(
            jnp.where(hit, 1.0, 0.0).astype(BF16), earlier, preferred_element_type=F32
        )
        running = before[:, :width] + jnp.concatenate([base, base], axis=1)
        rank = jnp.sum(jnp.where(hit, running, 0.0), axis=0, keepdims=True).astype(I32)
        base = base + before[:, width:]
        right_ref[:, part] = jnp.where(places == (own & 1) * 128 + rank, 1.0, 0.0).astype(BF16)
        half = pairs == (own >> 1)
        for c in range(3):
            value = value_ref[c : c + 1, part]
            high = value.astype(BF16).astype(F32)
            low = value - high
            left_ref[c * 64 : c * 64 + 64, part] = jnp.where(half, high, 0.0).astype(BF16)
            left_ref[192 + c * 64 : 256 + c * 64, part] = jnp.where(half, low, 0.0).astype(BF16)
    product = lax.dot_general(
        left_ref[...], right_ref[...], (((1,), (1,)), ((), ())), preferred_element_type=F32
    )
    both = product[:192] + product[192:]
    for c in range(3):
        for h in range(2):
            out_ref[pl.ds(h, 64, stride=2), c, :] = both[c * 64 : c * 64 + 64, h * 128 : h * 128 + 128]


def pack(owner, shell_motion):
    count = shell_motion.shape[1]
    return pl.pallas_call(
        pack_kernel,
        out_shape=jax.ShapeDtypeStruct((128, 3, 128), F32),
        in_specs=[VMEM] * 2,
        out_specs=VMEM,
        scratch_shapes=[pltpu.VMEM((384, count), BF16), pltpu.VMEM((256, count), BF16)],
        compiler_params=params(24),
        name="pack",
    )(owner.reshape(1, count), shell_motion)


def gather_kernel(received_ref, slot_ref, weight_ref, out_ref, table_ref):
    for c in range(3):
        flat = received_ref[:, c, :].T
        high = flat.astype(BF16).astype(F32)
        low = flat - high
        for part, base in ((high, 0), (low, 192)):
            at = base + c * 64
            table_ref[at : at + 64, :128] = part[:64].astype(BF16)
            table_ref[at : at + 64, 128:] = part[64:].astype(BF16)
    table = table_ref[...]
    picks = lax.broadcasted_iota(I32, (256, 256), 0)
    places = lax.broadcasted_iota(I32, (64, 256), 0)
    for y in range(2):
        for z in range(0, 8, 2):
            total = [jnp.zeros((64, 256), F32) for _ in range(3)]
            for t in range(4):
                slot = jnp.concatenate([slot_ref[t, y, z + k : z + k + 1, :] for k in BITS], axis=1)
                weight = jnp.concatenate([weight_ref[t, y, z + k : z + k + 1, :] for k in BITS], axis=1)
                pick = ((slot >> 6) & 1) * 128 + (slot >> 7)
                hot = jnp.where(picks == pick, 1.0, 0.0).astype(BF16)
                found = jnp.dot(table, hot, preferred_element_type=F32)
                share = jnp.where(places == (slot & 63), weight, 0.0)
                for c in range(3):
                    at = c * 64
                    total[c] = total[c] + share * (found[at : at + 64] + found[at + 192 : at + 256])
            for c in range(3):
                line = jnp.sum(total[c], axis=0, keepdims=True)
                for k in BITS:
                    out_ref[c, y, z + k : z + k + 1, :] = line[:, k * 128 : k * 128 + 128]


def gather(received, stencil_slot, stencil_weight):
    return pl.pallas_call(
        gather_kernel,
        out_shape=jax.ShapeDtypeStruct((3, 2, 8, 128), F32),
        in_specs=[VMEM] * 3,
        out_specs=VMEM,
        scratch_shapes=[pltpu.VMEM((384, 256), BF16)],
        compiler_params=params(16),
        name="gather",
    )(received, stencil_slot, stencil_weight)


def cross(u, v):
    return [
        u[1] * v[2] - u[2] * v[1],
        u[2] * v[0] - u[0] * v[2],
        u[0] * v[1] - u[1] * v[0],
    ]


def cell_blocks(corner, code):
    flip_y = code >= 2
    flip_z = (code == 1) | (code == 3)
    sign_y = jnp.where(flip_y, -1.0, 1.0)
    sign_z = jnp.where(flip_z, -1.0, 1.0)
    named = {}
    for a, b, c in CORNERS:
        named[a, b, c] = [jnp.where(flip_y, corner[a, 1 - b, c][p], corner[a, b, c][p]) for p in range(3)]
    named = {
        (a, b, c): [jnp.where(flip_z, named[a, b, 1 - c][p], named[a, b, c][p]) for p in range(3)]
        for a, b, c in CORNERS
    }
    edge = {}
    for v in CORNERS[1:]:
        moved = [named[v][p] - named[0, 0, 0][p] for p in range(3)]
        if v[0]:
            moved[0] = moved[0] + 1.0
        if v[1]:
            moved[1] = moved[1] + sign_y
        if v[2]:
            moved[2] = moved[2] + sign_z
        edge[v] = moved
    top = (1, 1, 1)
    over = {v: cross(edge[v], edge[top]) for v in CORNERS[1:-1]}
    blocks = {}
    for order in STEP_ORDERS:
        at = [0, 0, 0]
        path = [(0, 0, 0)]
        for axis in order:
            at[axis] = 1
            path.append(tuple(at))
        one, two = path[1], path[2]
        across = [over[two], [-w for w in over[one]], cross(edge[one], edge[two])]
        volume = sum(edge[one][p] * over[two][p] for p in range(3))
        inverse = 1.0 / volume
        grad = [None] + [[w * inverse for w in across[m]] for m in range(3)]
        grad[0] = [-(grad[1][p] + grad[2][p] + grad[3][p]) for p in range(3)]
        for i in range(4):
            for j in range(i + 1, 4):
                g, h = grad[i], grad[j]
                same = [g[p] * h[p] for p in range(3)]
                trace = same[0] + same[1] + same[2]
                block = [same[p] + same[p] + trace for p in range(3)]
                block += [g[p] * h[q] + g[q] * h[p] for p, q in ((0, 1), (0, 2), (1, 2))]
                key = (path[i], path[j])
                blocks[key] = [o + n for o, n in zip(blocks[key], block)] if key in blocks else block

    def pick(mask, yes, no):
        return [jnp.where(mask, y, n) for y, n in zip(yes, no)]

    def keep(mask, values):
        return [jnp.where(mask, v, 0.0) for v in values]

    along_x = {(b, c): blocks[(0, b, c), (1, b, c)] for b in BITS for c in BITS}
    along_x = {(b, c): pick(flip_y, along_x[1 - b, c], along_x[b, c]) for b, c in along_x}
    along_x = {(b, c): pick(flip_z, along_x[b, 1 - c], along_x[b, c]) for b, c in along_x}
    along_y = {(a, c): blocks[(a, 0, c), (a, 1, c)] for a in BITS for c in BITS}
    along_y = {(a, c): pick(flip_z, along_y[a, 1 - c], along_y[a, c]) for a, c in along_y}
    along_z = {(a, b): blocks[(a, b, 0), (a, b, 1)] for a in BITS for b in BITS}
    along_z = {(a, b): pick(flip_y, along_z[a, 1 - b], along_z[a, b]) for a, b in along_z}
    no_y, no_z, unlike = ~flip_y, ~flip_z, flip_y ^ flip_z
    in_xy = [blocks[(0, 0, c), (1, 1, c)] for c in BITS]
    in_xy = [pick(flip_z, in_xy[1 - c], in_xy[c]) for c in BITS]
    in_xz = [blocks[(0, b, 0), (1, b, 1)] for b in BITS]
    in_xz = [pick(flip_y, in_xz[1 - b], in_xz[b]) for b in BITS]
    in_yz = [blocks[(a, 0, 0), (a, 1, 1)] for a in BITS]
    body = blocks[(0, 0, 0), top]
    return dict(
        x=along_x,
        y=along_y,
        z=along_z,
        xy=[(keep(no_y, v), keep(flip_y, v)) for v in in_xy],
        xz=[(keep(no_z, v), keep(flip_z, v)) for v in in_xz],
        yz=[(keep(~unlike, v), keep(unlike, v)) for v in in_yz],
        xyz={
            (0, 0): keep(no_y & no_z, body),
            (0, 1): keep(no_y & flip_z, body),
            (1, 0): keep(flip_y & no_z, body),
            (1, 1): keep(flip_y & flip_z, body),
        },
    )


def fill_rows(target_ref, rows_refs, odd, channel, to, lanes):
    own, swap1, swap2, swap3 = rows_refs
    for r in range(2):
        one, three = swap1[channel, r, :, lanes], swap3[channel, r, :, lanes]
        for place, value in (
            (0, own[channel, r, :, lanes]),
            (2, jnp.where(odd, three, one)),
            (4, swap2[channel, r, :, lanes]),
            (6, jnp.where(odd, one, three)),
        ):
            target_ref[to, :, place + r, :] = value


def assemble_kernel(odd_ref, own_ref, swap1_ref, swap2_ref, swap3_ref, coef_ref, step_ref, field_ref):
    odd = odd_ref[0] == 1
    for c in range(4):
        fill_rows(field_ref, (own_ref, swap1_ref, swap2_ref, swap3_ref), odd, c, c, slice(None))
    planes = field_ref.shape[1]

    def back_y(values):
        return [pltpu.roll(v, 1, 0) for v in values]

    def back_x(values):
        return [pltpu.roll(v, 1, 1) for v in values]

    def plus(u, v):
        return [p + q for p, q in zip(u, v)]

    def put(plane, step, values):
        for e in range(6):
            coef_ref[plane, SLOT_OF[step], e] = values[e][:, 128:]

    def add(plane, step, values):
        for e in range(6):
            at = SLOT_OF[step]
            coef_ref[plane, at, e] = coef_ref[plane, at, e] + values[e][:, 128:]

    def cells(k, _):
        corner = {}
        for c in BITS:
            for p in range(3):
                low = field_ref[p, k + c]
                up = pltpu.roll(low, 7, 0)
                for b, row in ((0, low), (1, up)):
                    corner.setdefault((0, b, c), []).append(row)
                    corner.setdefault((1, b, c), []).append(pltpu.roll(row, 255, 1))
        kinds = cell_blocks(corner, field_ref[3, k])
        low, high = k, k + 1
        z = kinds["z"]
        both = [plus(z[a, 0], back_y(z[a, 1])) for a in BITS]
        s = plus(both[0], back_x(both[1]))
        put(low, (0, 0, 1), s)
        put(high, (0, 0, -1), s)
        (up0, down0), (up1, down1) = kinds["xz"]
        s = plus(up0, back_y(up1))
        put(low, (1, 0, 1), s)
        put(high, (-1, 0, -1), back_x(s))
        s = plus(down0, back_y(down1))
        put(high, (1, 0, -1), s)
        put(low, (-1, 0, 1), back_x(s))
        (up0, down0), (up1, down1) = kinds["yz"]
        s = plus(up0, back_x(up1))
        put(low, (0, 1, 1), s)
        put(high, (0, -1, -1), back_y(s))
        s = plus(down0, back_x(down1))
        put(high, (0, 1, -1), s)
        put(low, (0, -1, 1), back_y(s))
        body = kinds["xyz"]
        put(low, (1, 1, 1), body[0, 0])
        put(high, (-1, -1, -1), back_x(back_y(body[0, 0])))
        put(high, (1, 1, -1), body[0, 1])
        put(low, (-1, -1, 1), back_x(back_y(body[0, 1])))
        put(low, (1, -1, 1), back_y(body[1, 0]))
        put(high, (-1, 1, -1), back_x(body[1, 0]))
        put(high, (1, -1, -1), back_y(body[1, 1]))
        put(low, (-1, 1, 1), back_x(body[1, 1]))
        for c, plane, store in ((0, low, add), (1, high, put)):
            s = plus(kinds["x"][0, c], back_y(kinds["x"][1, c]))
            store(plane, (1, 0, 0), s)
            store(plane, (-1, 0, 0), back_x(s))
            s = plus(kinds["y"][0, c], back_x(kinds["y"][1, c]))
            store(plane, (0, 1, 0), s)
            store(plane, (0, -1, 0), back_y(s))
            up, down = kinds["xy"][c]
            store(plane, (1, 1, 0), up)
            store(plane, (-1, -1, 0), back_x(back_y(up)))
            store(plane, (1, -1, 0), back_y(down))
            store(plane, (-1, 1, 0), back_x(down))
        return 0

    lax.fori_loop(0, planes - 1, cells, 0)

    def selves(k, _):
        for e in range(6):
            total = coef_ref[k, 0, e]
            for m in range(1, SELF):
                total = total + coef_ref[k, m, e]
            coef_ref[k, SELF, e] = -total
            if e < 3:
                step_ref[k, e] = -RELAX_FACTOR / total
        return 0

    lax.fori_loop(1, planes - 1, selves, 0)


def assemble(odd, rows):
    planes = rows[0].shape[2]
    return pl.pallas_call(
        assemble_kernel,
        out_shape=(
            jax.ShapeDtypeStruct((planes, SELF + 1, 6, 8, 128), F32),
            jax.ShapeDtypeStruct((planes, 3, 8, 128), F32),
        ),
        in_specs=[pl.BlockSpec(memory_space=pltpu.SMEM)] + [VMEM] * 4,
        out_specs=(VMEM, VMEM),
        scratch_shapes=[pltpu.VMEM((4, planes, 8, 256), F32)],
        compiler_params=params(30),
        cost_estimate=pl.CostEstimate(flops=200000000, bytes_accessed=12000000, transcendentals=0),
        name="assemble",
    )(odd, *rows)


def sweep_kernel(odd_ref, *refs):
    prev_rows, wall_rows = refs[:4], refs[4:8]
    coef_ref, step_ref, wall_ref, out_ref, motion_ref, edge_ref, near_ref = refs[8:]
    odd = odd_ref[0] == 1
    planes = motion_ref.shape[1]
    for c in range(3):
        fill_rows(motion_ref, prev_rows, odd, c + 4, c, slice(128, 256))
        fill_rows(edge_ref, wall_rows, odd, c, c, slice(None))
    lane = lax.broadcasted_iota(I32, (8, 128), 1)
    first, last = lane == 0, lane == 127

    def neighbours(k, _):
        for c in range(3):
            here = motion_ref[c, k]
            side = edge_ref[c, k]
            for x, value in (
                (-1, jnp.where(first, pltpu.roll(side, 1, 1), pltpu.roll(here, 1, 1))),
                (0, here),
                (1, jnp.where(last, pltpu.roll(side, 127, 1), pltpu.roll(here, 127, 1))),
            ):
                near_ref[k, c, 1, x + 1] = value
                near_ref[k, c, 0, x + 1] = pltpu.roll(value, 1, 0)
                near_ref[k, c, 2, x + 1] = pltpu.roll(value, 7, 0)
        return 0

    def relax(k, _):
        force = [None] * 3
        for m, (x, y, z) in enumerate(STEPS + ((0, 0, 0),)):
            block = [coef_ref[k, m, e] for e in range(6)]
            other = [near_ref[k + z, c, y + 1, x + 1] for c in range(3)]
            for p in range(3):
                term = sum(block[ENTRY[p][q]] * other[q] for q in range(3))
                force[p] = term if force[p] is None else force[p] + term
        for p in range(3):
            motion_ref[p, k] = motion_ref[p, k] - step_ref[k, p] * force[p]
        return 0

    for sweep in range(SWEEPS):
        lax.fori_loop(sweep, planes - sweep, neighbours, 0)
        lax.fori_loop(sweep + 1, planes - sweep - 1, relax, 0)
    for c in range(3):
        for y in range(2):
            out_ref[c, y, :, :128] = wall_ref[c, y]
            out_ref[c, y, :, 128:] = motion_ref[c, DEPTH : planes - DEPTH, y, :]


def sweeps(odd, rows, wall_rows, coef, step, wall):
    planes = rows[0].shape[2]
    return pl.pallas_call(
        sweep_kernel,
        out_shape=jax.ShapeDtypeStruct((3, 2, planes - 2 * DEPTH, 256), F32),
        in_specs=[pl.BlockSpec(memory_space=pltpu.SMEM)] + [VMEM] * 11,
        out_specs=VMEM,
        scratch_shapes=[
            pltpu.VMEM((3, planes, 8, 128), F32),
            pltpu.VMEM((3, planes, 8, 128), F32),
            pltpu.VMEM((planes, 3, 3, 3, 8, 128), F32),
        ],
        compiler_params=params(30),
        name="sweeps",
    )(odd, *rows, *wall_rows, coef, step, wall)


def swap(block, partner):
    struct_count, fluid_count = lax.axis_size("struct"), lax.axis_size("fluid")
    route = []
    for s in range(struct_count):
        for f in range(fluid_count):
            to_s, to_f = partner(s, f)
            route.append((s * fluid_count + f, to_s * fluid_count + to_f % fluid_count))
    return lax.ppermute(block, BOTH, route)


def widen(block, even):
    count = block.shape[2]
    first, last = block[:, :, :DEPTH], block[:, :, count - DEPTH :]
    in_pair = swap(jnp.where(even, last, first), lambda s, f: (s, f ^ 1))
    next_pair = swap(jnp.where(even, first, last), lambda s, f: (s, ((f - 1) ^ 1) + 1))
    before = jnp.where(even, next_pair, in_pair)
    after = jnp.where(even, in_pair, next_pair)
    return jnp.concatenate([before, block, after], axis=2)


def all_rows(block):
    return [block] + [swap(block, lambda s, f, m=m: (s ^ m, f)) for m in (1, 2, 3)]


def shards(shell_motion, owner, stencil_slot, stencil_weight, prev_motion, node_offset, cell_split):
    odd = (lax.axis_index("struct") % 2).astype(I32).reshape(1)
    even = lax.axis_index("fluid") % 2 == 0
    packed = pack(owner, shell_motion)
    fields = jnp.concatenate([node_offset, cell_split.astype(F32)[None], prev_motion])
    rows = all_rows(widen(fields, even))
    received = lax.all_to_all(packed, BOTH, split_axis=0, concat_axis=0, tiled=True)
    coef, step = assemble(odd, rows)
    wall = gather(received, stencil_slot, stencil_weight)
    wall_rows = all_rows(widen(wall, even))
    return sweeps(odd, rows, wall_rows, coef, step, wall)


def solution(mesh):
    return jax.shard_map(
        shards,
        mesh=mesh,
        in_specs=(
            P(None, BOTH),
            P(BOTH, None),
            P(None, "struct", "fluid", None),
            P(None, "struct", "fluid", None),
            P(None, "struct", "fluid", None),
            P(None, "struct", "fluid", None),
            P("struct", "fluid", None),
        ),
        out_specs=P(None, "struct", "fluid", None),
        check_vma=False,
    )
```

time: 192 us -> 71.5 us (0.37)
  local copies, waits for them, and re-layouts: 78.6 us -> 3.18 us
  waiting for transfers between devices: 66 us -> 19.1 us
  Pallas kernels: 0 us -> 25.8 us
  other arithmetic: 21.9 us -> 2.48 us
  starting transfers between devices: 23.5 us -> 20.3 us
    ppermute x20 -> x10, waiting for transfers between devices: 60.4 us -> 8.44 us  [swap(): return lax.ppermute(block, BOTH, route)]
    gather x1 -> x0, local copies, waits for them, and re-layouts: 31.1 us -> none  [shards(): jnp.take(received, stencil_slot.reshape(-1), axis=1)]
    pallas_call x0 -> x4, Pallas kernels: none -> 25.8 us  [the longest x1 10.1 us: sweeps(): pl.pallas_call(sweep_kernel, out_shape=jax.ShapeDtypeStruct((3, 2, planes...]
    scatter x1 -> x0, local copies, waits for them, and re-layouts: 24.5 us -> none  [shards(): jnp.zeros((3, devices * capacity), jnp.float32).at[:, slot_place]]
    reduce_sum x49 -> x0, other arithmetic: 10.5 us -> none  [the longest x1 6.12 us: shards(): wall_values = jnp.sum(stencil_weight[None] * gathered, axis=1)]
    reshape x1 -> x0, local copies, waits for them, and re-layouts: 5.95 us -> none  [shards(): packed.reshape(3, devices, capacity)]
    all_to_all x1, waiting for transfers between devices: 5.54 us -> 10.7 us  [shards(): lax.all_to_all(packed, BOTH, split_axis=0, concat_axis=0, tiled=True)]
    all_to_all x1 -> x0, local copies, waits for them, and re-layouts: 4.86 us -> none  [shards(): lax.all_to_all(packed.reshape(3, devices, capacity), ('struct', 'fluid'),...]
  transfers between devices with their start and end apart: 21 -> 11, of which waited for: 20 -> 4; matrix products, arithmetic and copies ran while one was open for 24% -> 1% of each run, Pallas kernels for 0% -> 19%
where the time goes in v1:
time: 71.5 us; the launch traced here: 71 us
  Pallas kernels  25.8 us (36%)
  starting transfers between devices  20.3 us (28%)
  waiting for transfers between devices  19.1 us (27%)
  local copies, waits for them, and re-layouts  3.18 us (4%)
  other arithmetic  2.48 us (3%)
    ppermute x10, starting transfers between devices, swap(): return lax.ppermute(block, BOTH, route)  13.7 us
    all_to_all x1, waiting for transfers between devices, shards(): lax.all_to_all(packed, BOTH, split_axis=0, concat_axis=0, tiled=True)  10.7 us
    pallas_call x1, Pallas kernels, sweeps(): pl.pallas_call(sweep_kernel, out_shape=jax.ShapeDtypeStruct((3, 2, planes...  10.1 us
    pallas_call x1, Pallas kernels, assemble(): pl.pallas_call(assemble_kernel, out_shape=(jax.ShapeDtypeStruct((planes,...  9.56 us
    ppermute x10, waiting for transfers between devices, swap(): return lax.ppermute(block, BOTH, route)  8.44 us
    all_to_all x1, starting transfers between devices, shards(): lax.all_to_all(packed, BOTH, split_axis=0, concat_axis=0, tiled=True)  6.53 us
    pallas_call x1, Pallas kernels, pack(): pl.pallas_call(pack_kernel, out_shape=jax.ShapeDtypeStruct((128, 3, 128),...  4.07 us
    unnamed x8, local copies, waits for them, and re-layouts  3.18 us
  transfers between devices with their start and end apart: 11, of which 4 were waited for; matrix products, arithmetic and copies ran while one was open for 1% of the time, Pallas kernels for 19%

profile of v1, /device:TPU:0, one launch (start us, length us, event | category | flops | bytes accessed | tf_op | source)
XLA Modules:
  0.0 71.0 jit_solution(98231601649850703)
XLA Ops:
  0.0 0.7 %convert_bitcast_fusion = f32[1,2,8,256]{3,2,1,0:T(8,128)S(1)} fusion(s32[2,8,256]{2,1,0:T(8,128)} %param.13), kind=kLoop, calls=%fused_computation.7 | loop fusion | flops 4096 | bytes 32768 | tf_op jit(solution)/shard_map/broadcast_in_dim | solution.py:426
  0.7 0.8 %pad_maximum_fusion.1 = f32[7,2,8,256]{3,2,1,0:T(8,128)S(1)} fusion(f32[3,2,8,256]{3,2,1,0:T(8,128)} %param.11, f32[1,2,8,256]{3,2,1,0:T(8,128)S(1)} %convert_bitcast_fusion, f32[3,2,8,256]{3,2,1,0:T(8,128)} %param.12), kind=kLoop, calls=%fused_computation.1 | loop fusion | flops 57344 | bytes 229376 | tf_op jit(solution)/shard_map/concatenate | solution.py:426
  1.6 6.1 %collective-permute-start = (f32[7,2,4,256]{3,2,1,0:T(4,128)S(1)}, f32[7,2,4,256]{3,2,1,0:T(4,128)S(1)}, u32[]{:S(2)}, u32[]{:S(2)}) collective-permute-start(f32[7,2,4,256]{3,2,1,0:T(4,128)S(1)} %get-tuple-element.11), channel_id=1, source_target_pairs={{0,31},{1,2},{2,1},{3,4},{4,3},{5,6},{6,5},{7,8},{8,7},{9,10},{10,... | collective-permute-start | bytes 172040 | tf_op jit(solution)/shard_map/ppermute | solution.py:405
  7.7 0.9 %copy-done = f32[3,8192]{1,0:T(4,128)S(1)} copy-done((f32[3,8192]{1,0:T(4,128)S(1)}, f32[3,8192]{1,0:T(4,128)}, u32[]{:S(2)}) %copy-start) | copy-done | bytes 98328
  8.6 0.8 %copy-done.1 = s32[8192,1]{0,1:T(1,128)S(1)} copy-done((s32[8192,1]{0,1:T(1,128)S(1)}, s32[8192,1]{0,1:T(1,128)}, u32[]{:S(2)}) %copy-start.1) | copy-done | bytes 32792
  9.3 4.1 %pack.1 = f32[128,3,128]{2,1,0:T(4,128)} custom-call(s32[1,8192]{1,0:T(1,128)S(1)} %bitcast.12, f32[3,8192]{1,0:T(4,128)S(1)} %copy-done), custom_call_target="tpu_custom_call" | custom-call | tf_op jit(solution)/shard_map/pack/pallas_call | solution.py:68
  13.4 6.5 %all-to-all-start = ((f32[128,3,128]{2,1,0:T(4,128)}), f32[128,3,128]{2,1,0:T(4,128)S(1)}, u32[]{:S(2)}, u32[]{:S(2)}) async-start(f32[128,3,128]{2,1,0:T(4,128)} %pack.1), calls=%async_computation | async-start | bytes 524288 | tf_op jit(solution)/shard_map/all_to_all | solution.py:428
  19.9 0.0 collective-permute-done
  20.0 10.7 %all-to-all-done.received_ref = f32[128,3,128]{2,1,0:T(4,128)S(1)} async-done(((f32[128,3,128]{2,1,0:T(4,128)}), f32[128,3,128]{2,1,0:T(4,128)S(1)}, u32[]{:S(2)}, u32[]{:S(2)}) %all-to-all-start) | async-done | bytes 196640 | tf_op jit(solution)/shard_map/all_to_all | solution.py:428
  30.7 0.8 %copy-done.2 = s32[4,2,8,128]{3,2,1,0:T(8,128)S(1)} copy-done((s32[4,2,8,128]{3,2,1,0:T(8,128)S(1)}, s32[4,2,8,128]{3,2,1,0:T(8,128)}, u32[]{:S(2)}) %copy-start.2) | copy-done | bytes 32792
  31.5 0.8 %copy-done.3 = f32[4,2,8,128]{3,2,1,0:T(8,128)S(1)} copy-done((f32[4,2,8,128]{3,2,1,0:T(8,128)S(1)}, f32[4,2,8,128]{3,2,1,0:T(8,128)}, u32[]{:S(2)}) %copy-start.3) | copy-done | bytes 32792
  32.2 2.1 %gather.1.refs_10_ = f32[3,2,8,128]{3,2,1,0:T(8,128)S(1)} custom-call(f32[128,3,128]{2,1,0:T(4,128)S(1)} %all-to-all-done.received_ref, s32[4,2,8,128]{3,2,1,0:T(8,128)S(1)} %copy-done.2, f32[4,2,8,128]{3,2,1,0:T(8,128)S(1)} %copy-done.3), custom_call_target="tpu_custom_call" | custom-call | tf_op jit(solution)/shard_map/gather/pallas_call | solution.py:111
  34.3 0.7 %collective-permute-start.5 = (f32[3,2,4,128]{3,2,1,0:T(4,128)S(1)}, f32[3,2,4,128]{3,2,1,0:T(4,128)S(1)}, u32[]{:S(2)}, u32[]{:S(2)}) collective-permute-start(f32[3,2,4,128]{3,2,1,0:T(4,128)S(1)} %get-tuple-element.15), channel_id=1, source_target_pairs={{0,31},{1,2},{2,1},{3,4},{4,3},{5,6},{6,5},{7,8},{8,7},{9,10},{10,... | collective-permute-start | bytes 36872 | tf_op jit(solution)/shard_map/ppermute | solution.py:405
  35.0 0.9 %pad_maximum_fusion.own_ref.refs_0_ = f32[7,2,16,256]{3,2,1,0:T(8,128)S(1)} fusion(f32[7,2,4,256]{3,2,1,0:T(4,128)S(1)} %bitcast.14, f32[3,2,8,256]{3,2,1,0:T(8,128)} %param.11, f32[1,2,8,256]{3,2,1,0:T(8,128)S(1)} %convert_bitcast_fusion, f32[3,2,8,256]{3,2,1,0:T(8,128)} %param.12, f32[7,2,4,256]{3,2,1,0:T(4,128)S(1)} %bitcast.13), kind=kLoop, calls=%fused_computation | loop fusion | flops 229376 | bytes 458752 | tf_op jit(solution)/shard_map/concatenate | solution.py:415
  35.9 1.2 %collective-permute-start.4 = (f32[7,2,16,256]{3,2,1,0:T(8,128)S(1)}, f32[7,2,16,256]{3,2,1,0:T(8,128)S(1)}, u32[]{:S(2)}, u32[]{:S(2)}) collective-permute-start(f32[7,2,16,256]{3,2,1,0:T(8,128)S(1)} %pad_maximum_fusion.own_ref.refs_0_), channel_id=1, source_target_pairs={{0,96},{1,97},{2,98},{3,99},{4,100},{5,101},{6,102},{7,103},{8,104... | collective-permute-start | bytes 688136 | tf_op jit(solution)/shard_map/ppermute | solution.py:405
  37.1 1.5 %collective-permute-start.3 = (f32[7,2,16,256]{3,2,1,0:T(8,128)S(1)}, f32[7,2,16,256]{3,2,1,0:T(8,128)S(1)}, u32[]{:S(2)}, u32[]{:S(2)}) collective-permute-start(f32[7,2,16,256]{3,2,1,0:T(8,128)S(1)} %pad_maximum_fusion.own_ref.refs_0_), channel_id=1, source_target_pairs={{0,64},{1,65},{2,66},{3,67},{4,68},{5,69},{6,70},{7,71},{8,72},{9,... | collective-permute-start | bytes 688136 | tf_op jit(solution)/shard_map/ppermute | solution.py:405
  38.6 1.5 %collective-permute-start.2 = (f32[7,2,16,256]{3,2,1,0:T(8,128)S(1)}, f32[7,2,16,256]{3,2,1,0:T(8,128)S(1)}, u32[]{:S(2)}, u32[]{:S(2)}) collective-permute-start(f32[7,2,16,256]{3,2,1,0:T(8,128)S(1)} %pad_maximum_fusion.own_ref.refs_0_), channel_id=1, source_target_pairs={{0,32},{1,33},{2,34},{3,35},{4,36},{5,37},{6,38},{7,39},{8,40},{9,... | collective-permute-start | bytes 688136 | tf_op jit(solution)/shard_map/ppermute | solution.py:405
  40.1 0.7 %collective-permute-done.5 = f32[3,2,4,128]{3,2,1,0:T(4,128)S(1)} collective-permute-done((f32[3,2,4,128]{3,2,1,0:T(4,128)S(1)}, f32[3,2,4,128]{3,2,1,0:T(4,128)S(1)}, u32[]{:S(2)}, u32[]{:S(2)}) %collective-permute-start.5) | collective-permute-done | bytes 12320 | tf_op jit(solution)/shard_map/ppermute | solution.py:405
  40.8 1.2 %collective-permute-start.9 = (f32[3,2,16,128]{3,2,1,0:T(8,128)S(1)}, f32[3,2,16,128]{3,2,1,0:T(8,128)S(1)}, u32[]{:S(2)}, u32[]{:S(2)}) collective-permute-start(f32[3,2,16,128]{3,2,1,0:T(8,128)S(1)} %pad_maximum_fusion.2.refs_4_), channel_id=1, source_target_pairs={{0,96},{1,97},{2,98},{3,99},{4,100},{5,101},{6,102},{7,103},{8,104... | collective-permute-start | bytes 147464 | tf_op jit(solution)/shard_map/ppermute | solution.py:405
  42.1 1.5 %collective-permute-start.8 = (f32[3,2,16,128]{3,2,1,0:T(8,128)S(1)}, f32[3,2,16,128]{3,2,1,0:T(8,128)S(1)}, u32[]{:S(2)}, u32[]{:S(2)}) collective-permute-start(f32[3,2,16,128]{3,2,1,0:T(8,128)S(1)} %pad_maximum_fusion.2.refs_4_), channel_id=1, source_target_pairs={{0,64},{1,65},{2,66},{3,67},{4,68},{5,69},{6,70},{7,71},{8,72},{9,... | collective-permute-start | bytes 147464 | tf_op jit(solution)/shard_map/ppermute | solution.py:405
  43.6 6.9 %collective-permute-done.4.swap3_ref.refs_3_ = f32[7,2,16,256]{3,2,1,0:T(8,128)S(1)} collective-permute-done((f32[7,2,16,256]{3,2,1,0:T(8,128)S(1)}, f32[7,2,16,256]{3,2,1,0:T(8,128)S(1)}, u32[]{:S(2)}, u32[]{:S(2)}) %collective-permute-start.4) | collective-permute-done | bytes 229408 | tf_op jit(solution)/shard_map/ppermute | solution.py:405
  50.5 0.8 %collective-permute-done.2.swap1_ref.refs_1_ = f32[7,2,16,256]{3,2,1,0:T(8,128)S(1)} collective-permute-done((f32[7,2,16,256]{3,2,1,0:T(8,128)S(1)}, f32[7,2,16,256]{3,2,1,0:T(8,128)S(1)}, u32[]{:S(2)}, u32[]{:S(2)}) %collective-permute-start.2) | collective-permute-done | bytes 229408 | tf_op jit(solution)/shard_map/ppermute | solution.py:405
  51.3 9.6 %assemble.1 = (f32[16,27,6,8,128]{4,3,2,1,0:T(8,128)S(1)}, f32[16,3,8,128]{3,2,1,0:T(8,128)S(1)}) custom-call(s32[1]{0:T(128)} %bitcast.odd_ref, f32[7,2,16,256]{3,2,1,0:T(8,128)S(1)} %pad_maximum_fusion.own_ref.refs_0_, f32[7,2,16,256]{3,2,1,0:T(8,128)S(1)} %collective-permute-done.2.swap1_ref.refs_1_, ...), custom_call_target="tpu_custom_call" | custom-call | flops 200000000 | bytes 12000000 | tf_op jit(solution)/shard_map/assemble/pallas_call | solution.py:320
  60.9 10.1 %sweeps.1 = f32[3,2,8,256]{3,2,1,0:T(8,128)} custom-call(s32[1]{0:T(128)} %bitcast.odd_ref, f32[7,2,16,256]{3,2,1,0:T(8,128)S(1)} %pad_maximum_fusion.own_ref.refs_0_, f32[7,2,16,256]{3,2,1,0:T(8,128)S(1)} %collective-permute-done.2.swap1_ref.refs_1_, f32[7,2,16,256]{3,2,1,0:T(8,128)S(1)} %collective-permute-done.3.swap2_ref.refs_2_, ...), custom_call_target="tpu_custom_call" | custom-call | tf_op jit(solution)/shard_map/sweeps/pallas_call | solution.py:383
  (18 shorter events, 0.1 us)
Async XLA Ops:
  1.6 18.4 %collective-permute-start = (f32[7,2,4,256]{3,2,1,0:T(4,128)S(1)}, f32[7,2,4,256]{3,2,1,0:T(4,128)S(1)}, u32[]{:S(2)}, u32[]{:S(2)}) collective-permute-start(f32[7,2,4,256]{3,2,1,0:T(4,128)S(1)} %get-tuple-element.11), channel_id=1, source_target_pairs={{0,31},{1,2},{2,1},{3,4},{4,3},{5,6},{6,5},{7,8},{8,7},{9,10},{10,... | collective-permute-start | bytes 172040 | tf_op jit(solution)/shard_map/ppermute | solution.py:405
  7.7 12.3 %collective-permute-start.1 = (f32[7,2,4,256]{3,2,1,0:T(4,128)S(1)}, f32[7,2,4,256]{3,2,1,0:T(4,128)S(1)}, u32[]{:S(2)}, u32[]{:S(2)}) collective-permute-start(f32[7,2,4,256]{3,2,1,0:T(4,128)S(1)} %get-tuple-element.12), channel_id=1, source_target_pairs={{0,1},{1,0},{2,3},{3,2},{4,5},{5,4},{6,7},{7,6},{8,9},{9,8},{10,11... | collective-permute-start | bytes 172040 | tf_op jit(solution)/shard_map/ppermute | solution.py:405
  7.7 0.9 %copy-start = (f32[3,8192]{1,0:T(4,128)S(1)}, f32[3,8192]{1,0:T(4,128)}, u32[]{:S(2)}) copy-start(f32[3,8192]{1,0:T(4,128)} %value_ref.1) | copy-start | bytes 294916
  8.6 0.8 %copy-start.1 = (s32[8192,1]{0,1:T(1,128)S(1)}, s32[8192,1]{0,1:T(1,128)}, u32[]{:S(2)}) copy-start(s32[8192,1]{0,1:T(1,128)} %param.8) | copy-start | bytes 98308
  13.4 17.3 %all-to-all-start = ((f32[128,3,128]{2,1,0:T(4,128)}), f32[128,3,128]{2,1,0:T(4,128)S(1)}, u32[]{:S(2)}, u32[]{:S(2)}) async-start(f32[128,3,128]{2,1,0:T(4,128)} %pack.1), calls=%async_computation | async-start | bytes 524288 | tf_op jit(solution)/shard_map/all_to_all | solution.py:428
  30.7 0.8 %copy-start.2 = (s32[4,2,8,128]{3,2,1,0:T(8,128)S(1)}, s32[4,2,8,128]{3,2,1,0:T(8,128)}, u32[]{:S(2)}) copy-start(s32[4,2,8,128]{3,2,1,0:T(8,128)} %slot_ref.1) | copy-start | bytes 98308
  31.5 0.8 %copy-start.3 = (f32[4,2,8,128]{3,2,1,0:T(8,128)S(1)}, f32[4,2,8,128]{3,2,1,0:T(8,128)}, u32[]{:S(2)}) copy-start(f32[4,2,8,128]{3,2,1,0:T(8,128)} %weight_ref.1) | copy-start | bytes 98308
  34.3 6.5 %collective-permute-start.5 = (f32[3,2,4,128]{3,2,1,0:T(4,128)S(1)}, f32[3,2,4,128]{3,2,1,0:T(4,128)S(1)}, u32[]{:S(2)}, u32[]{:S(2)}) collective-permute-start(f32[3,2,4,128]{3,2,1,0:T(4,128)S(1)} %get-tuple-element.15), channel_id=1, source_target_pairs={{0,31},{1,2},{2,1},{3,4},{4,3},{5,6},{6,5},{7,8},{8,7},{9,10},{10,... | collective-permute-start | bytes 36872 | tf_op jit(solution)/shard_map/ppermute | solution.py:405
  35.0 5.8 %collective-permute-start.6 = (f32[3,2,4,128]{3,2,1,0:T(4,128)S(1)}, f32[3,2,4,128]{3,2,1,0:T(4,128)S(1)}, u32[]{:S(2)}, u32[]{:S(2)}) collective-permute-start(f32[3,2,4,128]{3,2,1,0:T(4,128)S(1)} %get-tuple-element.16), channel_id=1, source_target_pairs={{0,1},{1,0},{2,3},{3,2},{4,5},{5,4},{6,7},{7,6},{8,9},{9,8},{10,11... | collective-permute-start | bytes 36872 | tf_op jit(solution)/shard_map/ppermute | solution.py:405
  35.9 14.6 %collective-permute-start.4 = (f32[7,2,16,256]{3,2,1,0:T(8,128)S(1)}, f32[7,2,16,256]{3,2,1,0:T(8,128)S(1)}, u32[]{:S(2)}, u32[]{:S(2)}) collective-permute-start(f32[7,2,16,256]{3,2,1,0:T(8,128)S(1)} %pad_maximum_fusion.own_ref.refs_0_), channel_id=1, source_target_pairs={{0,96},{1,97},{2,98},{3,99},{4,100},{5,101},{6,102},{7,103},{8,104... | collective-permute-start | bytes 688136 | tf_op jit(solution)/shard_map/ppermute | solution.py:405
  37.1 13.4 %collective-permute-start.3 = (f32[7,2,16,256]{3,2,1,0:T(8,128)S(1)}, f32[7,2,16,256]{3,2,1,0:T(8,128)S(1)}, u32[]{:S(2)}, u32[]{:S(2)}) collective-permute-start(f32[7,2,16,256]{3,2,1,0:T(8,128)S(1)} %pad_maximum_fusion.own_ref.refs_0_), channel_id=1, source_target_pairs={{0,64},{1,65},{2,66},{3,67},{4,68},{5,69},{6,70},{7,71},{8,72},{9,... | collective-permute-start | bytes 688136 | tf_op jit(solution)/shard_map/ppermute | solution.py:405
  38.6 12.7 %collective-permute-start.2 = (f32[7,2,16,256]{3,2,1,0:T(8,128)S(1)}, f32[7,2,16,256]{3,2,1,0:T(8,128)S(1)}, u32[]{:S(2)}, u32[]{:S(2)}) collective-permute-start(f32[7,2,16,256]{3,2,1,0:T(8,128)S(1)} %pad_maximum_fusion.own_ref.refs_0_), channel_id=1, source_target_pairs={{0,32},{1,33},{2,34},{3,35},{4,36},{5,37},{6,38},{7,39},{8,40},{9,... | collective-permute-start | bytes 688136 | tf_op jit(solution)/shard_map/ppermute | solution.py:405
  40.8 20.0 %collective-permute-start.9 = (f32[3,2,16,128]{3,2,1,0:T(8,128)S(1)}, f32[3,2,16,128]{3,2,1,0:T(8,128)S(1)}, u32[]{:S(2)}, u32[]{:S(2)}) collective-permute-start(f32[3,2,16,128]{3,2,1,0:T(8,128)S(1)} %pad_maximum_fusion.2.refs_4_), channel_id=1, source_target_pairs={{0,96},{1,97},{2,98},{3,99},{4,100},{5,101},{6,102},{7,103},{8,104... | collective-permute-start | bytes 147464 | tf_op jit(solution)/shard_map/ppermute | solution.py:405
  42.1 18.8 %collective-permute-start.8 = (f32[3,2,16,128]{3,2,1,0:T(8,128)S(1)}, f32[3,2,16,128]{3,2,1,0:T(8,128)S(1)}, u32[]{:S(2)}, u32[]{:S(2)}) collective-permute-start(f32[3,2,16,128]{3,2,1,0:T(8,128)S(1)} %pad_maximum_fusion.2.refs_4_), channel_id=1, source_target_pairs={{0,64},{1,65},{2,66},{3,67},{4,68},{5,69},{6,70},{7,71},{8,72},{9,... | collective-permute-start | bytes 147464 | tf_op jit(solution)/shard_map/ppermute | solution.py:405
  50.5 10.4 %collective-permute-start.7 = (f32[3,2,16,128]{3,2,1,0:T(8,128)S(1)}, f32[3,2,16,128]{3,2,1,0:T(8,128)S(1)}, u32[]{:S(2)}, u32[]{:S(2)}) collective-permute-start(f32[3,2,16,128]{3,2,1,0:T(8,128)S(1)} %pad_maximum_fusion.2.refs_4_), channel_id=1, source_target_pairs={{0,32},{1,33},{2,34},{3,35},{4,36},{5,37},{6,38},{7,39},{8,40},{9,... | collective-permute-start | bytes 147464 | tf_op jit(solution)/shard_map/ppermute | solution.py:405

commit v2 on v1

--- a/solution.py
+++ b/solution.py
@@ -1,3 +1,5 @@
+from functools import partial
+
 import jax
 import jax.numpy as jnp
 from jax import lax
@@ -18,15 +20,31 @@
 ENTRY = ((0, 3, 4), (3, 1, 5), (4, 5, 2))
 BOTH = ("struct", "fluid")
 DEPTH = SWEEPS
+SETUP_FLOPS, PLANE_FLOPS = 20000000, 20000000
+FULL = 63
 F32, BF16, I32 = jnp.float32, jnp.bfloat16, jnp.int32
 VMEM = pl.BlockSpec(memory_space=pltpu.VMEM)
+SMEM = pl.BlockSpec(memory_space=pltpu.SMEM)
+HBM = pl.BlockSpec(memory_space=pltpu.HBM)
+
+
+def fetch(sources, targets, semaphores):
+    copies = [
+        pltpu.make_async_copy(source, target, semaphores.at[k])
+        for k, (source, target) in enumerate(zip(sources, targets))
+    ]
+    for copy in copies:
+        copy.start()
+    for copy in copies:
+        copy.wait()
 
 
 def params(mebibytes):
-    return pltpu.CompilerParams(vmem_limit_bytes=mebibytes * 2**20)
-
-
-def pack_kernel(owner_ref, value_ref, out_ref, left_ref, right_ref):
+    return pltpu.CompilerParams(vmem_limit_bytes=int(mebibytes * 2**20))
+
+
+def pack_kernel(owner_hbm, value_hbm, out_ref, left_ref, right_ref, owner_ref, value_ref, semaphores):
+    fetch((owner_hbm, value_hbm), (owner_ref, value_ref), semaphores)
     count = owner_ref.shape[1]
     width = 256
     rows = lax.broadcasted_iota(I32, (width, width + 128), 0)
@@ -68,15 +86,82 @@
     return pl.pallas_call(
         pack_kernel,
         out_shape=jax.ShapeDtypeStruct((128, 3, 128), F32),
-        in_specs=[VMEM] * 2,
+        in_specs=[HBM] * 2,
         out_specs=VMEM,
-        scratch_shapes=[pltpu.VMEM((384, count), BF16), pltpu.VMEM((256, count), BF16)],
-        compiler_params=params(24),
+        scratch_shapes=[
+            pltpu.VMEM((384, count), BF16),
+            pltpu.VMEM((256, count), BF16),
+            pltpu.VMEM((1, count), I32),
+            pltpu.VMEM((3, count), F32),
+            pltpu.SemaphoreType.DMA((2,)),
+        ],
+        compiler_params=params(FULL),
         name="pack",
     )(owner.reshape(1, count), shell_motion)
 
 
-def gather_kernel(received_ref, slot_ref, weight_ref, out_ref, table_ref):
+def payload(channels):
+    return (
+        jax.ShapeDtypeStruct((channels, 2, 8, 128), F32),
+        jax.ShapeDtypeStruct((channels, 2, DEPTH, 128), F32),
+        jax.ShapeDtypeStruct((channels, 2, DEPTH, 128), F32),
+    )
+
+
+def emit(refs, even, channel, y, value):
+    whole_ref, pair_ref, next_ref = refs
+    first, last = value[:DEPTH], value[DEPTH:]
+    whole_ref[channel, y] = value
+    pair_ref[channel, y] = jnp.where(even, last, first)
+    next_ref[channel, y] = jnp.where(even, first, last)
+
+
+def fields_kernel(even_ref, offset_hbm, split_hbm, prev_hbm, slot_hbm, weight_hbm, *refs):
+    out_refs, (slot_ref, weight_ref, offset_ref, split_ref, prev_ref, semaphores) = refs[:3], refs[3:]
+    fetch(
+        (offset_hbm, split_hbm, prev_hbm, slot_hbm, weight_hbm),
+        (offset_ref, split_ref, prev_ref, slot_ref, weight_ref),
+        semaphores,
+    )
+    even = even_ref[0] == 1
+    lane = lax.broadcasted_iota(I32, (8, 128), 1)
+    for y in range(2):
+        code = split_ref[y].astype(F32)
+        columns = jnp.where(lane == 3, pltpu.roll(code[:, :128], 4, 1), 0.0)
+        for p in range(3):
+            wall, free = offset_ref[p, y, :, :128], offset_ref[p, y, :, 128:]
+            columns = jnp.where(lane == p, pltpu.roll(wall, p + 1, 1), columns)
+            columns = jnp.where(lane == 4 + p, pltpu.roll(free, 4 + p, 1), columns)
+            columns = jnp.where(lane == 125 + p, pltpu.roll(wall, 125 + p, 1), columns)
+            emit(out_refs, even, p, y, free)
+            emit(out_refs, even, 5 + p, y, prev_ref[p, y, :, 128:])
+        emit(out_refs, even, 3, y, code[:, 128:])
+        emit(out_refs, even, 4, y, columns)
+
+
+def fields(even, node_offset, cell_split, prev_motion, stencil_slot, stencil_weight):
+    return pl.pallas_call(
+        fields_kernel,
+        out_shape=(
+            *payload(8),
+            jax.ShapeDtypeStruct(stencil_slot.shape, I32),
+            jax.ShapeDtypeStruct(stencil_weight.shape, F32),
+        ),
+        in_specs=[SMEM] + [HBM] * 5,
+        out_specs=(VMEM,) * 5,
+        scratch_shapes=[
+            pltpu.VMEM(node_offset.shape, F32),
+            pltpu.VMEM(cell_split.shape, I32),
+            pltpu.VMEM(prev_motion.shape, F32),
+            pltpu.SemaphoreType.DMA((5,)),
+        ],
+        compiler_params=params(FULL),
+        name="fields",
+    )(even, node_offset, cell_split, prev_motion, stencil_slot, stencil_weight)
+
+
+def gather_kernel(even_ref, received_ref, slot_ref, weight_ref, out_ref, *more_refs):
+    column_refs, table_ref = more_refs[:3], more_refs[3]
     for c in range(3):
         flat = received_ref[:, c, :].T
         high = flat.astype(BF16).astype(F32)
@@ -105,18 +190,26 @@
                 line = jnp.sum(total[c], axis=0, keepdims=True)
                 for k in BITS:
                     out_ref[c, y, z + k : z + k + 1, :] = line[:, k * 128 : k * 128 + 128]
-
-
-def gather(received, stencil_slot, stencil_weight):
+    lane = lax.broadcasted_iota(I32, (8, 128), 1)
+    for y in range(2):
+        columns = jnp.zeros((8, 128), F32)
+        for c in range(3):
+            wall = out_ref[c, y]
+            columns = jnp.where(lane == c, pltpu.roll(wall, c + 1, 1), columns)
+            columns = jnp.where(lane == 125 + c, pltpu.roll(wall, 125 + c, 1), columns)
+        emit(column_refs, even_ref[0] == 1, 0, y, columns)
+
+
+def gather(even, received, stencil_slot, stencil_weight):
     return pl.pallas_call(
         gather_kernel,
-        out_shape=jax.ShapeDtypeStruct((3, 2, 8, 128), F32),
-        in_specs=[VMEM] * 3,
-        out_specs=VMEM,
+        out_shape=(jax.ShapeDtypeStruct((3, 2, 8, 128), F32), *payload(1)),
+        in_specs=[SMEM] + [VMEM] * 3,
+        out_specs=(VMEM,) * 4,
         scratch_shapes=[pltpu.VMEM((384, 256), BF16)],
         compiler_params=params(16),
         name="gather",
-    )(received, stencil_slot, stencil_weight)
+    )(even, received, stencil_slot, stencil_weight)
 
 
 def cross(u, v):
@@ -210,97 +303,180 @@
     )
 
 
-def fill_rows(target_ref, rows_refs, odd, channel, to, lanes):
+def fill_rows(target_ref, rows_refs, odd, channel, to):
     own, swap1, swap2, swap3 = rows_refs
     for r in range(2):
-        one, three = swap1[channel, r, :, lanes], swap3[channel, r, :, lanes]
+        one, three = swap1[channel, r], swap3[channel, r]
         for place, value in (
-            (0, own[channel, r, :, lanes]),
+            (0, own[channel, r]),
             (2, jnp.where(odd, three, one)),
-            (4, swap2[channel, r, :, lanes]),
+            (4, swap2[channel, r]),
             (6, jnp.where(odd, one, three)),
         ):
             target_ref[to, :, place + r, :] = value
 
 
-def assemble_kernel(odd_ref, own_ref, swap1_ref, swap2_ref, swap3_ref, coef_ref, step_ref, field_ref):
+def back_y(values):
+    return [pltpu.roll(v, 1, 0) for v in values]
+
+
+def plus(u, v):
+    return [p + q for p, q in zip(u, v)]
+
+
+MOVING = ("z", "xz_up", "xz_down", "yz_up", "yz_down", "b00", "b01", "b10", "b11") + tuple(
+    (name, c) for c in BITS for name in ("x", "y", "up", "down")
+)
+
+
+def node_parts(kinds):
+    x, y, z = kinds["x"], kinds["y"], kinds["z"]
+    (xz_up0, xz_down0), (xz_up1, xz_down1) = kinds["xz"]
+    (yz_up0, yz_down0), (yz_up1, yz_down1) = kinds["yz"]
+    body = {key: (v, back_y(v)) for key, v in kinds["xyz"].items()}
+    moving = {
+        "z": plus(z[1, 0], back_y(z[1, 1])),
+        "xz_up": plus(xz_up0, back_y(xz_up1)),
+        "xz_down": plus(xz_down0, back_y(xz_down1)),
+        "yz_up": yz_up1,
+        "yz_down": yz_down1,
+        "b00": body[0, 0][1],
+        "b01": body[0, 1][1],
+        "b10": body[1, 0][0],
+        "b11": body[1, 1][0],
+    }
+    still = {
+        "z": plus(z[0, 0], back_y(z[0, 1])),
+        "yz_up": yz_up0,
+        "yz_down": yz_down0,
+        "b00": body[0, 0][0],
+        "b01": body[0, 1][0],
+        "b10": body[1, 0][1],
+        "b11": body[1, 1][1],
+    }
+    for c in BITS:
+        up, down = kinds["xy"][c]
+        moving["x", c] = plus(x[0, c], back_y(x[1, c]))
+        moving["y", c] = y[1, c]
+        moving["up", c] = back_y(up)
+        moving["down", c] = down
+        still["y", c] = y[0, c]
+        still["up", c] = up
+        still["down", c] = back_y(down)
+    return moving, still
+
+
+def setup_kernel(odd_ref, own_ref, swap1_ref, swap2_ref, swap3_ref, field_ref, side_ref):
     odd = odd_ref[0] == 1
-    for c in range(4):
-        fill_rows(field_ref, (own_ref, swap1_ref, swap2_ref, swap3_ref), odd, c, c, slice(None))
+    for c in range(5):
+        fill_rows(field_ref, (own_ref, swap1_ref, swap2_ref, swap3_ref), odd, c, c)
     planes = field_ref.shape[1]
-
-    def back_y(values):
-        return [pltpu.roll(v, 1, 0) for v in values]
-
-    def back_x(values):
-        return [pltpu.roll(v, 1, 1) for v in values]
-
-    def plus(u, v):
-        return [p + q for p, q in zip(u, v)]
-
-    def put(plane, step, values):
+    gap = 128 // planes
+    lane = lax.broadcasted_iota(I32, (8, 128), 1)
+
+    packed = jnp.zeros((8, 128), F32)
+    for k in range(planes):
+        packed = jnp.where(lane // gap == k, pltpu.roll(field_ref[4, k], k * gap, 1), packed)
+    corner = {}
+    for a in BITS:
+        for p in range(3):
+            low = pltpu.roll(packed, 128 - (4 * a + p), 1) if a or p else packed
+            for c, plane in ((0, low), (1, pltpu.roll(low, 128 - gap, 1))):
+                corner.setdefault((a, 0, c), []).append(plane)
+                corner.setdefault((a, 1, c), []).append(pltpu.roll(plane, 7, 0))
+    moving, _ = node_parts(cell_blocks(corner, pltpu.roll(packed, 125, 1)))
+    for m, name in enumerate(MOVING):
         for e in range(6):
-            coef_ref[plane, SLOT_OF[step], e] = values[e][:, 128:]
-
-    def add(plane, step, values):
-        for e in range(6):
-            at = SLOT_OF[step]
-            coef_ref[plane, at, e] = coef_ref[plane, at, e] + values[e][:, 128:]
+            side_ref[m, e] = moving[name][e]
+
+
+def setup(odd, rows):
+    planes = rows[0].shape[2]
+    return pl.pallas_call(
+        setup_kernel,
+        out_shape=(
+            jax.ShapeDtypeStruct((5, planes, 8, 128), F32),
+            jax.ShapeDtypeStruct((len(MOVING), 6, 8, 128), F32),
+        ),
+        in_specs=[SMEM] + [VMEM] * 4,
+        out_specs=(VMEM,) * 2,
+        compiler_params=params(4),
+        cost_estimate=pl.CostEstimate(flops=SETUP_FLOPS, bytes_accessed=1000000, transcendentals=0),
+        name="setup",
+    )(odd, *rows)
+
+
+def assemble_kernel(start, stop, field_ref, side_ref, coef_ref, step_ref):
+    planes = field_ref.shape[1]
+    gap = 128 // planes
+    lane = lax.broadcasted_iota(I32, (8, 128), 1)
+    first, last = lane == 0, lane == 127
 
     def cells(k, _):
         corner = {}
         for c in BITS:
+            edge = field_ref[4, k + c]
+            edges = (edge, pltpu.roll(edge, 7, 0))
             for p in range(3):
                 low = field_ref[p, k + c]
-                up = pltpu.roll(low, 7, 0)
-                for b, row in ((0, low), (1, up)):
+                for b, row in ((0, low), (1, pltpu.roll(low, 7, 0))):
+                    beyond = pltpu.roll(edges[b], 2 - p, 1) if p < 2 else edges[b]
                     corner.setdefault((0, b, c), []).append(row)
-                    corner.setdefault((1, b, c), []).append(pltpu.roll(row, 255, 1))
-        kinds = cell_blocks(corner, field_ref[3, k])
-        low, high = k, k + 1
-        z = kinds["z"]
-        both = [plus(z[a, 0], back_y(z[a, 1])) for a in BITS]
-        s = plus(both[0], back_x(both[1]))
+                    corner.setdefault((1, b, c), []).append(jnp.where(last, beyond, pltpu.roll(row, 127, 1)))
+        moving, still = node_parts(cell_blocks(corner, field_ref[3, k]))
+        shift = 128 - k * gap
+
+        def back_x(name):
+            m = MOVING.index(name)
+            return [
+                jnp.where(first, pltpu.roll(side_ref[m, e], shift, 1), pltpu.roll(moving[name][e], 1, 1))
+                for e in range(6)
+            ]
+
+        def put(plane, step, values):
+            for e in range(6):
+                coef_ref[plane, SLOT_OF[step], e] = values[e]
+
+        def add(plane, step, values):
+            at = SLOT_OF[step]
+            for e in range(6):
+                coef_ref[plane, at, e] = coef_ref[plane, at, e] + values[e]
+
+        low, high = k - start, k + 1 - start
+        s = plus(still["z"], back_x("z"))
         put(low, (0, 0, 1), s)
         put(high, (0, 0, -1), s)
-        (up0, down0), (up1, down1) = kinds["xz"]
-        s = plus(up0, back_y(up1))
-        put(low, (1, 0, 1), s)
-        put(high, (-1, 0, -1), back_x(s))
-        s = plus(down0, back_y(down1))
-        put(high, (1, 0, -1), s)
-        put(low, (-1, 0, 1), back_x(s))
-        (up0, down0), (up1, down1) = kinds["yz"]
-        s = plus(up0, back_x(up1))
+        put(low, (1, 0, 1), moving["xz_up"])
+        put(high, (-1, 0, -1), back_x("xz_up"))
+        put(high, (1, 0, -1), moving["xz_down"])
+        put(low, (-1, 0, 1), back_x("xz_down"))
+        s = plus(still["yz_up"], back_x("yz_up"))
         put(low, (0, 1, 1), s)
         put(high, (0, -1, -1), back_y(s))
-        s = plus(down0, back_x(down1))
+        s = plus(still["yz_down"], back_x("yz_down"))
         put(high, (0, 1, -1), s)
         put(low, (0, -1, 1), back_y(s))
-        body = kinds["xyz"]
-        put(low, (1, 1, 1), body[0, 0])
-        put(high, (-1, -1, -1), back_x(back_y(body[0, 0])))
-        put(high, (1, 1, -1), body[0, 1])
-        put(low, (-1, -1, 1), back_x(back_y(body[0, 1])))
-        put(low, (1, -1, 1), back_y(body[1, 0]))
-        put(high, (-1, 1, -1), back_x(body[1, 0]))
-        put(high, (1, -1, -1), back_y(body[1, 1]))
-        put(low, (-1, 1, 1), back_x(body[1, 1]))
+        put(low, (1, 1, 1), still["b00"])
+        put(high, (-1, -1, -1), back_x("b00"))
+        put(high, (1, 1, -1), still["b01"])
+        put(low, (-1, -1, 1), back_x("b01"))
+        put(low, (1, -1, 1), still["b10"])
+        put(high, (-1, 1, -1), back_x("b10"))
+        put(high, (1, -1, -1), still["b11"])
+        put(low, (-1, 1, 1), back_x("b11"))
         for c, plane, store in ((0, low, add), (1, high, put)):
-            s = plus(kinds["x"][0, c], back_y(kinds["x"][1, c]))
-            store(plane, (1, 0, 0), s)
-            store(plane, (-1, 0, 0), back_x(s))
-            s = plus(kinds["y"][0, c], back_x(kinds["y"][1, c]))
+            store(plane, (1, 0, 0), moving["x", c])
+            store(plane, (-1, 0, 0), back_x(("x", c)))
+            s = plus(still["y", c], back_x(("y", c)))
             store(plane, (0, 1, 0), s)
             store(plane, (0, -1, 0), back_y(s))
-            up, down = kinds["xy"][c]
-            store(plane, (1, 1, 0), up)
-            store(plane, (-1, -1, 0), back_x(back_y(up)))
-            store(plane, (1, -1, 0), back_y(down))
-            store(plane, (-1, 1, 0), back_x(down))
+            store(plane, (1, 1, 0), still["up", c])
+            store(plane, (-1, -1, 0), back_x(("up", c)))
+            store(plane, (1, -1, 0), still["down", c])
+            store(plane, (-1, 1, 0), back_x(("down", c)))
         return 0
 
-    lax.fori_loop(0, planes - 1, cells, 0)
+    lax.fori_loop(start, stop, cells, 0)
 
     def selves(k, _):
         for e in range(6):
@@ -312,87 +488,110 @@
                 step_ref[k, e] = -RELAX_FACTOR / total
         return 0
 
-    lax.fori_loop(1, planes - 1, selves, 0)
-
-
-def assemble(odd, rows):
-    planes = rows[0].shape[2]
+    lax.fori_loop(1, stop - start, selves, 0)
+
+
+def assemble(field, side, start, stop):
     return pl.pallas_call(
-        assemble_kernel,
+        partial(assemble_kernel, start, stop),
         out_shape=(
-            jax.ShapeDtypeStruct((planes, SELF + 1, 6, 8, 128), F32),
-            jax.ShapeDtypeStruct((planes, 3, 8, 128), F32),
+            jax.ShapeDtypeStruct((stop - start + 1, SELF + 1, 6, 8, 128), F32),
+            jax.ShapeDtypeStruct((stop - start + 1, 3, 8, 128), F32),
         ),
-        in_specs=[pl.BlockSpec(memory_space=pltpu.SMEM)] + [VMEM] * 4,
-        out_specs=(VMEM, VMEM),
-        scratch_shapes=[pltpu.VMEM((4, planes, 8, 256), F32)],
-        compiler_params=params(30),
-        cost_estimate=pl.CostEstimate(flops=200000000, bytes_accessed=12000000, transcendentals=0),
+        in_specs=[VMEM] * 2,
+        out_specs=(VMEM,) * 2,
+        compiler_params=params(4),
+        cost_estimate=pl.CostEstimate(
+            flops=PLANE_FLOPS * (stop - start), bytes_accessed=1000000, transcendentals=0
+        ),
         name="assemble",
-    )(odd, *rows)
+    )(field, side)
 
 
 def sweep_kernel(odd_ref, *refs):
-    prev_rows, wall_rows = refs[:4], refs[4:8]
-    coef_ref, step_ref, wall_ref, out_ref, motion_ref, edge_ref, near_ref = refs[8:]
+    rows_refs = refs[:4]
+    coef_a_ref, step_a_ref, coef_b_ref, step_b_ref, wall_ref, out_ref, motion_ref, edge_ref = refs[4:]
     odd = odd_ref[0] == 1
     planes = motion_ref.shape[1]
+    middle = planes // 2
     for c in range(3):
-        fill_rows(motion_ref, prev_rows, odd, c + 4, c, slice(128, 256))
-        fill_rows(edge_ref, wall_rows, odd, c, c, slice(None))
+        fill_rows(motion_ref, rows_refs, odd, c, c)
+    fill_rows(edge_ref, rows_refs, odd, 3, 0)
     lane = lax.broadcasted_iota(I32, (8, 128), 1)
     first, last = lane == 0, lane == 127
-
-    def neighbours(k, _):
+    lower = (coef_a_ref, step_a_ref, 0)
+    upper = (coef_b_ref, step_b_ref, middle - 1)
+
+    def from_plane(low, parts, k, sums):
+        side = edge_ref[0, k]
+        near = {}
         for c in range(3):
             here = motion_ref[c, k]
-            side = edge_ref[c, k]
+            before = pltpu.roll(side, 128 - c, 1) if c else side
+            beyond = pltpu.roll(side, 2 - c, 1) if c < 2 else side
             for x, value in (
-                (-1, jnp.where(first, pltpu.roll(side, 1, 1), pltpu.roll(here, 1, 1))),
+                (-1, jnp.where(first, before, pltpu.roll(here, 1, 1))),
                 (0, here),
-                (1, jnp.where(last, pltpu.roll(side, 127, 1), pltpu.roll(here, 127, 1))),
+                (1, jnp.where(last, beyond, pltpu.roll(here, 127, 1))),
             ):
-                near_ref[k, c, 1, x + 1] = value
-                near_ref[k, c, 0, x + 1] = pltpu.roll(value, 1, 0)
-                near_ref[k, c, 2, x + 1] = pltpu.roll(value, 7, 0)
+                near[c, 0, x] = value
+                near[c, -1, x] = pltpu.roll(value, 1, 0)
+                near[c, 1, x] = pltpu.roll(value, 7, 0)
+
+        def reach(part, plane, z):
+            coef_ref, _, base = part
+            force = [None] * 3
+            for y in (-1, 0, 1):
+                for x in (-1, 0, 1):
+                    at = SLOT_OF.get((x, y, z), SELF)
+                    block = [coef_ref[plane - base, at, e] for e in range(6)]
+                    for p in range(3):
+                        term = sum(block[ENTRY[p][q]] * near[q, y, x] for q in range(3))
+                        force[p] = term if force[p] is None else force[p] + term
+            return force
+
+        to = jnp.maximum(k - 1, 0)
+        below = plus(sums[:3], reach(parts[0], to, 1))
+        here = plus(sums[3:], reach(parts[1], k, 0))
+        above = reach(parts[2], jnp.minimum(k + 1, planes - 1), -1)
+        _, step_ref, base = parts[0]
+
+        @pl.when(k > low + 1)
+        def _():
+            for p in range(3):
+                motion_ref[p, to] = motion_ref[p, to] - step_ref[to - base, p] * below[p]
+
+        return tuple(here) + tuple(above)
+
+    def sweep(low, _):
+        sums = (jnp.zeros((8, 128), F32),) * 6
+        sums = lax.fori_loop(low, middle - 1, partial(from_plane, low, (lower, lower, lower)), sums)
+        sums = from_plane(low, (lower, lower, upper), middle - 1, sums)
+        sums = from_plane(low, (lower, upper, upper), middle, sums)
+        lax.fori_loop(middle + 1, planes - low, partial(from_plane, low, (upper, upper, upper)), sums)
         return 0
 
-    def relax(k, _):
-        force = [None] * 3
-        for m, (x, y, z) in enumerate(STEPS + ((0, 0, 0),)):
-            block = [coef_ref[k, m, e] for e in range(6)]
-            other = [near_ref[k + z, c, y + 1, x + 1] for c in range(3)]
-            for p in range(3):
-                term = sum(block[ENTRY[p][q]] * other[q] for q in range(3))
-                force[p] = term if force[p] is None else force[p] + term
-        for p in range(3):
-            motion_ref[p, k] = motion_ref[p, k] - step_ref[k, p] * force[p]
-        return 0
-
-    for sweep in range(SWEEPS):
-        lax.fori_loop(sweep, planes - sweep, neighbours, 0)
-        lax.fori_loop(sweep + 1, planes - sweep - 1, relax, 0)
+    lax.fori_loop(0, SWEEPS, sweep, 0)
     for c in range(3):
         for y in range(2):
             out_ref[c, y, :, :128] = wall_ref[c, y]
             out_ref[c, y, :, 128:] = motion_ref[c, DEPTH : planes - DEPTH, y, :]
 
 
-def sweeps(odd, rows, wall_rows, coef, step, wall):
+def sweeps(odd, rows, lower, upper, wall):
     planes = rows[0].shape[2]
     return pl.pallas_call(
         sweep_kernel,
         out_shape=jax.ShapeDtypeStruct((3, 2, planes - 2 * DEPTH, 256), F32),
-        in_specs=[pl.BlockSpec(memory_space=pltpu.SMEM)] + [VMEM] * 11,
+        in_specs=[SMEM] + [VMEM] * 9,
         out_specs=VMEM,
         scratch_shapes=[
             pltpu.VMEM((3, planes, 8, 128), F32),
-            pltpu.VMEM((3, planes, 8, 128), F32),
-            pltpu.VMEM((planes, 3, 3, 3, 8, 128), F32),
+            pltpu.VMEM((1, planes, 8, 128), F32),
         ],
-        compiler_params=params(30),
+        compiler_params=params(4),
         name="sweeps",
-    )(odd, *rows, *wall_rows, coef, step, wall)
+    )(odd, *rows, *lower, *upper, wall)
 
 
 def swap(block, partner):
@@ -405,14 +604,41 @@
     return lax.ppermute(block, BOTH, route)
 
 
-def widen(block, even):
-    count = block.shape[2]
-    first, last = block[:, :, :DEPTH], block[:, :, count - DEPTH :]
-    in_pair = swap(jnp.where(even, last, first), lambda s, f: (s, f ^ 1))
-    next_pair = swap(jnp.where(even, first, last), lambda s, f: (s, ((f - 1) ^ 1) + 1))
-    before = jnp.where(even, next_pair, in_pair)
-    after = jnp.where(even, in_pair, next_pair)
-    return jnp.concatenate([before, block, after], axis=2)
+def planes_apart(parts):
+    _, for_pair, for_next = parts
+    return (
+        swap(for_pair, lambda s, f: (s, f ^ 1)),
+        swap(for_next, lambda s, f: (s, ((f - 1) ^ 1) + 1)),
+    )
+
+
+def widen_kernel(even_ref, whole_ref, pair_ref, next_ref, *refs):
+    even = even_ref[0] == 1
+    channels, _, count, _ = whole_ref.shape
+    out_refs, head = refs, 0
+    if refs[0].shape[0] + channels == refs[-1].shape[0]:
+        head = refs[0].shape[0]
+        refs[1][:head] = refs[0][...]
+        out_refs = refs[1:]
+    for c in range(channels):
+        out_ref, to = (out_refs[0], c + head) if c + head < out_refs[0].shape[0] else (out_refs[1], c - out_refs[0].shape[0])
+        for y in range(2):
+            in_pair, next_pair = pair_ref[c, y], next_ref[c, y]
+            out_ref[to, y, :DEPTH] = jnp.where(even, next_pair, in_pair)
+            out_ref[to, y, DEPTH : DEPTH + count] = whole_ref[c, y]
+            out_ref[to, y, DEPTH + count :] = jnp.where(even, in_pair, next_pair)
+
+
+def widen(even, parts, channels, head=()):
+    _, rows, count, lanes = parts[0].shape
+    return pl.pallas_call(
+        widen_kernel,
+        out_shape=tuple(jax.ShapeDtypeStruct((n, rows, count + 2 * DEPTH, lanes), F32) for n in channels),
+        in_specs=[SMEM] + [VMEM] * (3 + len(head)),
+        out_specs=(VMEM,) * len(channels),
+        compiler_params=params(4),
+        name="widen",
+    )(even, *parts, *head)
 
 
 def all_rows(block):
@@ -420,16 +646,24 @@
 
 
 def shards(shell_motion, owner, stencil_slot, stencil_weight, prev_motion, node_offset, cell_split):
-    odd = (lax.axis_index("struct") % 2).astype(I32).reshape(1)
-    even = lax.axis_index("fluid") % 2 == 0
+    odd = (lax.axis_index("struct") & 1).astype(I32).reshape(1)
+    even = 1 - (lax.axis_index("fluid") & 1).astype(I32).reshape(1)
     packed = pack(owner, shell_motion)
-    fields = jnp.concatenate([node_offset, cell_split.astype(F32)[None], prev_motion])
-    rows = all_rows(widen(fields, even))
+    *sent, slot, weight = fields(even, node_offset, cell_split, prev_motion, stencil_slot, stencil_weight)
+    lattice, prev = widen(even, (sent[0], *planes_apart(sent)), (5, 3))
+    field, side = setup(odd, all_rows(lattice))
     received = lax.all_to_all(packed, BOTH, split_axis=0, concat_axis=0, tiled=True)
-    coef, step = assemble(odd, rows)
-    wall = gather(received, stencil_slot, stencil_weight)
-    wall_rows = all_rows(widen(wall, even))
-    return sweeps(odd, rows, wall_rows, coef, step, wall)
+    received, field, side = lax.optimization_barrier((received, field, side))
+    wall, *sent = gather(even, received, slot, weight)
+    field, side, *sent = lax.optimization_barrier((field, side, *sent))
+    apart = planes_apart(sent)
+    lower = assemble(field, side, 0, 8)
+    lower, apart = lax.optimization_barrier((lower, apart))
+    [joined] = widen(even, (sent[0], *apart), (4,), (prev,))
+    field, side, joined = lax.optimization_barrier((field, side, joined))
+    rows = all_rows(joined)
+    upper = assemble(field, side, 7, 15)
+    return sweeps(odd, rows, lower, upper, wall)
 
 
 def solution(mesh):

time: 71.5 us -> 63.6 us (0.89)
  waiting for transfers between devices: 19.1 us -> 7.18 us
  starting transfers between devices: 20.3 us -> 29.3 us
  other arithmetic: 2.48 us -> 0 us
  Pallas kernels: 25.8 us -> 24.2 us
  local copies, waits for them, and re-layouts: 3.18 us -> 2.35 us
    all_to_all x1, waiting for transfers between devices: 10.7 us -> 0.01 us  [shards(): lax.all_to_all(packed, BOTH, split_axis=0, concat_axis=0, tiled=True)]
    all_to_all x1, starting transfers between devices: 6.53 us -> 11.1 us  [shards(): lax.all_to_all(packed, BOTH, split_axis=0, concat_axis=0, tiled=True)]
    ppermute x10, starting transfers between devices: 13.7 us -> 18.1 us  [swap(): return lax.ppermute(block, BOTH, route)]
    pallas_call x1, Pallas kernels: 10.1 us -> 7.41 us  [sweeps(): pl.pallas_call(sweep_kernel, out_shape=jax.ShapeDtypeStruct((3, 2, planes...]
    concatenate x3 -> x0, other arithmetic: 1.71 us -> none  [the longest x2 0.88 us: widen(): return jnp.concatenate([before, block, after], axis=2)]
    ppermute x10, waiting for transfers between devices: 8.44 us -> 7.17 us  [swap(): return lax.ppermute(block, BOTH, route)]
    pallas_call x1, Pallas kernels: 4.07 us -> 5.03 us  [pack(): pl.pallas_call(pack_kernel, out_shape=jax.ShapeDtypeStruct((128, 3, 128),...]
    unnamed x8 -> x6, local copies, waits for them, and re-layouts: 3.18 us -> 2.35 us
  transfers between devices with their start and end apart: 11 -> 11, of which waited for: 4 -> 3; matrix products, arithmetic and copies ran while one was open for 1% -> 0% of each run, Pallas kernels for 19% -> 15%
where the time goes in v2:
time: 63.6 us; the launch traced here: 63.2 us
  starting transfers between devices  29.3 us (46%)
  Pallas kernels  24.2 us (38%)
  waiting for transfers between devices  7.18 us (11%)
  local copies, waits for them, and re-layouts  2.35 us (4%)
    ppermute x10, starting transfers between devices, swap(): return lax.ppermute(block, BOTH, route)  18.1 us
    all_to_all x1, starting transfers between devices, shards(): lax.all_to_all(packed, BOTH, split_axis=0, concat_axis=0, tiled=True)  11.1 us
    pallas_call x1, Pallas kernels, sweeps(): pl.pallas_call(sweep_kernel, out_shape=jax.ShapeDtypeStruct((3, 2, planes...  7.41 us
    pallas_call x2, Pallas kernels, assemble(): pl.pallas_call(partial(assemble_kernel, start, stop), out_shape=(jax.Shap...  7.4 us
    ppermute x10, waiting for transfers between devices, swap(): return lax.ppermute(block, BOTH, route)  7.17 us
    pallas_call x1, Pallas kernels, pack(): pl.pallas_call(pack_kernel, out_shape=jax.ShapeDtypeStruct((128, 3, 128),...  5.03 us
    unnamed x6, local copies, waits for them, and re-layouts  2.35 us
    pallas_call x1, Pallas kernels, gather(): pl.pallas_call(gather_kernel, out_shape=(jax.ShapeDtypeStruct((3, 2, 8, 1...  2.14 us
  transfers between devices with their start and end apart: 11, of which 3 were waited for; matrix products, arithmetic and copies ran while one was open for 0% of the time, Pallas kernels for 15%

profile of v2, /device:TPU:0, one launch (start us, length us, event | category | flops | bytes accessed | tf_op | source)
XLA Modules:
  0.0 63.2 jit_solution(17216498826775017700)
XLA Ops:
  0.0 5.0 %pack.1 = f32[128,3,128]{2,1,0:T(4,128)} custom-call(s32[1,8192]{1,0:T(1,128)} %bitcast.3, f32[3,8192]{1,0:T(4,128)} %value_hbm.1), custom_call_target="tpu_custom_call" | custom-call | tf_op jit(solution)/shard_map/pack/pallas_call | solution.py:86
  5.0 11.1 %all-to-all-start = ((f32[128,3,128]{2,1,0:T(4,128)}), f32[128,3,128]{2,1,0:T(4,128)S(1)}, u32[]{:S(2)}, u32[]{:S(2)}) async-start(f32[128,3,128]{2,1,0:T(4,128)} %pack.1), calls=%async_computation | async-start | bytes 524288 | tf_op jit(solution)/shard_map/all_to_all | solution.py:655
  16.2 1.6 %fields.1 = (f32[8,2,8,128]{3,2,1,0:T(8,128)}, f32[8,2,4,128]{3,2,1,0:T(4,128)}, f32[8,2,4,128]{3,2,1,0:T(4,128)}, s32[4,2,8,128]{3,2,1,0:T(8,128)}, f32[4,2,8,128]{3,2,1,0:T(8,128)}) custom-call(s32[1]{0:T(128)} %bitcast.2.even_ref, f32[3,2,8,256]{3,2,1,0:T(8,128)} %offset_hbm.1, s32[2,8,256]{2,1,0:T(8,128)} %split_hbm.1, f32[3,2,8,256]{3,2,1,0:T(8,128)} %prev_hbm.1, ...), custom_call_target="tpu_custom_call" | custom-call | tf_op jit(solution)/shard_map/fields/pallas_call | solution.py:143
  17.8 0.1 collective-permute-start
  17.9 5.2 %collective-permute-start.1 = (f32[8,2,4,128]{3,2,1,0:T(4,128)}, f32[8,2,4,128]{3,2,1,0:T(4,128)S(1)}, u32[]{:S(2)}, u32[]{:S(2)}) collective-permute-start(f32[8,2,4,128]{3,2,1,0:T(4,128)} %get-tuple-element.39), channel_id=1, source_target_pairs={{0,31},{1,2},{2,1},{3,4},{4,3},{5,6},{6,5},{7,8},{8,7},{9,10},{10,... | collective-permute-start | bytes 98312 | tf_op jit(solution)/shard_map/ppermute | solution.py:604
  23.2 2.7 %collective-permute-done.1.next_ref = f32[8,2,4,128]{3,2,1,0:T(4,128)S(1)} collective-permute-done((f32[8,2,4,128]{3,2,1,0:T(4,128)}, f32[8,2,4,128]{3,2,1,0:T(4,128)S(1)}, u32[]{:S(2)}, u32[]{:S(2)}) %collective-permute-start.1) | collective-permute-done | bytes 32800 | tf_op jit(solution)/shard_map/ppermute | solution.py:604
  25.8 0.8 %copy-done = f32[8,2,8,128]{3,2,1,0:T(8,128)S(1)} copy-done((f32[8,2,8,128]{3,2,1,0:T(8,128)S(1)}, f32[8,2,8,128]{3,2,1,0:T(8,128)}, u32[]{:S(2)}) %copy-start) | copy-done | bytes 65560
  26.7 1.0 %collective-permute-start.2 = (f32[5,2,16,128]{3,2,1,0:T(8,128)S(1)}, f32[5,2,16,128]{3,2,1,0:T(8,128)S(1)}, u32[]{:S(2)}, u32[]{:S(2)}) collective-permute-start(f32[5,2,16,128]{3,2,1,0:T(8,128)S(1)} %get-tuple-element.40.own_ref), channel_id=1, source_target_pairs={{0,32},{1,33},{2,34},{3,35},{4,36},{5,37},{6,38},{7,39},{8,40},{9,... | collective-permute-start | bytes 245768 | tf_op jit(solution)/shard_map/ppermute | solution.py:604
  27.7 2.7 %collective-permute-start.3 = (f32[5,2,16,128]{3,2,1,0:T(8,128)S(1)}, f32[5,2,16,128]{3,2,1,0:T(8,128)S(1)}, u32[]{:S(2)}, u32[]{:S(2)}) collective-permute-start(f32[5,2,16,128]{3,2,1,0:T(8,128)S(1)} %get-tuple-element.40.own_ref), channel_id=1, source_target_pairs={{0,64},{1,65},{2,66},{3,67},{4,68},{5,69},{6,70},{7,71},{8,72},{9,... | collective-permute-start | bytes 245768 | tf_op jit(solution)/shard_map/ppermute | solution.py:604
  30.3 1.2 %collective-permute-start.4 = (f32[5,2,16,128]{3,2,1,0:T(8,128)S(1)}, f32[5,2,16,128]{3,2,1,0:T(8,128)S(1)}, u32[]{:S(2)}, u32[]{:S(2)}) collective-permute-start(f32[5,2,16,128]{3,2,1,0:T(8,128)S(1)} %get-tuple-element.40.own_ref), channel_id=1, source_target_pairs={{0,96},{1,97},{2,98},{3,99},{4,100},{5,101},{6,102},{7,103},{8,104... | collective-permute-start | bytes 245768 | tf_op jit(solution)/shard_map/ppermute | solution.py:604
  31.5 2.1 %collective-permute-done.3.swap2_ref = f32[5,2,16,128]{3,2,1,0:T(8,128)S(1)} collective-permute-done((f32[5,2,16,128]{3,2,1,0:T(8,128)S(1)}, f32[5,2,16,128]{3,2,1,0:T(8,128)S(1)}, u32[]{:S(2)}, u32[]{:S(2)}) %collective-permute-start.3) | collective-permute-done | bytes 81952 | tf_op jit(solution)/shard_map/ppermute | solution.py:604
  33.6 2.4 %collective-permute-done.4.swap3_ref = f32[5,2,16,128]{3,2,1,0:T(8,128)S(1)} collective-permute-done((f32[5,2,16,128]{3,2,1,0:T(8,128)S(1)}, f32[5,2,16,128]{3,2,1,0:T(8,128)S(1)}, u32[]{:S(2)}, u32[]{:S(2)}) %collective-permute-start.4) | collective-permute-done | bytes 81952 | tf_op jit(solution)/shard_map/ppermute | solution.py:604
  36.0 0.6 setup.1
  36.6 0.7 %copy-done.1 = s32[4,2,8,128]{3,2,1,0:T(8,128)S(1)} copy-done((s32[4,2,8,128]{3,2,1,0:T(8,128)S(1)}, s32[4,2,8,128]{3,2,1,0:T(8,128)}, u32[]{:S(2)}) %copy-start.1) | copy-done | bytes 32792
  37.3 0.8 %copy-done.2 = f32[4,2,8,128]{3,2,1,0:T(8,128)S(1)} copy-done((f32[4,2,8,128]{3,2,1,0:T(8,128)S(1)}, f32[4,2,8,128]{3,2,1,0:T(8,128)}, u32[]{:S(2)}) %copy-start.2) | copy-done | bytes 32792
  38.1 2.1 %gather.1 = (f32[3,2,8,128]{3,2,1,0:T(8,128)S(1)}, f32[1,2,8,128]{3,2,1,0:T(8,128)S(1)}, f32[1,2,4,128]{3,2,1,0:T(4,128)S(1)}, f32[1,2,4,128]{3,2,1,0:T(4,128)S(1)}) custom-call(s32[1]{0:T(128)} %bitcast.2.even_ref, f32[128,3,128]{2,1,0:T(4,128)S(1)} %all-to-all-done.received_ref, s32[4,2,8,128]{3,2,1,0:T(8,128)S(1)} %copy-done.1, f32[4,2,8,128]{3,2,1,0:T(8,128)S(1)} %copy-done.2), custom_call_target="tpu_custom_call" | custom-call | tf_op jit(solution)/shard_map/gather/pallas_call | solution.py:204
  40.2 0.0 collective-permute-start.5
  40.3 3.2 %collective-permute-start.6 = (f32[1,2,4,128]{3,2,1,0:T(4,128)S(1)}, f32[1,2,4,128]{3,2,1,0:T(4,128)S(1)}, u32[]{:S(2)}, u32[]{:S(2)}) collective-permute-start(f32[1,2,4,128]{3,2,1,0:T(4,128)S(1)} %get-tuple-element.57), channel_id=1, source_target_pairs={{0,31},{1,2},{2,1},{3,4},{4,3},{5,6},{6,5},{7,8},{8,7},{9,10},{10,... | collective-permute-start | bytes 12296 | tf_op jit(solution)/shard_map/ppermute | solution.py:604
  43.5 3.7 %assemble.2 = (f32[9,27,6,8,128]{4,3,2,1,0:T(8,128)S(1)}, f32[9,3,8,128]{3,2,1,0:T(8,128)S(1)}) custom-call(f32[5,16,8,128]{3,2,1,0:T(8,128)S(1)} %get-tuple-element.64.field_ref, f32[17,6,8,128]{3,2,1,0:T(8,128)S(1)} %get-tuple-element.65.side_ref), custom_call_target="tpu_custom_call" | custom-call | flops 160000000 | bytes 1000000 | tf_op jit(solution)/shard_map/assemble/pallas_call | solution.py:495
  47.2 0.1 collective-permute-start.7
  47.3 2.3 %collective-permute-start.8 = (f32[4,2,16,128]{3,2,1,0:T(8,128)S(1)}, f32[4,2,16,128]{3,2,1,0:T(8,128)S(1)}, u32[]{:S(2)}, u32[]{:S(2)}) collective-permute-start(f32[4,2,16,128]{3,2,1,0:T(8,128)S(1)} %widen.3.refs_0_), channel_id=1, source_target_pairs={{0,64},{1,65},{2,66},{3,67},{4,68},{5,69},{6,70},{7,71},{8,72},{9,... | collective-permute-start | bytes 196616 | tf_op jit(solution)/shard_map/ppermute | solution.py:604
  49.6 2.4 %collective-permute-start.9 = (f32[4,2,16,128]{3,2,1,0:T(8,128)S(1)}, f32[4,2,16,128]{3,2,1,0:T(8,128)S(1)}, u32[]{:S(2)}, u32[]{:S(2)}) collective-permute-start(f32[4,2,16,128]{3,2,1,0:T(8,128)S(1)} %widen.3.refs_0_), channel_id=1, source_target_pairs={{0,96},{1,97},{2,98},{3,99},{4,100},{5,101},{6,102},{7,103},{8,104... | collective-permute-start | bytes 196616 | tf_op jit(solution)/shard_map/ppermute | solution.py:604
  52.0 3.7 %assemble.3 = (f32[9,27,6,8,128]{4,3,2,1,0:T(8,128)S(1)}, f32[9,3,8,128]{3,2,1,0:T(8,128)S(1)}) custom-call(f32[5,16,8,128]{3,2,1,0:T(8,128)S(1)} %get-tuple-element.64.field_ref, f32[17,6,8,128]{3,2,1,0:T(8,128)S(1)} %get-tuple-element.65.side_ref), custom_call_target="tpu_custom_call" | custom-call | flops 160000000 | bytes 1000000 | tf_op jit(solution)/shard_map/assemble/pallas_call | solution.py:495
  55.8 7.4 %sweeps.1 = f32[3,2,8,256]{3,2,1,0:T(8,128)} custom-call(s32[1]{0:T(128)} %bitcast.odd_ref, f32[4,2,16,128]{3,2,1,0:T(8,128)S(1)} %widen.3.refs_0_, f32[4,2,16,128]{3,2,1,0:T(8,128)S(1)} %collective-permute-done.7.refs_1_, f32[4,2,16,128]{3,2,1,0:T(8,128)S(1)} %collective-permute-done.8.refs_2_, f32[4,2,16,128]{3,2,1,0:T(8,128)S(1)} %collective-permute-done.9.refs_3_, ...), custom_call_target="tpu_custom_call" | custom-call | tf_op jit(solution)/shard_map/sweeps/pallas_call | solution.py:583
  (13 shorter events, 0.1 us)
Async XLA Ops:
  5.0 31.5 %all-to-all-start = ((f32[128,3,128]{2,1,0:T(4,128)}), f32[128,3,128]{2,1,0:T(4,128)S(1)}, u32[]{:S(2)}, u32[]{:S(2)}) async-start(f32[128,3,128]{2,1,0:T(4,128)} %pack.1), calls=%async_computation | async-start | bytes 524288 | tf_op jit(solution)/shard_map/all_to_all | solution.py:655
  17.8 5.3 %collective-permute-start = (f32[8,2,4,128]{3,2,1,0:T(4,128)}, f32[8,2,4,128]{3,2,1,0:T(4,128)S(1)}, u32[]{:S(2)}, u32[]{:S(2)}) collective-permute-start(f32[8,2,4,128]{3,2,1,0:T(4,128)} %get-tuple-element.38), channel_id=1, source_target_pairs={{0,1},{1,0},{2,3},{3,2},{4,5},{5,4},{6,7},{7,6},{8,9},{9,8},{10,11... | collective-permute-start | bytes 98312 | tf_op jit(solution)/shard_map/ppermute | solution.py:604
  17.9 7.9 %collective-permute-start.1 = (f32[8,2,4,128]{3,2,1,0:T(4,128)}, f32[8,2,4,128]{3,2,1,0:T(4,128)S(1)}, u32[]{:S(2)}, u32[]{:S(2)}) collective-permute-start(f32[8,2,4,128]{3,2,1,0:T(4,128)} %get-tuple-element.39), channel_id=1, source_target_pairs={{0,31},{1,2},{2,1},{3,4},{4,3},{5,6},{6,5},{7,8},{8,7},{9,10},{10,... | collective-permute-start | bytes 98312 | tf_op jit(solution)/shard_map/ppermute | solution.py:604
  25.8 0.8 %copy-start = (f32[8,2,8,128]{3,2,1,0:T(8,128)S(1)}, f32[8,2,8,128]{3,2,1,0:T(8,128)}, u32[]{:S(2)}) copy-start(f32[8,2,8,128]{3,2,1,0:T(8,128)} %get-tuple-element.37.whole_ref) | copy-start | bytes 196612
  26.7 4.8 %collective-permute-start.2 = (f32[5,2,16,128]{3,2,1,0:T(8,128)S(1)}, f32[5,2,16,128]{3,2,1,0:T(8,128)S(1)}, u32[]{:S(2)}, u32[]{:S(2)}) collective-permute-start(f32[5,2,16,128]{3,2,1,0:T(8,128)S(1)} %get-tuple-element.40.own_ref), channel_id=1, source_target_pairs={{0,32},{1,33},{2,34},{3,35},{4,36},{5,37},{6,38},{7,39},{8,40},{9,... | collective-permute-start | bytes 245768 | tf_op jit(solution)/shard_map/ppermute | solution.py:604
  27.7 5.9 %collective-permute-start.3 = (f32[5,2,16,128]{3,2,1,0:T(8,128)S(1)}, f32[5,2,16,128]{3,2,1,0:T(8,128)S(1)}, u32[]{:S(2)}, u32[]{:S(2)}) collective-permute-start(f32[5,2,16,128]{3,2,1,0:T(8,128)S(1)} %get-tuple-element.40.own_ref), channel_id=1, source_target_pairs={{0,64},{1,65},{2,66},{3,67},{4,68},{5,69},{6,70},{7,71},{8,72},{9,... | collective-permute-start | bytes 245768 | tf_op jit(solution)/shard_map/ppermute | solution.py:604
  30.3 5.7 %collective-permute-start.4 = (f32[5,2,16,128]{3,2,1,0:T(8,128)S(1)}, f32[5,2,16,128]{3,2,1,0:T(8,128)S(1)}, u32[]{:S(2)}, u32[]{:S(2)}) collective-permute-start(f32[5,2,16,128]{3,2,1,0:T(8,128)S(1)} %get-tuple-element.40.own_ref), channel_id=1, source_target_pairs={{0,96},{1,97},{2,98},{3,99},{4,100},{5,101},{6,102},{7,103},{8,104... | collective-permute-start | bytes 245768 | tf_op jit(solution)/shard_map/ppermute | solution.py:604
  36.6 0.8 %copy-start.1 = (s32[4,2,8,128]{3,2,1,0:T(8,128)S(1)}, s32[4,2,8,128]{3,2,1,0:T(8,128)}, u32[]{:S(2)}) copy-start(s32[4,2,8,128]{3,2,1,0:T(8,128)} %get-tuple-element.46.slot_ref) | copy-start | bytes 98308
  37.3 0.8 %copy-start.2 = (f32[4,2,8,128]{3,2,1,0:T(8,128)S(1)}, f32[4,2,8,128]{3,2,1,0:T(8,128)}, u32[]{:S(2)}) copy-start(f32[4,2,8,128]{3,2,1,0:T(8,128)} %get-tuple-element.47.weight_ref) | copy-start | bytes 98308
  40.2 7.0 %collective-permute-start.5 = (f32[1,2,4,128]{3,2,1,0:T(4,128)S(1)}, f32[1,2,4,128]{3,2,1,0:T(4,128)S(1)}, u32[]{:S(2)}, u32[]{:S(2)}) collective-permute-start(f32[1,2,4,128]{3,2,1,0:T(4,128)S(1)} %get-tuple-element.56), channel_id=1, source_target_pairs={{0,1},{1,0},{2,3},{3,2},{4,5},{5,4},{6,7},{7,6},{8,9},{9,8},{10,11... | collective-permute-start | bytes 12296 | tf_op jit(solution)/shard_map/ppermute | solution.py:604
  40.3 6.9 %collective-permute-start.6 = (f32[1,2,4,128]{3,2,1,0:T(4,128)S(1)}, f32[1,2,4,128]{3,2,1,0:T(4,128)S(1)}, u32[]{:S(2)}, u32[]{:S(2)}) collective-permute-start(f32[1,2,4,128]{3,2,1,0:T(4,128)S(1)} %get-tuple-element.57), channel_id=1, source_target_pairs={{0,31},{1,2},{2,1},{3,4},{4,3},{5,6},{6,5},{7,8},{8,7},{9,10},{10,... | collective-permute-start | bytes 12296 | tf_op jit(solution)/shard_map/ppermute | solution.py:604
  47.2 8.5 %collective-permute-start.7 = (f32[4,2,16,128]{3,2,1,0:T(8,128)S(1)}, f32[4,2,16,128]{3,2,1,0:T(8,128)S(1)}, u32[]{:S(2)}, u32[]{:S(2)}) collective-permute-start(f32[4,2,16,128]{3,2,1,0:T(8,128)S(1)} %widen.3.refs_0_), channel_id=1, source_target_pairs={{0,32},{1,33},{2,34},{3,35},{4,36},{5,37},{6,38},{7,39},{8,40},{9,... | collective-permute-start | bytes 196616 | tf_op jit(solution)/shard_map/ppermute | solution.py:604
  47.3 8.4 %collective-permute-start.8 = (f32[4,2,16,128]{3,2,1,0:T(8,128)S(1)}, f32[4,2,16,128]{3,2,1,0:T(8,128)S(1)}, u32[]{:S(2)}, u32[]{:S(2)}) collective-permute-start(f32[4,2,16,128]{3,2,1,0:T(8,128)S(1)} %widen.3.refs_0_), channel_id=1, source_target_pairs={{0,64},{1,65},{2,66},{3,67},{4,68},{5,69},{6,70},{7,71},{8,72},{9,... | collective-permute-start | bytes 196616 | tf_op jit(solution)/shard_map/ppermute | solution.py:604
  49.6 6.2 %collective-permute-start.9 = (f32[4,2,16,128]{3,2,1,0:T(8,128)S(1)}, f32[4,2,16,128]{3,2,1,0:T(8,128)S(1)}, u32[]{:S(2)}, u32[]{:S(2)}) collective-permute-start(f32[4,2,16,128]{3,2,1,0:T(8,128)S(1)} %widen.3.refs_0_), channel_id=1, source_target_pairs={{0,96},{1,97},{2,98},{3,99},{4,100},{5,101},{6,102},{7,103},{8,104... | collective-permute-start | bytes 196616 | tf_op jit(solution)/shard_map/ppermute | solution.py:604

commit v3 on v2

--- a/solution.py
+++ b/solution.py
@@ -100,11 +100,11 @@
     )(owner.reshape(1, count), shell_motion)
 
 
-def payload(channels):
+def payload(kept, sent):
     return (
-        jax.ShapeDtypeStruct((channels, 2, 8, 128), F32),
-        jax.ShapeDtypeStruct((channels, 2, DEPTH, 128), F32),
-        jax.ShapeDtypeStruct((channels, 2, DEPTH, 128), F32),
+        jax.ShapeDtypeStruct((kept, 2, 8, 128), F32),
+        jax.ShapeDtypeStruct((sent, 2, DEPTH, 128), F32),
+        jax.ShapeDtypeStruct((sent, 2, DEPTH, 128), F32),
     )
 
 
@@ -123,6 +123,8 @@
         (offset_ref, split_ref, prev_ref, slot_ref, weight_ref),
         semaphores,
     )
+    out_refs[0][8:12] = slot_ref[...].astype(F32)
+    out_refs[0][12:16] = weight_ref[...]
     even = even_ref[0] == 1
     lane = lax.broadcasted_iota(I32, (8, 128), 1)
     for y in range(2):
@@ -142,14 +144,12 @@
 def fields(even, node_offset, cell_split, prev_motion, stencil_slot, stencil_weight):
     return pl.pallas_call(
         fields_kernel,
-        out_shape=(
-            *payload(8),
-            jax.ShapeDtypeStruct(stencil_slot.shape, I32),
-            jax.ShapeDtypeStruct(stencil_weight.shape, F32),
-        ),
+        out_shape=payload(16, 8),
         in_specs=[SMEM] + [HBM] * 5,
-        out_specs=(VMEM,) * 5,
+        out_specs=(VMEM,) * 3,
         scratch_shapes=[
+            pltpu.VMEM(stencil_slot.shape, I32),
+            pltpu.VMEM(stencil_weight.shape, F32),
             pltpu.VMEM(node_offset.shape, F32),
             pltpu.VMEM(cell_split.shape, I32),
             pltpu.VMEM(prev_motion.shape, F32),
@@ -160,8 +160,58 @@
     )(even, node_offset, cell_split, prev_motion, stencil_slot, stencil_weight)
 
 
-def gather_kernel(even_ref, received_ref, slot_ref, weight_ref, out_ref, *more_refs):
-    column_refs, table_ref = more_refs[:3], more_refs[3]
+def columns_kernel(even_ref, received_ref, plan_ref, *refs):
+    column_refs, table_ref = refs[:3], refs[3]
+    for c in range(3):
+        flat = received_ref[:, c, :]
+        high = flat.astype(BF16).astype(F32)
+        low = flat - high
+        for part, base in ((high, 0), (low, 192)):
+            at = slice(base + c * 64, base + c * 64 + 64)
+            table_ref[:128, at] = part[:, :64].astype(BF16)
+            table_ref[128:, at] = part[:, 64:].astype(BF16)
+
+    def stacked(first):
+        return jnp.concatenate(
+            [
+                plan_ref[first + t, y, :, x : x + 1]
+                for t in range(4)
+                for y in range(2)
+                for x in (127, 0)
+            ]
+        )
+
+    slot = stacked(0).astype(I32)
+    weight = stacked(4)
+    pick = ((slot >> 6) & 1) * 128 + (slot >> 7)
+    hot = jnp.where(lax.broadcasted_iota(I32, (128, 256), 1) == pick, 1.0, 0.0).astype(BF16)
+    found = jnp.dot(hot, table_ref[...], preferred_element_type=F32)
+    found = found[:, :192] + found[:, 192:]
+    share = jnp.where(lax.broadcasted_iota(I32, (128, 192), 1) % 64 == (slot & 63), weight, 0.0) * found
+    share = share[:32] + share[32:64] + share[64:96] + share[96:]
+    values = [jnp.sum(share[:, c * 64 : c * 64 + 64], axis=1, keepdims=True) for c in range(3)]
+    lane = lax.broadcasted_iota(I32, (8, 128), 1)
+    for y in range(2):
+        columns = jnp.zeros((8, 128), F32)
+        for c in range(3):
+            columns = jnp.where(lane == c, values[c][y * 16 : y * 16 + 8], columns)
+            columns = jnp.where(lane == 125 + c, values[c][y * 16 + 8 : y * 16 + 16], columns)
+        emit(column_refs, even_ref[0] == 1, 0, y, columns)
+
+
+def wall_columns(even, received, plan):
+    return pl.pallas_call(
+        columns_kernel,
+        out_shape=payload(1, 1),
+        in_specs=[SMEM] + [VMEM] * 2,
+        out_specs=(VMEM,) * 3,
+        scratch_shapes=[pltpu.VMEM((256, 384), BF16)],
+        compiler_params=params(8),
+        name="columns",
+    )(even, received, plan)
+
+
+def gather_kernel(received_ref, plan_ref, out_ref, table_ref):
     for c in range(3):
         flat = received_ref[:, c, :].T
         high = flat.astype(BF16).astype(F32)
@@ -177,8 +227,11 @@
         for z in range(0, 8, 2):
             total = [jnp.zeros((64, 256), F32) for _ in range(3)]
             for t in range(4):
-                slot = jnp.concatenate([slot_ref[t, y, z + k : z + k + 1, :] for k in BITS], axis=1)
-                weight = jnp.concatenate([weight_ref[t, y, z + k : z + k + 1, :] for k in BITS], axis=1)
+                slot, weight = [
+                    jnp.concatenate([plan_ref[first + t, y, z + k : z + k + 1, :] for k in BITS], axis=1)
+                    for first in (0, 4)
+                ]
+                slot = slot.astype(I32)
                 pick = ((slot >> 6) & 1) * 128 + (slot >> 7)
                 hot = jnp.where(picks == pick, 1.0, 0.0).astype(BF16)
                 found = jnp.dot(table, hot, preferred_element_type=F32)
@@ -190,26 +243,19 @@
                 line = jnp.sum(total[c], axis=0, keepdims=True)
                 for k in BITS:
                     out_ref[c, y, z + k : z + k + 1, :] = line[:, k * 128 : k * 128 + 128]
-    lane = lax.broadcasted_iota(I32, (8, 128), 1)
-    for y in range(2):
-        columns = jnp.zeros((8, 128), F32)
-        for c in range(3):
-            wall = out_ref[c, y]
-            columns = jnp.where(lane == c, pltpu.roll(wall, c + 1, 1), columns)
-            columns = jnp.where(lane == 125 + c, pltpu.roll(wall, 125 + c, 1), columns)
-        emit(column_refs, even_ref[0] == 1, 0, y, columns)
-
-
-def gather(even, received, stencil_slot, stencil_weight):
+
+
+def gather(received, plan):
     return pl.pallas_call(
         gather_kernel,
-        out_shape=(jax.ShapeDtypeStruct((3, 2, 8, 128), F32), *payload(1)),
-        in_specs=[SMEM] + [VMEM] * 3,
-        out_specs=(VMEM,) * 4,
+        out_shape=jax.ShapeDtypeStruct((3, 2, 8, 128), F32),
+        in_specs=[VMEM] * 2,
+        out_specs=VMEM,
         scratch_shapes=[pltpu.VMEM((384, 256), BF16)],
-        compiler_params=params(16),
+        compiler_params=params(8),
+        cost_estimate=pl.CostEstimate(flops=60000000, bytes_accessed=1000000, transcendentals=0),
         name="gather",
-    )(even, received, stencil_slot, stencil_weight)
+    )(received, plan)
 
 
 def cross(u, v):
@@ -476,7 +522,7 @@
             store(plane, (-1, 1, 0), back_x(("down", c)))
         return 0
 
-    lax.fori_loop(start, stop, cells, 0)
+    lax.fori_loop(start, stop, cells, 0, unroll=2)
 
     def selves(k, _):
         for e in range(6):
@@ -488,7 +534,7 @@
                 step_ref[k, e] = -RELAX_FACTOR / total
         return 0
 
-    lax.fori_loop(1, stop - start, selves, 0)
+    lax.fori_loop(1, stop - start, selves, 0, unroll=7)
 
 
 def assemble(field, side, start, stop):
@@ -500,7 +546,7 @@
         ),
         in_specs=[VMEM] * 2,
         out_specs=(VMEM,) * 2,
-        compiler_params=params(4),
+        compiler_params=params(12),
         cost_estimate=pl.CostEstimate(
             flops=PLANE_FLOPS * (stop - start), bytes_accessed=1000000, transcendentals=0
         ),
@@ -519,10 +565,8 @@
     fill_rows(edge_ref, rows_refs, odd, 3, 0)
     lane = lax.broadcasted_iota(I32, (8, 128), 1)
     first, last = lane == 0, lane == 127
-    lower = (coef_a_ref, step_a_ref, 0)
-    upper = (coef_b_ref, step_b_ref, middle - 1)
-
-    def from_plane(low, parts, k, sums):
+
+    def neighbours(k):
         side = edge_ref[0, k]
         near = {}
         for c in range(3):
@@ -537,41 +581,31 @@
                 near[c, 0, x] = value
                 near[c, -1, x] = pltpu.roll(value, 1, 0)
                 near[c, 1, x] = pltpu.roll(value, 7, 0)
-
-        def reach(part, plane, z):
-            coef_ref, _, base = part
-            force = [None] * 3
-            for y in (-1, 0, 1):
-                for x in (-1, 0, 1):
-                    at = SLOT_OF.get((x, y, z), SELF)
-                    block = [coef_ref[plane - base, at, e] for e in range(6)]
-                    for p in range(3):
-                        term = sum(block[ENTRY[p][q]] * near[q, y, x] for q in range(3))
-                        force[p] = term if force[p] is None else force[p] + term
-            return force
-
-        to = jnp.maximum(k - 1, 0)
-        below = plus(sums[:3], reach(parts[0], to, 1))
-        here = plus(sums[3:], reach(parts[1], k, 0))
-        above = reach(parts[2], jnp.minimum(k + 1, planes - 1), -1)
-        _, step_ref, base = parts[0]
-
-        @pl.when(k > low + 1)
-        def _():
-            for p in range(3):
-                motion_ref[p, to] = motion_ref[p, to] - step_ref[to - base, p] * below[p]
-
-        return tuple(here) + tuple(above)
-
-    def sweep(low, _):
-        sums = (jnp.zeros((8, 128), F32),) * 6
-        sums = lax.fori_loop(low, middle - 1, partial(from_plane, low, (lower, lower, lower)), sums)
-        sums = from_plane(low, (lower, lower, upper), middle - 1, sums)
-        sums = from_plane(low, (lower, upper, upper), middle, sums)
-        lax.fori_loop(middle + 1, planes - low, partial(from_plane, low, (upper, upper, upper)), sums)
-        return 0
-
-    lax.fori_loop(0, SWEEPS, sweep, 0)
+        return near
+
+    def reach(force, near, plane, z):
+        coef_ref, at = (coef_a_ref, plane) if plane < middle else (coef_b_ref, plane - middle + 1)
+        for y in (-1, 0, 1):
+            for x in (-1, 0, 1):
+                m = SLOT_OF.get((x, y, z), SELF)
+                block = [coef_ref[at, m, e] for e in range(6)]
+                for p in range(3):
+                    term = sum(block[ENTRY[p][q]] * near[q, y, x] for q in range(3))
+                    force[p] = term if force[p] is None else force[p] + term
+
+    for sweep in range(SWEEPS):
+        low, high = sweep + 1, planes - 2 - sweep
+        force = {k: [None] * 3 for k in range(low, high + 1)}
+        for k in range(low - 1, high + 2):
+            near = neighbours(k)
+            for z in (1, 0, -1):
+                if low <= k - z <= high:
+                    reach(force[k - z], near, k - z, z)
+            done = k - 1
+            if done in force:
+                step_ref, at = (step_a_ref, done) if done < middle else (step_b_ref, done - middle + 1)
+                for p in range(3):
+                    motion_ref[p, done] = motion_ref[p, done] - step_ref[at, p] * force[done][p]
     for c in range(3):
         for y in range(2):
             out_ref[c, y, :, :128] = wall_ref[c, y]
@@ -589,7 +623,7 @@
             pltpu.VMEM((3, planes, 8, 128), F32),
             pltpu.VMEM((1, planes, 8, 128), F32),
         ],
-        compiler_params=params(4),
+        compiler_params=params(20),
         name="sweeps",
     )(odd, *rows, *lower, *upper, wall)
 
@@ -612,33 +646,51 @@
     )
 
 
-def widen_kernel(even_ref, whole_ref, pair_ref, next_ref, *refs):
+def widened(even, out_ref, to, whole, in_pair, next_pair):
+    count = whole.shape[1]
+    out_ref[to, :, :DEPTH] = jnp.where(even, next_pair, in_pair)
+    out_ref[to, :, DEPTH : DEPTH + count] = whole
+    out_ref[to, :, DEPTH + count :] = jnp.where(even, in_pair, next_pair)
+
+
+def widen_fields_kernel(even_ref, whole_ref, pair_ref, next_ref, lattice_ref, prev_ref, plan_ref):
     even = even_ref[0] == 1
-    channels, _, count, _ = whole_ref.shape
-    out_refs, head = refs, 0
-    if refs[0].shape[0] + channels == refs[-1].shape[0]:
-        head = refs[0].shape[0]
-        refs[1][:head] = refs[0][...]
-        out_refs = refs[1:]
-    for c in range(channels):
-        out_ref, to = (out_refs[0], c + head) if c + head < out_refs[0].shape[0] else (out_refs[1], c - out_refs[0].shape[0])
-        for y in range(2):
-            in_pair, next_pair = pair_ref[c, y], next_ref[c, y]
-            out_ref[to, y, :DEPTH] = jnp.where(even, next_pair, in_pair)
-            out_ref[to, y, DEPTH : DEPTH + count] = whole_ref[c, y]
-            out_ref[to, y, DEPTH + count :] = jnp.where(even, in_pair, next_pair)
-
-
-def widen(even, parts, channels, head=()):
-    _, rows, count, lanes = parts[0].shape
-    return pl.pallas_call(
-        widen_kernel,
-        out_shape=tuple(jax.ShapeDtypeStruct((n, rows, count + 2 * DEPTH, lanes), F32) for n in channels),
-        in_specs=[SMEM] + [VMEM] * (3 + len(head)),
-        out_specs=(VMEM,) * len(channels),
+    for c in range(8):
+        out_ref, to = (lattice_ref, c) if c < 5 else (prev_ref, c - 5)
+        widened(even, out_ref, to, whole_ref[c], pair_ref[c], next_ref[c])
+    plan_ref[...] = whole_ref[8:]
+
+
+def widen_fields(even, whole, in_pair, next_pair):
+    _, rows, count, lanes = whole.shape
+    return pl.pallas_call(
+        widen_fields_kernel,
+        out_shape=(
+            jax.ShapeDtypeStruct((5, rows, count + 2 * DEPTH, lanes), F32),
+            jax.ShapeDtypeStruct((3, rows, count + 2 * DEPTH, lanes), F32),
+            jax.ShapeDtypeStruct((8, rows, count, lanes), F32),
+        ),
+        in_specs=[SMEM] + [VMEM] * 3,
+        out_specs=(VMEM,) * 3,
         compiler_params=params(4),
-        name="widen",
-    )(even, *parts, *head)
+        name="widen_fields",
+    )(even, whole, in_pair, next_pair)
+
+
+def widen_wall_kernel(even_ref, prev_ref, columns_ref, pair_ref, next_ref, out_ref):
+    out_ref[:3] = prev_ref[...]
+    widened(even_ref[0] == 1, out_ref, 3, columns_ref[0], pair_ref[0], next_ref[0])
+
+
+def widen_wall(even, prev, columns, in_pair, next_pair):
+    return pl.pallas_call(
+        widen_wall_kernel,
+        out_shape=jax.ShapeDtypeStruct((4, *prev.shape[1:]), F32),
+        in_specs=[SMEM] + [VMEM] * 4,
+        out_specs=VMEM,
+        compiler_params=params(4),
+        name="widen_wall",
+    )(even, prev, columns, in_pair, next_pair)
 
 
 def all_rows(block):
@@ -649,20 +701,23 @@
     odd = (lax.axis_index("struct") & 1).astype(I32).reshape(1)
     even = 1 - (lax.axis_index("fluid") & 1).astype(I32).reshape(1)
     packed = pack(owner, shell_motion)
-    *sent, slot, weight = fields(even, node_offset, cell_split, prev_motion, stencil_slot, stencil_weight)
-    lattice, prev = widen(even, (sent[0], *planes_apart(sent)), (5, 3))
+    sent = fields(even, node_offset, cell_split, prev_motion, stencil_slot, stencil_weight)
+    apart = planes_apart(sent)
+    packed, apart = lax.optimization_barrier((packed, apart))
+    lattice, prev, plan = widen_fields(even, sent[0], *apart)
     field, side = setup(odd, all_rows(lattice))
     received = lax.all_to_all(packed, BOTH, split_axis=0, concat_axis=0, tiled=True)
     received, field, side = lax.optimization_barrier((received, field, side))
-    wall, *sent = gather(even, received, slot, weight)
+    sent = wall_columns(even, received, plan)
     field, side, *sent = lax.optimization_barrier((field, side, *sent))
     apart = planes_apart(sent)
     lower = assemble(field, side, 0, 8)
     lower, apart = lax.optimization_barrier((lower, apart))
-    [joined] = widen(even, (sent[0], *apart), (4,), (prev,))
-    field, side, joined = lax.optimization_barrier((field, side, joined))
+    joined = widen_wall(even, prev, sent[0], *apart)
+    field, side, received, joined = lax.optimization_barrier((field, side, received, joined))
     rows = all_rows(joined)
     upper = assemble(field, side, 7, 15)
+    wall = gather(received, plan)
     return sweeps(odd, rows, lower, upper, wall)
 
 

time: 63.6 us -> 54.3 us (0.85)
  Pallas kernels: 24.2 us -> 21.1 us
  starting transfers between devices: 29.3 us -> 26.8 us
  waiting for transfers between devices: 7.18 us -> 5.11 us
  local copies, waits for them, and re-layouts: 2.35 us -> 0.9 us
    all_to_all x1, starting transfers between devices: 11.1 us -> 6.2 us  [shards(): lax.all_to_all(packed, BOTH, split_axis=0, concat_axis=0, tiled=True)]
    pallas_call x1, Pallas kernels: 7.41 us -> 4.19 us  [sweeps(): pl.pallas_call(sweep_kernel, out_shape=jax.ShapeDtypeStruct((3, 2, planes...]
    ppermute x10, waiting for transfers between devices: 7.17 us -> 4.7 us  [swap(): return lax.ppermute(block, BOTH, route)]
    ppermute x10, starting transfers between devices: 18.1 us -> 20.6 us  [swap(): return lax.ppermute(block, BOTH, route)]
    unnamed x6 -> x2, local copies, waits for them, and re-layouts: 2.35 us -> 0.9 us
    pallas_call x4 -> x5, Pallas kernels: 3.79 us -> 4.72 us  [the longest x1 2.1 us: gather(): pl.pallas_call(gather_kernel, out_shape=jax.ShapeDtypeStruct((3, 2, 8, 12...]
    pallas_call x2, Pallas kernels: 7.4 us -> 6.61 us  [assemble(): pl.pallas_call(partial(assemble_kernel, start, stop), out_shape=(jax.Shap...]
  transfers between devices with their start and end apart: 11 -> 11, of which waited for: 3 -> 3; matrix products, arithmetic and copies ran while one was open for 0% -> 0% of each run, Pallas kernels for 15% -> 27%
where the time goes in v3:
time: 54.3 us; the launch traced here: 54.1 us
  starting transfers between devices  26.8 us (49%)
  Pallas kernels  21.1 us (39%)
  waiting for transfers between devices  5.11 us (9%)
  local copies, waits for them, and re-layouts  0.9 us (2%)
    ppermute x10, starting transfers between devices, swap(): return lax.ppermute(block, BOTH, route)  20.6 us
    pallas_call x2, Pallas kernels, assemble(): pl.pallas_call(partial(assemble_kernel, start, stop), out_shape=(jax.Shap...  6.61 us
    all_to_all x1, starting transfers between devices, shards(): lax.all_to_all(packed, BOTH, split_axis=0, concat_axis=0, tiled=True)  6.2 us
    pallas_call x1, Pallas kernels, pack(): pl.pallas_call(pack_kernel, out_shape=jax.ShapeDtypeStruct((128, 3, 128),...  5.03 us
    ppermute x10, waiting for transfers between devices, swap(): return lax.ppermute(block, BOTH, route)  4.7 us
    pallas_call x1, Pallas kernels, sweeps(): pl.pallas_call(sweep_kernel, out_shape=jax.ShapeDtypeStruct((3, 2, planes...  4.19 us
    pallas_call x1, Pallas kernels, gather(): pl.pallas_call(gather_kernel, out_shape=jax.ShapeDtypeStruct((3, 2, 8, 12...  2.1 us
    pallas_call x1, Pallas kernels, fields(): pl.pallas_call(fields_kernel, out_shape=payload(16, 8), in_specs=[SMEM] +...  1.63 us
  transfers between devices with their start and end apart: 11, of which 3 were waited for; matrix products, arithmetic and copies ran while one was open for 0% of the time, Pallas kernels for 27%

profile of v3, /device:TPU:0, one launch (start us, length us, event | category | flops | bytes accessed | tf_op | source)
XLA Modules:
  0.0 54.1 jit_solution(16608060080612152330)
XLA Ops:
  0.0 1.6 %fields.1 = (f32[16,2,8,128]{3,2,1,0:T(8,128)}, f32[8,2,4,128]{3,2,1,0:T(4,128)}, f32[8,2,4,128]{3,2,1,0:T(4,128)}) custom-call(s32[1]{0:T(128)} %bitcast.2.even_ref, f32[3,2,8,256]{3,2,1,0:T(8,128)} %offset_hbm.1, s32[2,8,256]{2,1,0:T(8,128)} %split_hbm.1, f32[3,2,8,256]{3,2,1,0:T(8,128)} %prev_hbm.1, s32[4,2,8,128]{3,2,1,0:T(8,128)} %slot_hbm.1, ...), custom_call_target="tpu_custom_call" | custom-call | tf_op jit(solution)/shard_map/fields/pallas_call | solution.py:145
  1.6 0.1 collective-permute-start
  1.7 6.7 %collective-permute-start.1 = (f32[8,2,4,128]{3,2,1,0:T(4,128)}, f32[8,2,4,128]{3,2,1,0:T(4,128)S(1)}, u32[]{:S(2)}, u32[]{:S(2)}) collective-permute-start(f32[8,2,4,128]{3,2,1,0:T(4,128)} %get-tuple-element.40), channel_id=1, source_target_pairs={{0,31},{1,2},{2,1},{3,4},{4,3},{5,6},{6,5},{7,8},{8,7},{9,10},{10,... | collective-permute-start | bytes 98312 | tf_op jit(solution)/shard_map/ppermute | solution.py:638
  8.4 5.0 %pack.1 = f32[128,3,128]{2,1,0:T(4,128)} custom-call(s32[1,8192]{1,0:T(1,128)} %bitcast.3, f32[3,8192]{1,0:T(4,128)} %value_hbm.1), custom_call_target="tpu_custom_call" | custom-call | tf_op jit(solution)/shard_map/pack/pallas_call | solution.py:86
  13.5 0.0 collective-permute-done.1.next_ref
  13.5 6.2 %all-to-all-start = ((f32[128,3,128]{2,1,0:T(4,128)}), f32[128,3,128]{2,1,0:T(4,128)S(1)}, u32[]{:S(2)}, u32[]{:S(2)}) async-start(f32[128,3,128]{2,1,0:T(4,128)} %pack.1), calls=%async_computation | async-start | bytes 524288 | tf_op jit(solution)/shard_map/all_to_all | solution.py:709
  19.7 0.9 %copy-done = f32[16,2,8,128]{3,2,1,0:T(8,128)S(1)} copy-done((f32[16,2,8,128]{3,2,1,0:T(8,128)S(1)}, f32[16,2,8,128]{3,2,1,0:T(8,128)}, u32[]{:S(2)}) %copy-start) | copy-done | bytes 131096
  20.6 2.3 %collective-permute-start.4 = (f32[5,2,16,128]{3,2,1,0:T(8,128)S(1)}, f32[5,2,16,128]{3,2,1,0:T(8,128)S(1)}, u32[]{:S(2)}, u32[]{:S(2)}) collective-permute-start(f32[5,2,16,128]{3,2,1,0:T(8,128)S(1)} %get-tuple-element.45.own_ref), channel_id=1, source_target_pairs={{0,96},{1,97},{2,98},{3,99},{4,100},{5,101},{6,102},{7,103},{8,104... | collective-permute-start | bytes 245768 | tf_op jit(solution)/shard_map/ppermute | solution.py:638
  22.9 0.9 %collective-permute-start.3 = (f32[5,2,16,128]{3,2,1,0:T(8,128)S(1)}, f32[5,2,16,128]{3,2,1,0:T(8,128)S(1)}, u32[]{:S(2)}, u32[]{:S(2)}) collective-permute-start(f32[5,2,16,128]{3,2,1,0:T(8,128)S(1)} %get-tuple-element.45.own_ref), channel_id=1, source_target_pairs={{0,64},{1,65},{2,66},{3,67},{4,68},{5,69},{6,70},{7,71},{8,72},{9,... | collective-permute-start | bytes 245768 | tf_op jit(solution)/shard_map/ppermute | solution.py:638
  23.7 1.1 %collective-permute-start.2 = (f32[5,2,16,128]{3,2,1,0:T(8,128)S(1)}, f32[5,2,16,128]{3,2,1,0:T(8,128)S(1)}, u32[]{:S(2)}, u32[]{:S(2)}) collective-permute-start(f32[5,2,16,128]{3,2,1,0:T(8,128)S(1)} %get-tuple-element.45.own_ref), channel_id=1, source_target_pairs={{0,32},{1,33},{2,34},{3,35},{4,36},{5,37},{6,38},{7,39},{8,40},{9,... | collective-permute-start | bytes 245768 | tf_op jit(solution)/shard_map/ppermute | solution.py:638
  24.8 2.0 %collective-permute-done.4.swap3_ref = f32[5,2,16,128]{3,2,1,0:T(8,128)S(1)} collective-permute-done((f32[5,2,16,128]{3,2,1,0:T(8,128)S(1)}, f32[5,2,16,128]{3,2,1,0:T(8,128)S(1)}, u32[]{:S(2)}, u32[]{:S(2)}) %collective-permute-start.4) | collective-permute-done | bytes 81952 | tf_op jit(solution)/shard_map/ppermute | solution.py:638
  26.7 2.7 %collective-permute-done.3.swap2_ref = f32[5,2,16,128]{3,2,1,0:T(8,128)S(1)} collective-permute-done((f32[5,2,16,128]{3,2,1,0:T(8,128)S(1)}, f32[5,2,16,128]{3,2,1,0:T(8,128)S(1)}, u32[]{:S(2)}, u32[]{:S(2)}) %collective-permute-start.3) | collective-permute-done | bytes 81952 | tf_op jit(solution)/shard_map/ppermute | solution.py:638
  29.5 0.6 %setup.1 = (f32[5,16,8,128]{3,2,1,0:T(8,128)S(1)}, f32[17,6,8,128]{3,2,1,0:T(8,128)S(1)}) custom-call(s32[1]{0:T(128)} %bitcast.odd_ref, f32[5,2,16,128]{3,2,1,0:T(8,128)S(1)} %get-tuple-element.45.own_ref, f32[5,2,16,128]{3,2,1,0:T(8,128)S(1)} %collective-permute-done.2.swap1_ref, f32[5,2,16,128]{3,2,1,0:T(8,128)S(1)} %collective-permute-done.3.swap2_ref, ...), custom_call_target="tpu_custom_call" | custom-call | flops 20000000 | bytes 1000000 | tf_op jit(solution)/shard_map/setup/pallas_call | solution.py:441
  30.1 0.4 all-to-all-done.received_ref
  30.5 1.0 %columns.1 = (f32[1,2,8,128]{3,2,1,0:T(8,128)S(1)}, f32[1,2,4,128]{3,2,1,0:T(4,128)S(1)}, f32[1,2,4,128]{3,2,1,0:T(4,128)S(1)}) custom-call(s32[1]{0:T(128)} %bitcast.2.even_ref, f32[128,3,128]{2,1,0:T(4,128)S(1)} %all-to-all-done.received_ref, f32[8,2,8,128]{3,2,1,0:T(8,128)S(1)} %get-tuple-element.51.plan_ref), custom_call_target="tpu_custom_call" | custom-call | tf_op jit(solution)/shard_map/columns/pallas_call | solution.py:203
  31.4 0.1 collective-permute-start.5
  31.5 5.4 %collective-permute-start.6 = (f32[1,2,4,128]{3,2,1,0:T(4,128)S(1)}, f32[1,2,4,128]{3,2,1,0:T(4,128)S(1)}, u32[]{:S(2)}, u32[]{:S(2)}) collective-permute-start(f32[1,2,4,128]{3,2,1,0:T(4,128)S(1)} %get-tuple-element.62), channel_id=1, source_target_pairs={{0,31},{1,2},{2,1},{3,4},{4,3},{5,6},{6,5},{7,8},{8,7},{9,10},{10,... | collective-permute-start | bytes 12296 | tf_op jit(solution)/shard_map/ppermute | solution.py:638
  36.9 3.3 %assemble.2 = (f32[9,27,6,8,128]{4,3,2,1,0:T(8,128)S(1)}, f32[9,3,8,128]{3,2,1,0:T(8,128)S(1)}) custom-call(f32[5,16,8,128]{3,2,1,0:T(8,128)S(1)} %get-tuple-element.68.field_ref, f32[17,6,8,128]{3,2,1,0:T(8,128)S(1)} %get-tuple-element.69.side_ref), custom_call_target="tpu_custom_call" | custom-call | flops 160000000 | bytes 1000000 | tf_op jit(solution)/shard_map/assemble/pallas_call | solution.py:541
  40.2 1.5 %collective-permute-start.9 = (f32[4,2,16,128]{3,2,1,0:T(8,128)S(1)}, f32[4,2,16,128]{3,2,1,0:T(8,128)S(1)}, u32[]{:S(2)}, u32[]{:S(2)}) collective-permute-start(f32[4,2,16,128]{3,2,1,0:T(8,128)S(1)} %widen_wall.1.refs_0_), channel_id=1, source_target_pairs={{0,96},{1,97},{2,98},{3,99},{4,100},{5,101},{6,102},{7,103},{8,104... | collective-permute-start | bytes 196616 | tf_op jit(solution)/shard_map/ppermute | solution.py:638
  41.8 0.9 %collective-permute-start.8 = (f32[4,2,16,128]{3,2,1,0:T(8,128)S(1)}, f32[4,2,16,128]{3,2,1,0:T(8,128)S(1)}, u32[]{:S(2)}, u32[]{:S(2)}) collective-permute-start(f32[4,2,16,128]{3,2,1,0:T(8,128)S(1)} %widen_wall.1.refs_0_), channel_id=1, source_target_pairs={{0,64},{1,65},{2,66},{3,67},{4,68},{5,69},{6,70},{7,71},{8,72},{9,... | collective-permute-start | bytes 196616 | tf_op jit(solution)/shard_map/ppermute | solution.py:638
  42.7 1.8 %collective-permute-start.7 = (f32[4,2,16,128]{3,2,1,0:T(8,128)S(1)}, f32[4,2,16,128]{3,2,1,0:T(8,128)S(1)}, u32[]{:S(2)}, u32[]{:S(2)}) collective-permute-start(f32[4,2,16,128]{3,2,1,0:T(8,128)S(1)} %widen_wall.1.refs_0_), channel_id=1, source_target_pairs={{0,32},{1,33},{2,34},{3,35},{4,36},{5,37},{6,38},{7,39},{8,40},{9,... | collective-permute-start | bytes 196616 | tf_op jit(solution)/shard_map/ppermute | solution.py:638
  44.4 2.1 %gather.1.refs_8_ = f32[3,2,8,128]{3,2,1,0:T(8,128)S(1)} custom-call(f32[128,3,128]{2,1,0:T(4,128)S(1)} %all-to-all-done.received_ref, f32[8,2,8,128]{3,2,1,0:T(8,128)S(1)} %get-tuple-element.51.plan_ref), custom_call_target="tpu_custom_call" | custom-call | flops 60000000 | bytes 1000000 | tf_op jit(solution)/shard_map/gather/pallas_call | solution.py:249
  46.5 3.3 %assemble.3 = (f32[9,27,6,8,128]{4,3,2,1,0:T(8,128)S(1)}, f32[9,3,8,128]{3,2,1,0:T(8,128)S(1)}) custom-call(f32[5,16,8,128]{3,2,1,0:T(8,128)S(1)} %get-tuple-element.68.field_ref, f32[17,6,8,128]{3,2,1,0:T(8,128)S(1)} %get-tuple-element.69.side_ref), custom_call_target="tpu_custom_call" | custom-call | flops 160000000 | bytes 1000000 | tf_op jit(solution)/shard_map/assemble/pallas_call | solution.py:541
  49.9 4.2 %sweeps.1 = f32[3,2,8,256]{3,2,1,0:T(8,128)} custom-call(s32[1]{0:T(128)} %bitcast.odd_ref, f32[4,2,16,128]{3,2,1,0:T(8,128)S(1)} %widen_wall.1.refs_0_, f32[4,2,16,128]{3,2,1,0:T(8,128)S(1)} %collective-permute-done.7.refs_1_, f32[4,2,16,128]{3,2,1,0:T(8,128)S(1)} %collective-permute-done.8.refs_2_, f32[4,2,16,128]{3,2,1,0:T(8,128)S(1)} %collective-permute-done.9.refs_3_, ...), custom_call_target="tpu_custom_call" | custom-call | tf_op jit(solution)/shard_map/sweeps/pallas_call | solution.py:617
  (10 shorter events, 0.1 us)
Async XLA Ops:
  1.6 11.8 %collective-permute-start = (f32[8,2,4,128]{3,2,1,0:T(4,128)}, f32[8,2,4,128]{3,2,1,0:T(4,128)S(1)}, u32[]{:S(2)}, u32[]{:S(2)}) collective-permute-start(f32[8,2,4,128]{3,2,1,0:T(4,128)} %get-tuple-element.39), channel_id=1, source_target_pairs={{0,1},{1,0},{2,3},{3,2},{4,5},{5,4},{6,7},{7,6},{8,9},{9,8},{10,11... | collective-permute-start | bytes 98312 | tf_op jit(solution)/shard_map/ppermute | solution.py:638
  1.7 11.7 %collective-permute-start.1 = (f32[8,2,4,128]{3,2,1,0:T(4,128)}, f32[8,2,4,128]{3,2,1,0:T(4,128)S(1)}, u32[]{:S(2)}, u32[]{:S(2)}) collective-permute-start(f32[8,2,4,128]{3,2,1,0:T(4,128)} %get-tuple-element.40), channel_id=1, source_target_pairs={{0,31},{1,2},{2,1},{3,4},{4,3},{5,6},{6,5},{7,8},{8,7},{9,10},{10,... | collective-permute-start | bytes 98312 | tf_op jit(solution)/shard_map/ppermute | solution.py:638
  13.5 17.0 %all-to-all-start = ((f32[128,3,128]{2,1,0:T(4,128)}), f32[128,3,128]{2,1,0:T(4,128)S(1)}, u32[]{:S(2)}, u32[]{:S(2)}) async-start(f32[128,3,128]{2,1,0:T(4,128)} %pack.1), calls=%async_computation | async-start | bytes 524288 | tf_op jit(solution)/shard_map/all_to_all | solution.py:709
  19.7 0.9 %copy-start = (f32[16,2,8,128]{3,2,1,0:T(8,128)S(1)}, f32[16,2,8,128]{3,2,1,0:T(8,128)}, u32[]{:S(2)}) copy-start(f32[16,2,8,128]{3,2,1,0:T(8,128)} %get-tuple-element.42.whole_ref) | copy-start | bytes 393220
  20.6 6.1 %collective-permute-start.4 = (f32[5,2,16,128]{3,2,1,0:T(8,128)S(1)}, f32[5,2,16,128]{3,2,1,0:T(8,128)S(1)}, u32[]{:S(2)}, u32[]{:S(2)}) collective-permute-start(f32[5,2,16,128]{3,2,1,0:T(8,128)S(1)} %get-tuple-element.45.own_ref), channel_id=1, source_target_pairs={{0,96},{1,97},{2,98},{3,99},{4,100},{5,101},{6,102},{7,103},{8,104... | collective-permute-start | bytes 245768 | tf_op jit(solution)/shard_map/ppermute | solution.py:638
  22.9 6.6 %collective-permute-start.3 = (f32[5,2,16,128]{3,2,1,0:T(8,128)S(1)}, f32[5,2,16,128]{3,2,1,0:T(8,128)S(1)}, u32[]{:S(2)}, u32[]{:S(2)}) collective-permute-start(f32[5,2,16,128]{3,2,1,0:T(8,128)S(1)} %get-tuple-element.45.own_ref), channel_id=1, source_target_pairs={{0,64},{1,65},{2,66},{3,67},{4,68},{5,69},{6,70},{7,71},{8,72},{9,... | collective-permute-start | bytes 245768 | tf_op jit(solution)/shard_map/ppermute | solution.py:638
  23.7 5.7 %collective-permute-start.2 = (f32[5,2,16,128]{3,2,1,0:T(8,128)S(1)}, f32[5,2,16,128]{3,2,1,0:T(8,128)S(1)}, u32[]{:S(2)}, u32[]{:S(2)}) collective-permute-start(f32[5,2,16,128]{3,2,1,0:T(8,128)S(1)} %get-tuple-element.45.own_ref), channel_id=1, source_target_pairs={{0,32},{1,33},{2,34},{3,35},{4,36},{5,37},{6,38},{7,39},{8,40},{9,... | collective-permute-start | bytes 245768 | tf_op jit(solution)/shard_map/ppermute | solution.py:638
  31.4 8.8 %collective-permute-start.5 = (f32[1,2,4,128]{3,2,1,0:T(4,128)S(1)}, f32[1,2,4,128]{3,2,1,0:T(4,128)S(1)}, u32[]{:S(2)}, u32[]{:S(2)}) collective-permute-start(f32[1,2,4,128]{3,2,1,0:T(4,128)S(1)} %get-tuple-element.61), channel_id=1, source_target_pairs={{0,1},{1,0},{2,3},{3,2},{4,5},{5,4},{6,7},{7,6},{8,9},{9,8},{10,11... | collective-permute-start | bytes 12296 | tf_op jit(solution)/shard_map/ppermute | solution.py:638
  31.5 8.7 %collective-permute-start.6 = (f32[1,2,4,128]{3,2,1,0:T(4,128)S(1)}, f32[1,2,4,128]{3,2,1,0:T(4,128)S(1)}, u32[]{:S(2)}, u32[]{:S(2)}) collective-permute-start(f32[1,2,4,128]{3,2,1,0:T(4,128)S(1)} %get-tuple-element.62), channel_id=1, source_target_pairs={{0,31},{1,2},{2,1},{3,4},{4,3},{5,6},{6,5},{7,8},{8,7},{9,10},{10,... | collective-permute-start | bytes 12296 | tf_op jit(solution)/shard_map/ppermute | solution.py:638
  40.2 9.6 %collective-permute-start.9 = (f32[4,2,16,128]{3,2,1,0:T(8,128)S(1)}, f32[4,2,16,128]{3,2,1,0:T(8,128)S(1)}, u32[]{:S(2)}, u32[]{:S(2)}) collective-permute-start(f32[4,2,16,128]{3,2,1,0:T(8,128)S(1)} %widen_wall.1.refs_0_), channel_id=1, source_target_pairs={{0,96},{1,97},{2,98},{3,99},{4,100},{5,101},{6,102},{7,103},{8,104... | collective-permute-start | bytes 196616 | tf_op jit(solution)/shard_map/ppermute | solution.py:638
  41.8 8.1 %collective-permute-start.8 = (f32[4,2,16,128]{3,2,1,0:T(8,128)S(1)}, f32[4,2,16,128]{3,2,1,0:T(8,128)S(1)}, u32[]{:S(2)}, u32[]{:S(2)}) collective-permute-start(f32[4,2,16,128]{3,2,1,0:T(8,128)S(1)} %widen_wall.1.refs_0_), channel_id=1, source_target_pairs={{0,64},{1,65},{2,66},{3,67},{4,68},{5,69},{6,70},{7,71},{8,72},{9,... | collective-permute-start | bytes 196616 | tf_op jit(solution)/shard_map/ppermute | solution.py:638
  42.7 7.2 %collective-permute-start.7 = (f32[4,2,16,128]{3,2,1,0:T(8,128)S(1)}, f32[4,2,16,128]{3,2,1,0:T(8,128)S(1)}, u32[]{:S(2)}, u32[]{:S(2)}) collective-permute-start(f32[4,2,16,128]{3,2,1,0:T(8,128)S(1)} %widen_wall.1.refs_0_), channel_id=1, source_target_pairs={{0,32},{1,33},{2,34},{3,35},{4,36},{5,37},{6,38},{7,39},{8,40},{9,... | collective-permute-start | bytes 196616 | tf_op jit(solution)/shard_map/ppermute | solution.py:638

commit v4 on v3

--- a/solution.py
+++ b/solution.py
@@ -258,6 +258,14 @@
     )(received, plan)
 
 
+def back_y(values):
+    return [pltpu.roll(v, 1, 0) for v in values]
+
+
+def plus(u, v):
+    return [p + q for p, q in zip(u, v)]
+
+
 def cross(u, v):
     return [
         u[1] * v[2] - u[2] * v[1],
@@ -298,20 +306,24 @@
             at[axis] = 1
             path.append(tuple(at))
         one, two = path[1], path[2]
-        across = [over[two], [-w for w in over[one]], cross(edge[one], edge[two])]
+        third = cross(edge[one], edge[two])
         volume = sum(edge[one][p] * over[two][p] for p in range(3))
         inverse = 1.0 / volume
-        grad = [None] + [[w * inverse for w in across[m]] for m in range(3)]
-        grad[0] = [-(grad[1][p] + grad[2][p] + grad[3][p]) for p in range(3)]
+        minus = -inverse
+        grad = [None, [w * inverse for w in over[two]], [w * minus for w in over[one]], [w * inverse for w in third]]
+        grad[0] = [grad[1][p] + grad[2][p] + grad[3][p] for p in range(3)]
         for i in range(4):
             for j in range(i + 1, 4):
                 g, h = grad[i], grad[j]
-                same = [g[p] * h[p] for p in range(3)]
-                trace = same[0] + same[1] + same[2]
-                block = [same[p] + same[p] + trace for p in range(3)]
+                block = [g[p] * h[p] for p in range(3)]
                 block += [g[p] * h[q] + g[q] * h[p] for p, q in ((0, 1), (0, 2), (1, 2))]
                 key = (path[i], path[j])
-                blocks[key] = [o + n for o, n in zip(blocks[key], block)] if key in blocks else block
+                blocks[key] = plus(blocks[key], block) if key in blocks else block
+    for (v, _), block in blocks.items():
+        trace = block[0] + block[1] + block[2]
+        block[:3] = [same + same + trace for same in block[:3]]
+        if v == (0, 0, 0):
+            block[:] = [-w for w in block]
 
     def pick(mask, yes, no):
         return [jnp.where(mask, y, n) for y, n in zip(yes, no)]
@@ -360,14 +372,6 @@
             (6, jnp.where(odd, one, three)),
         ):
             target_ref[to, :, place + r, :] = value
-
-
-def back_y(values):
-    return [pltpu.roll(v, 1, 0) for v in values]
-
-
-def plus(u, v):
-    return [p + q for p, q in zip(u, v)]
 
 
 MOVING = ("z", "xz_up", "xz_down", "yz_up", "yz_down", "b00", "b01", "b10", "b11") + tuple(
@@ -412,7 +416,7 @@
     return moving, still
 
 
-def setup_kernel(odd_ref, own_ref, swap1_ref, swap2_ref, swap3_ref, field_ref, side_ref):
+def setup_kernel(odd_ref, own_ref, swap1_ref, swap2_ref, swap3_ref, _, field_ref, side_ref):
     odd = odd_ref[0] == 1
     for c in range(5):
         fill_rows(field_ref, (own_ref, swap1_ref, swap2_ref, swap3_ref), odd, c, c)
@@ -436,7 +440,7 @@
             side_ref[m, e] = moving[name][e]
 
 
-def setup(odd, rows):
+def setup(odd, rows, after):
     planes = rows[0].shape[2]
     return pl.pallas_call(
         setup_kernel,
@@ -444,12 +448,12 @@
             jax.ShapeDtypeStruct((5, planes, 8, 128), F32),
             jax.ShapeDtypeStruct((len(MOVING), 6, 8, 128), F32),
         ),
-        in_specs=[SMEM] + [VMEM] * 4,
+        in_specs=[SMEM] + [VMEM] * 5,
         out_specs=(VMEM,) * 2,
         compiler_params=params(4),
         cost_estimate=pl.CostEstimate(flops=SETUP_FLOPS, bytes_accessed=1000000, transcendentals=0),
         name="setup",
-    )(odd, *rows)
+    )(odd, *rows, after)
 
 
 def assemble_kernel(start, stop, field_ref, side_ref, coef_ref, step_ref):
@@ -522,7 +526,7 @@
             store(plane, (-1, 1, 0), back_x(("down", c)))
         return 0
 
-    lax.fori_loop(start, stop, cells, 0, unroll=2)
+    lax.fori_loop(start, stop, cells, 0, unroll=8)
 
     def selves(k, _):
         for e in range(6):
@@ -705,11 +709,10 @@
     apart = planes_apart(sent)
     packed, apart = lax.optimization_barrier((packed, apart))
     lattice, prev, plan = widen_fields(even, sent[0], *apart)
-    field, side = setup(odd, all_rows(lattice))
+    rows = all_rows(lattice)
     received = lax.all_to_all(packed, BOTH, split_axis=0, concat_axis=0, tiled=True)
-    received, field, side = lax.optimization_barrier((received, field, side))
     sent = wall_columns(even, received, plan)
-    field, side, *sent = lax.optimization_barrier((field, side, *sent))
+    field, side = setup(odd, rows, sent[0])
     apart = planes_apart(sent)
     lower = assemble(field, side, 0, 8)
     lower, apart = lax.optimization_barrier((lower, apart))

time: 54.3 us -> 51.7 us (0.952)
  starting transfers between devices: 26.8 us -> 22.7 us
  waiting for transfers between devices: 5.11 us -> 7.32 us
  Pallas kernels: 21.1 us -> 20.4 us
    all_to_all x1, waiting for transfers between devices: 0.42 us -> 5.69 us  [shards(): lax.all_to_all(packed, BOTH, split_axis=0, concat_axis=0, tiled=True)]
    ppermute x10, starting transfers between devices: 20.6 us -> 16.5 us  [swap(): return lax.ppermute(block, BOTH, route)]
    ppermute x10, waiting for transfers between devices: 4.7 us -> 1.63 us  [swap(): return lax.ppermute(block, BOTH, route)]
    pallas_call x2, Pallas kernels: 6.61 us -> 5.92 us  [assemble(): pl.pallas_call(partial(assemble_kernel, start, stop), out_shape=(jax.Shap...]
  transfers between devices with their start and end apart: 11 -> 11, of which waited for: 3 -> 2; matrix products, arithmetic and copies ran while one was open for 0% -> 0% of each run, Pallas kernels for 27% -> 28%
where the time goes in v4:
time: 51.7 us; the launch traced here: 51.5 us
  starting transfers between devices  22.7 us (44%)
  Pallas kernels  20.4 us (39%)
  waiting for transfers between devices  7.32 us (14%)
  local copies, waits for them, and re-layouts  0.9 us (2%)
    ppermute x10, starting transfers between devices, swap(): return lax.ppermute(block, BOTH, route)  16.5 us
    all_to_all x1, starting transfers between devices, shards(): lax.all_to_all(packed, BOTH, split_axis=0, concat_axis=0, tiled=True)  6.2 us
    pallas_call x2, Pallas kernels, assemble(): pl.pallas_call(partial(assemble_kernel, start, stop), out_shape=(jax.Shap...  5.92 us
    all_to_all x1, waiting for transfers between devices, shards(): lax.all_to_all(packed, BOTH, split_axis=0, concat_axis=0, tiled=True)  5.69 us
    pallas_call x1, Pallas kernels, pack(): pl.pallas_call(pack_kernel, out_shape=jax.ShapeDtypeStruct((128, 3, 128),...  5.03 us
    pallas_call x1, Pallas kernels, sweeps(): pl.pallas_call(sweep_kernel, out_shape=jax.ShapeDtypeStruct((3, 2, planes...  4.19 us
    pallas_call x1, Pallas kernels, gather(): pl.pallas_call(gather_kernel, out_shape=jax.ShapeDtypeStruct((3, 2, 8, 12...  2.1 us
    pallas_call x1, Pallas kernels, fields(): pl.pallas_call(fields_kernel, out_shape=payload(16, 8), in_specs=[SMEM] +...  1.63 us
  transfers between devices with their start and end apart: 11, of which 2 were waited for; matrix products, arithmetic and copies ran while one was open for 0% of the time, Pallas kernels for 28%

profile of v4, /device:TPU:0, one launch (start us, length us, event | category | flops | bytes accessed | tf_op | source)
XLA Modules:
  0.0 51.5 jit_solution(12446488480990643977)
XLA Ops:
  0.0 1.6 %fields.1 = (f32[16,2,8,128]{3,2,1,0:T(8,128)}, f32[8,2,4,128]{3,2,1,0:T(4,128)}, f32[8,2,4,128]{3,2,1,0:T(4,128)}) custom-call(s32[1]{0:T(128)} %bitcast.1.even_ref, f32[3,2,8,256]{3,2,1,0:T(8,128)} %offset_hbm.1, s32[2,8,256]{2,1,0:T(8,128)} %split_hbm.1, f32[3,2,8,256]{3,2,1,0:T(8,128)} %prev_hbm.1, s32[4,2,8,128]{3,2,1,0:T(8,128)} %slot_hbm.1, ...), custom_call_target="tpu_custom_call" | custom-call | tf_op jit(solution)/shard_map/fields/pallas_call | solution.py:145
  1.6 0.1 collective-permute-start
  1.7 6.7 %collective-permute-start.1 = (f32[8,2,4,128]{3,2,1,0:T(4,128)}, f32[8,2,4,128]{3,2,1,0:T(4,128)S(1)}, u32[]{:S(2)}, u32[]{:S(2)}) collective-permute-start(f32[8,2,4,128]{3,2,1,0:T(4,128)} %get-tuple-element.33), channel_id=1, source_target_pairs={{0,31},{1,2},{2,1},{3,4},{4,3},{5,6},{6,5},{7,8},{8,7},{9,10},{10,... | collective-permute-start | bytes 98312 | tf_op jit(solution)/shard_map/ppermute | solution.py:642
  8.4 5.0 %pack.1 = f32[128,3,128]{2,1,0:T(4,128)} custom-call(s32[1,8192]{1,0:T(1,128)} %bitcast.3, f32[3,8192]{1,0:T(4,128)} %value_hbm.1), custom_call_target="tpu_custom_call" | custom-call | tf_op jit(solution)/shard_map/pack/pallas_call | solution.py:86
  13.5 0.0 collective-permute-done.1.next_ref
  13.5 6.2 %all-to-all-start = ((f32[128,3,128]{2,1,0:T(4,128)}), f32[128,3,128]{2,1,0:T(4,128)S(1)}, u32[]{:S(2)}, u32[]{:S(2)}) async-start(f32[128,3,128]{2,1,0:T(4,128)} %pack.1), calls=%async_computation | async-start | bytes 524288 | tf_op jit(solution)/shard_map/all_to_all | solution.py:713
  19.7 0.9 %copy-done = f32[16,2,8,128]{3,2,1,0:T(8,128)S(1)} copy-done((f32[16,2,8,128]{3,2,1,0:T(8,128)S(1)}, f32[16,2,8,128]{3,2,1,0:T(8,128)}, u32[]{:S(2)}) %copy-start) | copy-done | bytes 131096
  20.6 2.3 %collective-permute-start.4 = (f32[5,2,16,128]{3,2,1,0:T(8,128)S(1)}, f32[5,2,16,128]{3,2,1,0:T(8,128)S(1)}, u32[]{:S(2)}, u32[]{:S(2)}) collective-permute-start(f32[5,2,16,128]{3,2,1,0:T(8,128)S(1)} %get-tuple-element.36.own_ref), channel_id=1, source_target_pairs={{0,96},{1,97},{2,98},{3,99},{4,100},{5,101},{6,102},{7,103},{8,104... | collective-permute-start | bytes 245768 | tf_op jit(solution)/shard_map/ppermute | solution.py:642
  22.9 0.9 %collective-permute-start.3 = (f32[5,2,16,128]{3,2,1,0:T(8,128)S(1)}, f32[5,2,16,128]{3,2,1,0:T(8,128)S(1)}, u32[]{:S(2)}, u32[]{:S(2)}) collective-permute-start(f32[5,2,16,128]{3,2,1,0:T(8,128)S(1)} %get-tuple-element.36.own_ref), channel_id=1, source_target_pairs={{0,64},{1,65},{2,66},{3,67},{4,68},{5,69},{6,70},{7,71},{8,72},{9,... | collective-permute-start | bytes 245768 | tf_op jit(solution)/shard_map/ppermute | solution.py:642
  23.7 1.1 %collective-permute-start.2 = (f32[5,2,16,128]{3,2,1,0:T(8,128)S(1)}, f32[5,2,16,128]{3,2,1,0:T(8,128)S(1)}, u32[]{:S(2)}, u32[]{:S(2)}) collective-permute-start(f32[5,2,16,128]{3,2,1,0:T(8,128)S(1)} %get-tuple-element.36.own_ref), channel_id=1, source_target_pairs={{0,32},{1,33},{2,34},{3,35},{4,36},{5,37},{6,38},{7,39},{8,40},{9,... | collective-permute-start | bytes 245768 | tf_op jit(solution)/shard_map/ppermute | solution.py:642
  24.8 5.7 %all-to-all-done.received_ref = f32[128,3,128]{2,1,0:T(4,128)S(1)} async-done(((f32[128,3,128]{2,1,0:T(4,128)}), f32[128,3,128]{2,1,0:T(4,128)S(1)}, u32[]{:S(2)}, u32[]{:S(2)}) %all-to-all-start) | async-done | bytes 196640 | tf_op jit(solution)/shard_map/all_to_all | solution.py:713
  30.5 1.0 %columns.1 = (f32[1,2,8,128]{3,2,1,0:T(8,128)S(1)}, f32[1,2,4,128]{3,2,1,0:T(4,128)S(1)}, f32[1,2,4,128]{3,2,1,0:T(4,128)S(1)}) custom-call(s32[1]{0:T(128)} %bitcast.1.even_ref, f32[128,3,128]{2,1,0:T(4,128)S(1)} %all-to-all-done.received_ref, f32[8,2,8,128]{3,2,1,0:T(8,128)S(1)} %get-tuple-element.38.plan_ref), custom_call_target="tpu_custom_call" | custom-call | tf_op jit(solution)/shard_map/columns/pallas_call | solution.py:203
  31.4 0.1 collective-permute-start.5
  31.5 1.3 %collective-permute-start.6 = (f32[1,2,4,128]{3,2,1,0:T(4,128)S(1)}, f32[1,2,4,128]{3,2,1,0:T(4,128)S(1)}, u32[]{:S(2)}, u32[]{:S(2)}) collective-permute-start(f32[1,2,4,128]{3,2,1,0:T(4,128)S(1)} %get-tuple-element.46), channel_id=1, source_target_pairs={{0,31},{1,2},{2,1},{3,4},{4,3},{5,6},{6,5},{7,8},{8,7},{9,10},{10,... | collective-permute-start | bytes 12296 | tf_op jit(solution)/shard_map/ppermute | solution.py:642
  32.8 0.0 collective-permute-done.4.swap3_ref
  32.8 0.6 %setup.1 = (f32[5,16,8,128]{3,2,1,0:T(8,128)S(1)}, f32[17,6,8,128]{3,2,1,0:T(8,128)S(1)}) custom-call(s32[1]{0:T(128)} %bitcast.odd_ref, f32[5,2,16,128]{3,2,1,0:T(8,128)S(1)} %get-tuple-element.36.own_ref, f32[5,2,16,128]{3,2,1,0:T(8,128)S(1)} %collective-permute-done.2.swap1_ref, f32[5,2,16,128]{3,2,1,0:T(8,128)S(1)} %collective-permute-done.3.swap2_ref, ...), custom_call_target="tpu_custom_call" | custom-call | flops 20000000 | bytes 1000000 | tf_op jit(solution)/shard_map/setup/pallas_call | solution.py:445
  33.4 2.9 %assemble.2 = (f32[9,27,6,8,128]{4,3,2,1,0:T(8,128)S(1)}, f32[9,3,8,128]{3,2,1,0:T(8,128)S(1)}) custom-call(f32[5,16,8,128]{3,2,1,0:T(8,128)S(1)} %get-tuple-element.52.field_ref, f32[17,6,8,128]{3,2,1,0:T(8,128)S(1)} %get-tuple-element.53.side_ref), custom_call_target="tpu_custom_call" | custom-call | flops 160000000 | bytes 1000000 | tf_op jit(solution)/shard_map/assemble/pallas_call | solution.py:545
  36.3 1.6 %collective-permute-done.6.next_ref = f32[1,2,4,128]{3,2,1,0:T(4,128)S(1)} collective-permute-done((f32[1,2,4,128]{3,2,1,0:T(4,128)S(1)}, f32[1,2,4,128]{3,2,1,0:T(4,128)S(1)}, u32[]{:S(2)}, u32[]{:S(2)}) %collective-permute-start.6) | collective-permute-done | bytes 4128 | tf_op jit(solution)/shard_map/ppermute | solution.py:642
  38.0 1.2 %collective-permute-start.9 = (f32[4,2,16,128]{3,2,1,0:T(8,128)S(1)}, f32[4,2,16,128]{3,2,1,0:T(8,128)S(1)}, u32[]{:S(2)}, u32[]{:S(2)}) collective-permute-start(f32[4,2,16,128]{3,2,1,0:T(8,128)S(1)} %widen_wall.1.refs_0_), channel_id=1, source_target_pairs={{0,96},{1,97},{2,98},{3,99},{4,100},{5,101},{6,102},{7,103},{8,104... | collective-permute-start | bytes 196616 | tf_op jit(solution)/shard_map/ppermute | solution.py:642
  39.1 1.5 %collective-permute-start.8 = (f32[4,2,16,128]{3,2,1,0:T(8,128)S(1)}, f32[4,2,16,128]{3,2,1,0:T(8,128)S(1)}, u32[]{:S(2)}, u32[]{:S(2)}) collective-permute-start(f32[4,2,16,128]{3,2,1,0:T(8,128)S(1)} %widen_wall.1.refs_0_), channel_id=1, source_target_pairs={{0,64},{1,65},{2,66},{3,67},{4,68},{5,69},{6,70},{7,71},{8,72},{9,... | collective-permute-start | bytes 196616 | tf_op jit(solution)/shard_map/ppermute | solution.py:642
  40.6 1.5 %collective-permute-start.7 = (f32[4,2,16,128]{3,2,1,0:T(8,128)S(1)}, f32[4,2,16,128]{3,2,1,0:T(8,128)S(1)}, u32[]{:S(2)}, u32[]{:S(2)}) collective-permute-start(f32[4,2,16,128]{3,2,1,0:T(8,128)S(1)} %widen_wall.1.refs_0_), channel_id=1, source_target_pairs={{0,32},{1,33},{2,34},{3,35},{4,36},{5,37},{6,38},{7,39},{8,40},{9,... | collective-permute-start | bytes 196616 | tf_op jit(solution)/shard_map/ppermute | solution.py:642
  42.1 2.1 %gather.1.refs_8_ = f32[3,2,8,128]{3,2,1,0:T(8,128)S(1)} custom-call(f32[128,3,128]{2,1,0:T(4,128)S(1)} %all-to-all-done.received_ref, f32[8,2,8,128]{3,2,1,0:T(8,128)S(1)} %get-tuple-element.38.plan_ref), custom_call_target="tpu_custom_call" | custom-call | flops 60000000 | bytes 1000000 | tf_op jit(solution)/shard_map/gather/pallas_call | solution.py:249
  44.2 3.0 %assemble.3 = (f32[9,27,6,8,128]{4,3,2,1,0:T(8,128)S(1)}, f32[9,3,8,128]{3,2,1,0:T(8,128)S(1)}) custom-call(f32[5,16,8,128]{3,2,1,0:T(8,128)S(1)} %get-tuple-element.52.field_ref, f32[17,6,8,128]{3,2,1,0:T(8,128)S(1)} %get-tuple-element.53.side_ref), custom_call_target="tpu_custom_call" | custom-call | flops 160000000 | bytes 1000000 | tf_op jit(solution)/shard_map/assemble/pallas_call | solution.py:545
  47.3 4.2 %sweeps.1 = f32[3,2,8,256]{3,2,1,0:T(8,128)} custom-call(s32[1]{0:T(128)} %bitcast.odd_ref, f32[4,2,16,128]{3,2,1,0:T(8,128)S(1)} %widen_wall.1.refs_0_, f32[4,2,16,128]{3,2,1,0:T(8,128)S(1)} %collective-permute-done.7.refs_1_, f32[4,2,16,128]{3,2,1,0:T(8,128)S(1)} %collective-permute-done.8.refs_2_, f32[4,2,16,128]{3,2,1,0:T(8,128)S(1)} %collective-permute-done.9.refs_3_, ...), custom_call_target="tpu_custom_call" | custom-call | tf_op jit(solution)/shard_map/sweeps/pallas_call | solution.py:621
  (10 shorter events, 0.0 us)
Async XLA Ops:
  1.6 11.8 %collective-permute-start = (f32[8,2,4,128]{3,2,1,0:T(4,128)}, f32[8,2,4,128]{3,2,1,0:T(4,128)S(1)}, u32[]{:S(2)}, u32[]{:S(2)}) collective-permute-start(f32[8,2,4,128]{3,2,1,0:T(4,128)} %get-tuple-element.32), channel_id=1, source_target_pairs={{0,1},{1,0},{2,3},{3,2},{4,5},{5,4},{6,7},{7,6},{8,9},{9,8},{10,11... | collective-permute-start | bytes 98312 | tf_op jit(solution)/shard_map/ppermute | solution.py:642
  1.7 11.7 %collective-permute-start.1 = (f32[8,2,4,128]{3,2,1,0:T(4,128)}, f32[8,2,4,128]{3,2,1,0:T(4,128)S(1)}, u32[]{:S(2)}, u32[]{:S(2)}) collective-permute-start(f32[8,2,4,128]{3,2,1,0:T(4,128)} %get-tuple-element.33), channel_id=1, source_target_pairs={{0,31},{1,2},{2,1},{3,4},{4,3},{5,6},{6,5},{7,8},{8,7},{9,10},{10,... | collective-permute-start | bytes 98312 | tf_op jit(solution)/shard_map/ppermute | solution.py:642
  13.5 17.0 %all-to-all-start = ((f32[128,3,128]{2,1,0:T(4,128)}), f32[128,3,128]{2,1,0:T(4,128)S(1)}, u32[]{:S(2)}, u32[]{:S(2)}) async-start(f32[128,3,128]{2,1,0:T(4,128)} %pack.1), calls=%async_computation | async-start | bytes 524288 | tf_op jit(solution)/shard_map/all_to_all | solution.py:713
  19.7 0.9 %copy-start = (f32[16,2,8,128]{3,2,1,0:T(8,128)S(1)}, f32[16,2,8,128]{3,2,1,0:T(8,128)}, u32[]{:S(2)}) copy-start(f32[16,2,8,128]{3,2,1,0:T(8,128)} %get-tuple-element.31.whole_ref) | copy-start | bytes 393220
  20.6 12.2 %collective-permute-start.4 = (f32[5,2,16,128]{3,2,1,0:T(8,128)S(1)}, f32[5,2,16,128]{3,2,1,0:T(8,128)S(1)}, u32[]{:S(2)}, u32[]{:S(2)}) collective-permute-start(f32[5,2,16,128]{3,2,1,0:T(8,128)S(1)} %get-tuple-element.36.own_ref), channel_id=1, source_target_pairs={{0,96},{1,97},{2,98},{3,99},{4,100},{5,101},{6,102},{7,103},{8,104... | collective-permute-start | bytes 245768 | tf_op jit(solution)/shard_map/ppermute | solution.py:642
  22.9 10.0 %collective-permute-start.3 = (f32[5,2,16,128]{3,2,1,0:T(8,128)S(1)}, f32[5,2,16,128]{3,2,1,0:T(8,128)S(1)}, u32[]{:S(2)}, u32[]{:S(2)}) collective-permute-start(f32[5,2,16,128]{3,2,1,0:T(8,128)S(1)} %get-tuple-element.36.own_ref), channel_id=1, source_target_pairs={{0,64},{1,65},{2,66},{3,67},{4,68},{5,69},{6,70},{7,71},{8,72},{9,... | collective-permute-start | bytes 245768 | tf_op jit(solution)/shard_map/ppermute | solution.py:642
  23.7 9.1 %collective-permute-start.2 = (f32[5,2,16,128]{3,2,1,0:T(8,128)S(1)}, f32[5,2,16,128]{3,2,1,0:T(8,128)S(1)}, u32[]{:S(2)}, u32[]{:S(2)}) collective-permute-start(f32[5,2,16,128]{3,2,1,0:T(8,128)S(1)} %get-tuple-element.36.own_ref), channel_id=1, source_target_pairs={{0,32},{1,33},{2,34},{3,35},{4,36},{5,37},{6,38},{7,39},{8,40},{9,... | collective-permute-start | bytes 245768 | tf_op jit(solution)/shard_map/ppermute | solution.py:642
  31.4 4.9 %collective-permute-start.5 = (f32[1,2,4,128]{3,2,1,0:T(4,128)S(1)}, f32[1,2,4,128]{3,2,1,0:T(4,128)S(1)}, u32[]{:S(2)}, u32[]{:S(2)}) collective-permute-start(f32[1,2,4,128]{3,2,1,0:T(4,128)S(1)} %get-tuple-element.45), channel_id=1, source_target_pairs={{0,1},{1,0},{2,3},{3,2},{4,5},{5,4},{6,7},{7,6},{8,9},{9,8},{10,11... | collective-permute-start | bytes 12296 | tf_op jit(solution)/shard_map/ppermute | solution.py:642
  31.5 6.4 %collective-permute-start.6 = (f32[1,2,4,128]{3,2,1,0:T(4,128)S(1)}, f32[1,2,4,128]{3,2,1,0:T(4,128)S(1)}, u32[]{:S(2)}, u32[]{:S(2)}) collective-permute-start(f32[1,2,4,128]{3,2,1,0:T(4,128)S(1)} %get-tuple-element.46), channel_id=1, source_target_pairs={{0,31},{1,2},{2,1},{3,4},{4,3},{5,6},{6,5},{7,8},{8,7},{9,10},{10,... | collective-permute-start | bytes 12296 | tf_op jit(solution)/shard_map/ppermute | solution.py:642
  38.0 9.3 %collective-permute-start.9 = (f32[4,2,16,128]{3,2,1,0:T(8,128)S(1)}, f32[4,2,16,128]{3,2,1,0:T(8,128)S(1)}, u32[]{:S(2)}, u32[]{:S(2)}) collective-permute-start(f32[4,2,16,128]{3,2,1,0:T(8,128)S(1)} %widen_wall.1.refs_0_), channel_id=1, source_target_pairs={{0,96},{1,97},{2,98},{3,99},{4,100},{5,101},{6,102},{7,103},{8,104... | collective-permute-start | bytes 196616 | tf_op jit(solution)/shard_map/ppermute | solution.py:642
  39.1 8.1 %collective-permute-start.8 = (f32[4,2,16,128]{3,2,1,0:T(8,128)S(1)}, f32[4,2,16,128]{3,2,1,0:T(8,128)S(1)}, u32[]{:S(2)}, u32[]{:S(2)}) collective-permute-start(f32[4,2,16,128]{3,2,1,0:T(8,128)S(1)} %widen_wall.1.refs_0_), channel_id=1, source_target_pairs={{0,64},{1,65},{2,66},{3,67},{4,68},{5,69},{6,70},{7,71},{8,72},{9,... | collective-permute-start | bytes 196616 | tf_op jit(solution)/shard_map/ppermute | solution.py:642
  40.6 6.6 %collective-permute-start.7 = (f32[4,2,16,128]{3,2,1,0:T(8,128)S(1)}, f32[4,2,16,128]{3,2,1,0:T(8,128)S(1)}, u32[]{:S(2)}, u32[]{:S(2)}) collective-permute-start(f32[4,2,16,128]{3,2,1,0:T(8,128)S(1)} %widen_wall.1.refs_0_), channel_id=1, source_target_pairs={{0,32},{1,33},{2,34},{3,35},{4,36},{5,37},{6,38},{7,39},{8,40},{9,... | collective-permute-start | bytes 196616 | tf_op jit(solution)/shard_map/ppermute | solution.py:642

commit v5 on v4

--- a/solution.py
+++ b/solution.py
@@ -43,8 +43,7 @@
     return pltpu.CompilerParams(vmem_limit_bytes=int(mebibytes * 2**20))
 
 
-def pack_kernel(owner_hbm, value_hbm, out_ref, left_ref, right_ref, owner_ref, value_ref, semaphores):
-    fetch((owner_hbm, value_hbm), (owner_ref, value_ref), semaphores)
+def pack(owner_ref, value_ref, out_ref, left_ref, right_ref):
     count = owner_ref.shape[1]
     width = 256
     rows = lax.broadcasted_iota(I32, (width, width + 128), 0)
@@ -81,25 +80,6 @@
             out_ref[pl.ds(h, 64, stride=2), c, :] = both[c * 64 : c * 64 + 64, h * 128 : h * 128 + 128]
 
 
-def pack(owner, shell_motion):
-    count = shell_motion.shape[1]
-    return pl.pallas_call(
-        pack_kernel,
-        out_shape=jax.ShapeDtypeStruct((128, 3, 128), F32),
-        in_specs=[HBM] * 2,
-        out_specs=VMEM,
-        scratch_shapes=[
-            pltpu.VMEM((384, count), BF16),
-            pltpu.VMEM((256, count), BF16),
-            pltpu.VMEM((1, count), I32),
-            pltpu.VMEM((3, count), F32),
-            pltpu.SemaphoreType.DMA((2,)),
-        ],
-        compiler_params=params(FULL),
-        name="pack",
-    )(owner.reshape(1, count), shell_motion)
-
-
 def payload(kept, sent):
     return (
         jax.ShapeDtypeStruct((kept, 2, 8, 128), F32),
@@ -116,16 +96,9 @@
     next_ref[channel, y] = jnp.where(even, first, last)
 
 
-def fields_kernel(even_ref, offset_hbm, split_hbm, prev_hbm, slot_hbm, weight_hbm, *refs):
-    out_refs, (slot_ref, weight_ref, offset_ref, split_ref, prev_ref, semaphores) = refs[:3], refs[3:]
-    fetch(
-        (offset_hbm, split_hbm, prev_hbm, slot_hbm, weight_hbm),
-        (offset_ref, split_ref, prev_ref, slot_ref, weight_ref),
-        semaphores,
-    )
+def fields(even, offset_ref, split_ref, prev_ref, slot_ref, weight_ref, out_refs):
     out_refs[0][8:12] = slot_ref[...].astype(F32)
     out_refs[0][12:16] = weight_ref[...]
-    even = even_ref[0] == 1
     lane = lax.broadcasted_iota(I32, (8, 128), 1)
     for y in range(2):
         code = split_ref[y].astype(F32)
@@ -141,23 +114,31 @@
         emit(out_refs, even, 4, y, columns)
 
 
-def fields(even, node_offset, cell_split, prev_motion, stencil_slot, stencil_weight):
-    return pl.pallas_call(
-        fields_kernel,
-        out_shape=payload(16, 8),
-        in_specs=[SMEM] + [HBM] * 5,
-        out_specs=(VMEM,) * 3,
+def first_kernel(even_ref, *refs):
+    sources, outs, inputs = refs[:7], refs[7:11], refs[11:18]
+    left_ref, right_ref, semaphores = refs[18:]
+    fetch(sources, inputs, semaphores)
+    fields(even_ref[0] == 1, *inputs[2:], outs[1:])
+    pack(*inputs[:2], outs[0], left_ref, right_ref)
+
+
+def pack_and_fields(even, owner, *others):
+    count = owner.shape[0]
+    inputs = (owner.reshape(1, count), *others)
+    return pl.pallas_call(
+        first_kernel,
+        out_shape=(jax.ShapeDtypeStruct((128, 3, 128), F32), *payload(16, 8)),
+        in_specs=[SMEM] + [HBM] * 7,
+        out_specs=(VMEM,) * 4,
         scratch_shapes=[
-            pltpu.VMEM(stencil_slot.shape, I32),
-            pltpu.VMEM(stencil_weight.shape, F32),
-            pltpu.VMEM(node_offset.shape, F32),
-            pltpu.VMEM(cell_split.shape, I32),
-            pltpu.VMEM(prev_motion.shape, F32),
-            pltpu.SemaphoreType.DMA((5,)),
+            *(pltpu.VMEM(x.shape, x.dtype) for x in inputs),
+            pltpu.VMEM((384, count), BF16),
+            pltpu.VMEM((256, count), BF16),
+            pltpu.SemaphoreType.DMA((7,)),
         ],
         compiler_params=params(FULL),
-        name="fields",
-    )(even, node_offset, cell_split, prev_motion, stencil_slot, stencil_weight)
+        name="first",
+    )(even, *inputs)
 
 
 def columns_kernel(even_ref, received_ref, plan_ref, *refs):
@@ -650,6 +631,22 @@
     )
 
 
+def hold_kernel(whole_ref, out_ref):
+    out_ref[...] = whole_ref[...]
+
+
+def hold(whole):
+    return pl.pallas_call(
+        hold_kernel,
+        out_shape=jax.ShapeDtypeStruct(whole.shape, F32),
+        in_specs=[VMEM],
+        out_specs=VMEM,
+        compiler_params=params(4),
+        cost_estimate=pl.CostEstimate(flops=2000000, bytes_accessed=1000000, transcendentals=0),
+        name="hold",
+    )(whole)
+
+
 def widened(even, out_ref, to, whole, in_pair, next_pair):
     count = whole.shape[1]
     out_ref[to, :, :DEPTH] = jnp.where(even, next_pair, in_pair)
@@ -704,11 +701,13 @@
 def shards(shell_motion, owner, stencil_slot, stencil_weight, prev_motion, node_offset, cell_split):
     odd = (lax.axis_index("struct") & 1).astype(I32).reshape(1)
     even = 1 - (lax.axis_index("fluid") & 1).astype(I32).reshape(1)
-    packed = pack(owner, shell_motion)
-    sent = fields(even, node_offset, cell_split, prev_motion, stencil_slot, stencil_weight)
+    packed, *sent = pack_and_fields(
+        even, owner, shell_motion, node_offset, cell_split, prev_motion, stencil_slot, stencil_weight
+    )
     apart = planes_apart(sent)
-    packed, apart = lax.optimization_barrier((packed, apart))
-    lattice, prev, plan = widen_fields(even, sent[0], *apart)
+    whole = hold(sent[0])
+    whole, *apart = lax.optimization_barrier((whole, *apart))
+    lattice, prev, plan = widen_fields(even, whole, *apart)
     rows = all_rows(lattice)
     received = lax.all_to_all(packed, BOTH, split_axis=0, concat_axis=0, tiled=True)
     sent = wall_columns(even, received, plan)

time: 51.7 us -> 50.9 us (0.985)
  starting transfers between devices: 22.7 us -> 29 us
  waiting for transfers between devices: 7.32 us -> 1.79 us
  Pallas kernels: 20.4 us -> 18.9 us
    all_to_all x1, waiting for transfers between devices: 5.69 us -> 0.01 us  [shards(): lax.all_to_all(packed, BOTH, split_axis=0, concat_axis=0, tiled=True)]
    all_to_all x1, starting transfers between devices: 6.2 us -> 11.2 us  [shards(): lax.all_to_all(packed, BOTH, split_axis=0, concat_axis=0, tiled=True)]
    pallas_call x2, Pallas kernels: 6.66 us -> 5.15 us  [the longest x1 5.14 us: pack_and_fields(): pl.pallas_call(first_kernel, out_shape=(jax.ShapeDtypeStruct((128, 3, 128...]
    ppermute x10, starting transfers between devices: 16.5 us -> 17.8 us  [swap(): return lax.ppermute(block, BOTH, route)]
  transfers between devices with their start and end apart: 11 -> 11, of which waited for: 2 -> 2; matrix products, arithmetic and copies ran while one was open for 0% -> 0% of each run, Pallas kernels for 28% -> 19%
where the time goes in v5:
time: 50.9 us; the launch traced here: 50.7 us
  starting transfers between devices  29 us (57%)
  Pallas kernels  18.9 us (37%)
  waiting for transfers between devices  1.79 us (4%)
  local copies, waits for them, and re-layouts  0.9 us (2%)
    ppermute x10, starting transfers between devices, swap(): return lax.ppermute(block, BOTH, route)  17.8 us
    all_to_all x1, starting transfers between devices, shards(): lax.all_to_all(packed, BOTH, split_axis=0, concat_axis=0, tiled=True)  11.2 us
    pallas_call x2, Pallas kernels, assemble(): pl.pallas_call(partial(assemble_kernel, start, stop), out_shape=(jax.Shap...  5.92 us
    pallas_call x1, Pallas kernels, pack_and_fields(): pl.pallas_call(first_kernel, out_shape=(jax.ShapeDtypeStruct((128, 3, 128...  5.14 us
    pallas_call x1, Pallas kernels, sweeps(): pl.pallas_call(sweep_kernel, out_shape=jax.ShapeDtypeStruct((3, 2, planes...  4.19 us
    pallas_call x1, Pallas kernels, gather(): pl.pallas_call(gather_kernel, out_shape=jax.ShapeDtypeStruct((3, 2, 8, 12...  2.1 us
    ppermute x10, waiting for transfers between devices, swap(): return lax.ppermute(block, BOTH, route)  1.79 us
  transfers between devices with their start and end apart: 11, of which 2 were waited for; matrix products, arithmetic and copies ran while one was open for 0% of the time, Pallas kernels for 19%

profile of v5, /device:TPU:0, one launch (start us, length us, event | category | flops | bytes accessed | tf_op | source)
XLA Modules:
  0.0 50.7 jit_solution(693758923810489501)
XLA Ops:
  0.0 5.1 %first.1 = (f32[128,3,128]{2,1,0:T(4,128)}, f32[16,2,8,128]{3,2,1,0:T(8,128)}, f32[8,2,4,128]{3,2,1,0:T(4,128)}, f32[8,2,4,128]{3,2,1,0:T(4,128)}) custom-call(s32[1]{0:T(128)} %bitcast.1.even_ref, s32[1,8192]{1,0:T(1,128)} %bitcast.3, f32[3,8192]{1,0:T(4,128)} %refs_1_.1, f32[3,2,8,256]{3,2,1,0:T(8,128)} %refs_2_.1, s32[2,8,256]{2,1,0:T(8,128)} %refs_3_.1, ...), custom_call_target="tpu_custom_call" | custom-call | tf_op jit(solution)/shard_map/first/pallas_call | solution.py:128
  5.1 11.2 %all-to-all-start = ((f32[128,3,128]{2,1,0:T(4,128)}), f32[128,3,128]{2,1,0:T(4,128)S(1)}, u32[]{:S(2)}, u32[]{:S(2)}) async-start(f32[128,3,128]{2,1,0:T(4,128)} %get-tuple-element.39), calls=%async_computation | async-start | bytes 524288 | tf_op jit(solution)/shard_map/all_to_all | solution.py:712
  16.3 0.1 collective-permute-start
  16.4 5.2 %collective-permute-start.1 = (f32[8,2,4,128]{3,2,1,0:T(4,128)}, f32[8,2,4,128]{3,2,1,0:T(4,128)S(1)}, u32[]{:S(2)}, u32[]{:S(2)}) collective-permute-start(f32[8,2,4,128]{3,2,1,0:T(4,128)} %get-tuple-element.34), channel_id=1, source_target_pairs={{0,31},{1,2},{2,1},{3,4},{4,3},{5,6},{6,5},{7,8},{8,7},{9,10},{10,... | collective-permute-start | bytes 98312 | tf_op jit(solution)/shard_map/ppermute | solution.py:623
  21.6 0.9 %copy-done = f32[16,2,8,128]{3,2,1,0:T(8,128)S(1)} copy-done((f32[16,2,8,128]{3,2,1,0:T(8,128)S(1)}, f32[16,2,8,128]{3,2,1,0:T(8,128)}, u32[]{:S(2)}) %copy-start) | copy-done | bytes 131096
  22.6 1.1 %collective-permute-done.1.next_ref = f32[8,2,4,128]{3,2,1,0:T(4,128)S(1)} collective-permute-done((f32[8,2,4,128]{3,2,1,0:T(4,128)}, f32[8,2,4,128]{3,2,1,0:T(4,128)S(1)}, u32[]{:S(2)}, u32[]{:S(2)}) %collective-permute-start.1) | collective-permute-done | bytes 32800 | tf_op jit(solution)/shard_map/ppermute | solution.py:623
  23.7 3.9 %collective-permute-start.4 = (f32[5,2,16,128]{3,2,1,0:T(8,128)S(1)}, f32[5,2,16,128]{3,2,1,0:T(8,128)S(1)}, u32[]{:S(2)}, u32[]{:S(2)}) collective-permute-start(f32[5,2,16,128]{3,2,1,0:T(8,128)S(1)} %get-tuple-element.38.own_ref), channel_id=1, source_target_pairs={{0,96},{1,97},{2,98},{3,99},{4,100},{5,101},{6,102},{7,103},{8,104... | collective-permute-start | bytes 245768 | tf_op jit(solution)/shard_map/ppermute | solution.py:623
  27.7 1.0 %collective-permute-start.3 = (f32[5,2,16,128]{3,2,1,0:T(8,128)S(1)}, f32[5,2,16,128]{3,2,1,0:T(8,128)S(1)}, u32[]{:S(2)}, u32[]{:S(2)}) collective-permute-start(f32[5,2,16,128]{3,2,1,0:T(8,128)S(1)} %get-tuple-element.38.own_ref), channel_id=1, source_target_pairs={{0,64},{1,65},{2,66},{3,67},{4,68},{5,69},{6,70},{7,71},{8,72},{9,... | collective-permute-start | bytes 245768 | tf_op jit(solution)/shard_map/ppermute | solution.py:623
  28.6 0.0 collective-permute-start.2
  28.6 0.0 all-to-all-done.received_ref
  28.6 1.0 %columns.1 = (f32[1,2,8,128]{3,2,1,0:T(8,128)S(1)}, f32[1,2,4,128]{3,2,1,0:T(4,128)S(1)}, f32[1,2,4,128]{3,2,1,0:T(4,128)S(1)}) custom-call(s32[1]{0:T(128)} %bitcast.1.even_ref, f32[128,3,128]{2,1,0:T(4,128)S(1)} %all-to-all-done.received_ref, f32[8,2,8,128]{3,2,1,0:T(8,128)S(1)} %get-tuple-element.40.plan_ref), custom_call_target="tpu_custom_call" | custom-call | tf_op jit(solution)/shard_map/columns/pallas_call | solution.py:184
  29.6 0.1 collective-permute-start.5
  29.7 3.3 %collective-permute-start.6 = (f32[1,2,4,128]{3,2,1,0:T(4,128)S(1)}, f32[1,2,4,128]{3,2,1,0:T(4,128)S(1)}, u32[]{:S(2)}, u32[]{:S(2)}) collective-permute-start(f32[1,2,4,128]{3,2,1,0:T(4,128)S(1)} %get-tuple-element.48), channel_id=1, source_target_pairs={{0,31},{1,2},{2,1},{3,4},{4,3},{5,6},{6,5},{7,8},{8,7},{9,10},{10,... | collective-permute-start | bytes 12296 | tf_op jit(solution)/shard_map/ppermute | solution.py:623
  33.0 0.6 %collective-permute-done.3.swap2_ref = f32[5,2,16,128]{3,2,1,0:T(8,128)S(1)} collective-permute-done((f32[5,2,16,128]{3,2,1,0:T(8,128)S(1)}, f32[5,2,16,128]{3,2,1,0:T(8,128)S(1)}, u32[]{:S(2)}, u32[]{:S(2)}) %collective-permute-start.3) | collective-permute-done | bytes 81952 | tf_op jit(solution)/shard_map/ppermute | solution.py:623
  33.6 0.0 collective-permute-done.2.swap1_ref
  33.6 0.6 %setup.1 = (f32[5,16,8,128]{3,2,1,0:T(8,128)S(1)}, f32[17,6,8,128]{3,2,1,0:T(8,128)S(1)}) custom-call(s32[1]{0:T(128)} %bitcast.odd_ref, f32[5,2,16,128]{3,2,1,0:T(8,128)S(1)} %get-tuple-element.38.own_ref, f32[5,2,16,128]{3,2,1,0:T(8,128)S(1)} %collective-permute-done.2.swap1_ref, f32[5,2,16,128]{3,2,1,0:T(8,128)S(1)} %collective-permute-done.3.swap2_ref, ...), custom_call_target="tpu_custom_call" | custom-call | flops 20000000 | bytes 1000000 | tf_op jit(solution)/shard_map/setup/pallas_call | solution.py:426
  34.2 2.9 %assemble.2 = (f32[9,27,6,8,128]{4,3,2,1,0:T(8,128)S(1)}, f32[9,3,8,128]{3,2,1,0:T(8,128)S(1)}) custom-call(f32[5,16,8,128]{3,2,1,0:T(8,128)S(1)} %get-tuple-element.54.field_ref, f32[17,6,8,128]{3,2,1,0:T(8,128)S(1)} %get-tuple-element.55.side_ref), custom_call_target="tpu_custom_call" | custom-call | flops 160000000 | bytes 1000000 | tf_op jit(solution)/shard_map/assemble/pallas_call | solution.py:526
  37.1 0.0 collective-permute-done.6.next_ref
  37.2 2.2 %collective-permute-start.9 = (f32[4,2,16,128]{3,2,1,0:T(8,128)S(1)}, f32[4,2,16,128]{3,2,1,0:T(8,128)S(1)}, u32[]{:S(2)}, u32[]{:S(2)}) collective-permute-start(f32[4,2,16,128]{3,2,1,0:T(8,128)S(1)} %widen_wall.1.refs_0_), channel_id=1, source_target_pairs={{0,96},{1,97},{2,98},{3,99},{4,100},{5,101},{6,102},{7,103},{8,104... | collective-permute-start | bytes 196616 | tf_op jit(solution)/shard_map/ppermute | solution.py:623
  39.4 0.9 %collective-permute-start.8 = (f32[4,2,16,128]{3,2,1,0:T(8,128)S(1)}, f32[4,2,16,128]{3,2,1,0:T(8,128)S(1)}, u32[]{:S(2)}, u32[]{:S(2)}) collective-permute-start(f32[4,2,16,128]{3,2,1,0:T(8,128)S(1)} %widen_wall.1.refs_0_), channel_id=1, source_target_pairs={{0,64},{1,65},{2,66},{3,67},{4,68},{5,69},{6,70},{7,71},{8,72},{9,... | collective-permute-start | bytes 196616 | tf_op jit(solution)/shard_map/ppermute | solution.py:623
  40.3 1.1 %collective-permute-start.7 = (f32[4,2,16,128]{3,2,1,0:T(8,128)S(1)}, f32[4,2,16,128]{3,2,1,0:T(8,128)S(1)}, u32[]{:S(2)}, u32[]{:S(2)}) collective-permute-start(f32[4,2,16,128]{3,2,1,0:T(8,128)S(1)} %widen_wall.1.refs_0_), channel_id=1, source_target_pairs={{0,32},{1,33},{2,34},{3,35},{4,36},{5,37},{6,38},{7,39},{8,40},{9,... | collective-permute-start | bytes 196616 | tf_op jit(solution)/shard_map/ppermute | solution.py:623
  41.4 2.1 %gather.1.refs_8_ = f32[3,2,8,128]{3,2,1,0:T(8,128)S(1)} custom-call(f32[128,3,128]{2,1,0:T(4,128)S(1)} %all-to-all-done.received_ref, f32[8,2,8,128]{3,2,1,0:T(8,128)S(1)} %get-tuple-element.40.plan_ref), custom_call_target="tpu_custom_call" | custom-call | flops 60000000 | bytes 1000000 | tf_op jit(solution)/shard_map/gather/pallas_call | solution.py:230
  43.5 3.0 %assemble.3 = (f32[9,27,6,8,128]{4,3,2,1,0:T(8,128)S(1)}, f32[9,3,8,128]{3,2,1,0:T(8,128)S(1)}) custom-call(f32[5,16,8,128]{3,2,1,0:T(8,128)S(1)} %get-tuple-element.54.field_ref, f32[17,6,8,128]{3,2,1,0:T(8,128)S(1)} %get-tuple-element.55.side_ref), custom_call_target="tpu_custom_call" | custom-call | flops 160000000 | bytes 1000000 | tf_op jit(solution)/shard_map/assemble/pallas_call | solution.py:526
  46.5 4.2 %sweeps.1 = f32[3,2,8,256]{3,2,1,0:T(8,128)} custom-call(s32[1]{0:T(128)} %bitcast.odd_ref, f32[4,2,16,128]{3,2,1,0:T(8,128)S(1)} %widen_wall.1.refs_0_, f32[4,2,16,128]{3,2,1,0:T(8,128)S(1)} %collective-permute-done.7.refs_1_, f32[4,2,16,128]{3,2,1,0:T(8,128)S(1)} %collective-permute-done.8.refs_2_, f32[4,2,16,128]{3,2,1,0:T(8,128)S(1)} %collective-permute-done.9.refs_3_, ...), custom_call_target="tpu_custom_call" | custom-call | tf_op jit(solution)/shard_map/sweeps/pallas_call | solution.py:602
  (10 shorter events, 0.1 us)
Async XLA Ops:
  5.1 23.5 %all-to-all-start = ((f32[128,3,128]{2,1,0:T(4,128)}), f32[128,3,128]{2,1,0:T(4,128)S(1)}, u32[]{:S(2)}, u32[]{:S(2)}) async-start(f32[128,3,128]{2,1,0:T(4,128)} %get-tuple-element.39), calls=%async_computation | async-start | bytes 524288 | tf_op jit(solution)/shard_map/all_to_all | solution.py:712
  16.3 6.3 %collective-permute-start = (f32[8,2,4,128]{3,2,1,0:T(4,128)}, f32[8,2,4,128]{3,2,1,0:T(4,128)S(1)}, u32[]{:S(2)}, u32[]{:S(2)}) collective-permute-start(f32[8,2,4,128]{3,2,1,0:T(4,128)} %get-tuple-element.33), channel_id=1, source_target_pairs={{0,1},{1,0},{2,3},{3,2},{4,5},{5,4},{6,7},{7,6},{8,9},{9,8},{10,11... | collective-permute-start | bytes 98312 | tf_op jit(solution)/shard_map/ppermute | solution.py:623
  16.4 7.3 %collective-permute-start.1 = (f32[8,2,4,128]{3,2,1,0:T(4,128)}, f32[8,2,4,128]{3,2,1,0:T(4,128)S(1)}, u32[]{:S(2)}, u32[]{:S(2)}) collective-permute-start(f32[8,2,4,128]{3,2,1,0:T(4,128)} %get-tuple-element.34), channel_id=1, source_target_pairs={{0,31},{1,2},{2,1},{3,4},{4,3},{5,6},{6,5},{7,8},{8,7},{9,10},{10,... | collective-permute-start | bytes 98312 | tf_op jit(solution)/shard_map/ppermute | solution.py:623
  21.6 0.9 %copy-start = (f32[16,2,8,128]{3,2,1,0:T(8,128)S(1)}, f32[16,2,8,128]{3,2,1,0:T(8,128)}, u32[]{:S(2)}) copy-start(f32[16,2,8,128]{3,2,1,0:T(8,128)} %get-tuple-element.32.whole_ref) | copy-start | bytes 393220
  23.7 9.3 %collective-permute-start.4 = (f32[5,2,16,128]{3,2,1,0:T(8,128)S(1)}, f32[5,2,16,128]{3,2,1,0:T(8,128)S(1)}, u32[]{:S(2)}, u32[]{:S(2)}) collective-permute-start(f32[5,2,16,128]{3,2,1,0:T(8,128)S(1)} %get-tuple-element.38.own_ref), channel_id=1, source_target_pairs={{0,96},{1,97},{2,98},{3,99},{4,100},{5,101},{6,102},{7,103},{8,104... | collective-permute-start | bytes 245768 | tf_op jit(solution)/shard_map/ppermute | solution.py:623
  27.7 5.9 %collective-permute-start.3 = (f32[5,2,16,128]{3,2,1,0:T(8,128)S(1)}, f32[5,2,16,128]{3,2,1,0:T(8,128)S(1)}, u32[]{:S(2)}, u32[]{:S(2)}) collective-permute-start(f32[5,2,16,128]{3,2,1,0:T(8,128)S(1)} %get-tuple-element.38.own_ref), channel_id=1, source_target_pairs={{0,64},{1,65},{2,66},{3,67},{4,68},{5,69},{6,70},{7,71},{8,72},{9,... | collective-permute-start | bytes 245768 | tf_op jit(solution)/shard_map/ppermute | solution.py:623
  28.6 5.0 %collective-permute-start.2 = (f32[5,2,16,128]{3,2,1,0:T(8,128)S(1)}, f32[5,2,16,128]{3,2,1,0:T(8,128)S(1)}, u32[]{:S(2)}, u32[]{:S(2)}) collective-permute-start(f32[5,2,16,128]{3,2,1,0:T(8,128)S(1)} %get-tuple-element.38.own_ref), channel_id=1, source_target_pairs={{0,32},{1,33},{2,34},{3,35},{4,36},{5,37},{6,38},{7,39},{8,40},{9,... | collective-permute-start | bytes 245768 | tf_op jit(solution)/shard_map/ppermute | solution.py:623
  29.6 7.5 %collective-permute-start.5 = (f32[1,2,4,128]{3,2,1,0:T(4,128)S(1)}, f32[1,2,4,128]{3,2,1,0:T(4,128)S(1)}, u32[]{:S(2)}, u32[]{:S(2)}) collective-permute-start(f32[1,2,4,128]{3,2,1,0:T(4,128)S(1)} %get-tuple-element.47), channel_id=1, source_target_pairs={{0,1},{1,0},{2,3},{3,2},{4,5},{5,4},{6,7},{7,6},{8,9},{9,8},{10,11... | collective-permute-start | bytes 12296 | tf_op jit(solution)/shard_map/ppermute | solution.py:623
  29.7 7.5 %collective-permute-start.6 = (f32[1,2,4,128]{3,2,1,0:T(4,128)S(1)}, f32[1,2,4,128]{3,2,1,0:T(4,128)S(1)}, u32[]{:S(2)}, u32[]{:S(2)}) collective-permute-start(f32[1,2,4,128]{3,2,1,0:T(4,128)S(1)} %get-tuple-element.48), channel_id=1, source_target_pairs={{0,31},{1,2},{2,1},{3,4},{4,3},{5,6},{6,5},{7,8},{8,7},{9,10},{10,... | collective-permute-start | bytes 12296 | tf_op jit(solution)/shard_map/ppermute | solution.py:623
  37.2 9.3 %collective-permute-start.9 = (f32[4,2,16,128]{3,2,1,0:T(8,128)S(1)}, f32[4,2,16,128]{3,2,1,0:T(8,128)S(1)}, u32[]{:S(2)}, u32[]{:S(2)}) collective-permute-start(f32[4,2,16,128]{3,2,1,0:T(8,128)S(1)} %widen_wall.1.refs_0_), channel_id=1, source_target_pairs={{0,96},{1,97},{2,98},{3,99},{4,100},{5,101},{6,102},{7,103},{8,104... | collective-permute-start | bytes 196616 | tf_op jit(solution)/shard_map/ppermute | solution.py:623
  39.4 7.1 %collective-permute-start.8 = (f32[4,2,16,128]{3,2,1,0:T(8,128)S(1)}, f32[4,2,16,128]{3,2,1,0:T(8,128)S(1)}, u32[]{:S(2)}, u32[]{:S(2)}) collective-permute-start(f32[4,2,16,128]{3,2,1,0:T(8,128)S(1)} %widen_wall.1.refs_0_), channel_id=1, source_target_pairs={{0,64},{1,65},{2,66},{3,67},{4,68},{5,69},{6,70},{7,71},{8,72},{9,... | collective-permute-start | bytes 196616 | tf_op jit(solution)/shard_map/ppermute | solution.py:623
  40.3 6.2 %collective-permute-start.7 = (f32[4,2,16,128]{3,2,1,0:T(8,128)S(1)}, f32[4,2,16,128]{3,2,1,0:T(8,128)S(1)}, u32[]{:S(2)}, u32[]{:S(2)}) collective-permute-start(f32[4,2,16,128]{3,2,1,0:T(8,128)S(1)} %widen_wall.1.refs_0_), channel_id=1, source_target_pairs={{0,32},{1,33},{2,34},{3,35},{4,36},{5,37},{6,38},{7,39},{8,40},{9,... | collective-permute-start | bytes 196616 | tf_op jit(solution)/shard_map/ppermute | solution.py:623

commit v6 on v5

--- a/solution.py
+++ b/solution.py
@@ -255,7 +255,7 @@
     ]
 
 
-def cell_blocks(corner, code):
+def cell_gradients(corner, code):
     flip_y = code >= 2
     flip_z = (code == 1) | (code == 3)
     sign_y = jnp.where(flip_y, -1.0, 1.0)
@@ -279,7 +279,7 @@
         edge[v] = moved
     top = (1, 1, 1)
     over = {v: cross(edge[v], edge[top]) for v in CORNERS[1:-1]}
-    blocks = {}
+    tetrahedra = []
     for order in STEP_ORDERS:
         at = [0, 0, 0]
         path = [(0, 0, 0)]
@@ -293,18 +293,36 @@
         minus = -inverse
         grad = [None, [w * inverse for w in over[two]], [w * minus for w in over[one]], [w * inverse for w in third]]
         grad[0] = [grad[1][p] + grad[2][p] + grad[3][p] for p in range(3)]
+        tetrahedra.append((path, grad))
+    return (flip_y, flip_z), tetrahedra
+
+
+def edge_products(tetrahedra, p, q):
+    sums = {}
+    for path, grad in tetrahedra:
         for i in range(4):
             for j in range(i + 1, 4):
                 g, h = grad[i], grad[j]
-                block = [g[p] * h[p] for p in range(3)]
-                block += [g[p] * h[q] + g[q] * h[p] for p, q in ((0, 1), (0, 2), (1, 2))]
+                product = g[p] * h[p] if p == q else g[p] * h[q] + g[q] * h[p]
                 key = (path[i], path[j])
-                blocks[key] = plus(blocks[key], block) if key in blocks else block
-    for (v, _), block in blocks.items():
-        trace = block[0] + block[1] + block[2]
-        block[:3] = [same + same + trace for same in block[:3]]
-        if v == (0, 0, 0):
-            block[:] = [-w for w in block]
+                sums[key] = sums[key] + product if key in sums else product
+    return sums
+
+
+def edge_entries(tetrahedra):
+    squares = [edge_products(tetrahedra, p, p) for p in range(3)]
+    trace = {key: squares[0][key] + squares[1][key] + squares[2][key] for key in squares[0]}
+    for e, (p, q) in enumerate(((0, 0), (1, 1), (2, 2), (0, 1), (0, 2), (1, 2))):
+        if p == q:
+            values = {key: v + v + trace[key] for key, v in squares[p].items()}
+        else:
+            values = edge_products(tetrahedra, p, q)
+        yield e, {key: [-v if key[0] == (0, 0, 0) else v] for key, v in values.items()}
+
+
+def cell_kinds(blocks, flips):
+    flip_y, flip_z = flips
+    top = (1, 1, 1)
 
     def pick(mask, yes, no):
         return [jnp.where(mask, y, n) for y, n in zip(yes, no)]
@@ -415,10 +433,11 @@
             for c, plane in ((0, low), (1, pltpu.roll(low, 128 - gap, 1))):
                 corner.setdefault((a, 0, c), []).append(plane)
                 corner.setdefault((a, 1, c), []).append(pltpu.roll(plane, 7, 0))
-    moving, _ = node_parts(cell_blocks(corner, pltpu.roll(packed, 125, 1)))
-    for m, name in enumerate(MOVING):
-        for e in range(6):
-            side_ref[m, e] = moving[name][e]
+    flips, tetrahedra = cell_gradients(corner, pltpu.roll(packed, 125, 1))
+    for e, blocks in edge_entries(tetrahedra):
+        moving, _ = node_parts(cell_kinds(blocks, flips))
+        for m, name in enumerate(MOVING):
+            side_ref[m, e] = moving[name][0]
 
 
 def setup(odd, rows, after):
@@ -443,35 +462,19 @@
     lane = lax.broadcasted_iota(I32, (8, 128), 1)
     first, last = lane == 0, lane == 127
 
-    def cells(k, _):
-        corner = {}
-        for c in BITS:
-            edge = field_ref[4, k + c]
-            edges = (edge, pltpu.roll(edge, 7, 0))
-            for p in range(3):
-                low = field_ref[p, k + c]
-                for b, row in ((0, low), (1, pltpu.roll(low, 7, 0))):
-                    beyond = pltpu.roll(edges[b], 2 - p, 1) if p < 2 else edges[b]
-                    corner.setdefault((0, b, c), []).append(row)
-                    corner.setdefault((1, b, c), []).append(jnp.where(last, beyond, pltpu.roll(row, 127, 1)))
-        moving, still = node_parts(cell_blocks(corner, field_ref[3, k]))
+    def scatter(k, e, moving, still):
         shift = 128 - k * gap
 
         def back_x(name):
             m = MOVING.index(name)
-            return [
-                jnp.where(first, pltpu.roll(side_ref[m, e], shift, 1), pltpu.roll(moving[name][e], 1, 1))
-                for e in range(6)
-            ]
+            return [jnp.where(first, pltpu.roll(side_ref[m, e], shift, 1), pltpu.roll(moving[name][0], 1, 1))]
 
         def put(plane, step, values):
-            for e in range(6):
-                coef_ref[plane, SLOT_OF[step], e] = values[e]
+            coef_ref[plane, SLOT_OF[step], e] = values[0]
 
         def add(plane, step, values):
             at = SLOT_OF[step]
-            for e in range(6):
-                coef_ref[plane, at, e] = coef_ref[plane, at, e] + values[e]
+            coef_ref[plane, at, e] = coef_ref[plane, at, e] + values[0]
 
         low, high = k - start, k + 1 - start
         s = plus(still["z"], back_x("z"))
@@ -505,6 +508,21 @@
             store(plane, (-1, -1, 0), back_x(("up", c)))
             store(plane, (1, -1, 0), still["down", c])
             store(plane, (-1, 1, 0), back_x(("down", c)))
+
+    def cells(k, _):
+        corner = {}
+        for c in BITS:
+            edge = field_ref[4, k + c]
+            edges = (edge, pltpu.roll(edge, 7, 0))
+            for p in range(3):
+                low = field_ref[p, k + c]
+                for b, row in ((0, low), (1, pltpu.roll(low, 7, 0))):
+                    beyond = pltpu.roll(edges[b], 2 - p, 1) if p < 2 else edges[b]
+                    corner.setdefault((0, b, c), []).append(row)
+                    corner.setdefault((1, b, c), []).append(jnp.where(last, beyond, pltpu.roll(row, 127, 1)))
+        flips, tetrahedra = cell_gradients(corner, field_ref[3, k])
+        for e, blocks in edge_entries(tetrahedra):
+            scatter(k, e, *node_parts(cell_kinds(blocks, flips)))
         return 0
 
     lax.fori_loop(start, stop, cells, 0, unroll=8)

time: 50.9 us -> 51 us (level)
  no operation moved by 1% of the time
where the time goes in v6:
time: 51 us; the launch traced here: 50.8 us
  starting transfers between devices  29 us (57%)
  Pallas kernels  19 us (37%)
  waiting for transfers between devices  1.79 us (4%)
  local copies, waits for them, and re-layouts  0.9 us (2%)
    ppermute x10, starting transfers between devices, swap(): return lax.ppermute(block, BOTH, route)  17.8 us
    all_to_all x1, starting transfers between devices, shards(): lax.all_to_all(packed, BOTH, split_axis=0, concat_axis=0, tiled=True)  11.2 us
    pallas_call x2, Pallas kernels, assemble(): pl.pallas_call(partial(assemble_kernel, start, stop), out_shape=(jax.Shap...  6.01 us
    pallas_call x1, Pallas kernels, pack_and_fields(): pl.pallas_call(first_kernel, out_shape=(jax.ShapeDtypeStruct((128, 3, 128...  5.14 us
    pallas_call x1, Pallas kernels, sweeps(): pl.pallas_call(sweep_kernel, out_shape=jax.ShapeDtypeStruct((3, 2, planes...  4.19 us
    pallas_call x1, Pallas kernels, gather(): pl.pallas_call(gather_kernel, out_shape=jax.ShapeDtypeStruct((3, 2, 8, 12...  2.1 us
    ppermute x10, waiting for transfers between devices, swap(): return lax.ppermute(block, BOTH, route)  1.79 us
  transfers between devices with their start and end apart: 11, of which 2 were waited for; matrix products, arithmetic and copies ran while one was open for 0% of the time, Pallas kernels for 19%

profile of v6, /device:TPU:0, one launch (start us, length us, event | category | flops | bytes accessed | tf_op | source)
XLA Modules:
  0.0 50.8 jit_solution(10444332264146809388)
XLA Ops:
  0.0 5.1 %first.1 = (f32[128,3,128]{2,1,0:T(4,128)}, f32[16,2,8,128]{3,2,1,0:T(8,128)}, f32[8,2,4,128]{3,2,1,0:T(4,128)}, f32[8,2,4,128]{3,2,1,0:T(4,128)}) custom-call(s32[1]{0:T(128)} %bitcast.1.even_ref, s32[1,8192]{1,0:T(1,128)} %bitcast.3, f32[3,8192]{1,0:T(4,128)} %refs_1_.1, f32[3,2,8,256]{3,2,1,0:T(8,128)} %refs_2_.1, s32[2,8,256]{2,1,0:T(8,128)} %refs_3_.1, ...), custom_call_target="tpu_custom_call" | custom-call | tf_op jit(solution)/shard_map/first/pallas_call | solution.py:128
  5.1 11.2 %all-to-all-start = ((f32[128,3,128]{2,1,0:T(4,128)}), f32[128,3,128]{2,1,0:T(4,128)S(1)}, u32[]{:S(2)}, u32[]{:S(2)}) async-start(f32[128,3,128]{2,1,0:T(4,128)} %get-tuple-element.39), calls=%async_computation | async-start | bytes 524288 | tf_op jit(solution)/shard_map/all_to_all | solution.py:730
  16.3 0.1 collective-permute-start
  16.4 5.2 %collective-permute-start.1 = (f32[8,2,4,128]{3,2,1,0:T(4,128)}, f32[8,2,4,128]{3,2,1,0:T(4,128)S(1)}, u32[]{:S(2)}, u32[]{:S(2)}) collective-permute-start(f32[8,2,4,128]{3,2,1,0:T(4,128)} %get-tuple-element.34), channel_id=1, source_target_pairs={{0,31},{1,2},{2,1},{3,4},{4,3},{5,6},{6,5},{7,8},{8,7},{9,10},{10,... | collective-permute-start | bytes 98312 | tf_op jit(solution)/shard_map/ppermute | solution.py:641
  21.6 0.9 %copy-done = f32[16,2,8,128]{3,2,1,0:T(8,128)S(1)} copy-done((f32[16,2,8,128]{3,2,1,0:T(8,128)S(1)}, f32[16,2,8,128]{3,2,1,0:T(8,128)}, u32[]{:S(2)}) %copy-start) | copy-done | bytes 131096
  22.6 1.1 %collective-permute-done.1.next_ref = f32[8,2,4,128]{3,2,1,0:T(4,128)S(1)} collective-permute-done((f32[8,2,4,128]{3,2,1,0:T(4,128)}, f32[8,2,4,128]{3,2,1,0:T(4,128)S(1)}, u32[]{:S(2)}, u32[]{:S(2)}) %collective-permute-start.1) | collective-permute-done | bytes 32800 | tf_op jit(solution)/shard_map/ppermute | solution.py:641
  23.7 3.9 %collective-permute-start.4 = (f32[5,2,16,128]{3,2,1,0:T(8,128)S(1)}, f32[5,2,16,128]{3,2,1,0:T(8,128)S(1)}, u32[]{:S(2)}, u32[]{:S(2)}) collective-permute-start(f32[5,2,16,128]{3,2,1,0:T(8,128)S(1)} %get-tuple-element.38.own_ref), channel_id=1, source_target_pairs={{0,96},{1,97},{2,98},{3,99},{4,100},{5,101},{6,102},{7,103},{8,104... | collective-permute-start | bytes 245768 | tf_op jit(solution)/shard_map/ppermute | solution.py:641
  27.7 1.0 %collective-permute-start.3 = (f32[5,2,16,128]{3,2,1,0:T(8,128)S(1)}, f32[5,2,16,128]{3,2,1,0:T(8,128)S(1)}, u32[]{:S(2)}, u32[]{:S(2)}) collective-permute-start(f32[5,2,16,128]{3,2,1,0:T(8,128)S(1)} %get-tuple-element.38.own_ref), channel_id=1, source_target_pairs={{0,64},{1,65},{2,66},{3,67},{4,68},{5,69},{6,70},{7,71},{8,72},{9,... | collective-permute-start | bytes 245768 | tf_op jit(solution)/shard_map/ppermute | solution.py:641
  28.6 0.0 collective-permute-start.2
  28.6 0.0 all-to-all-done.received_ref
  28.6 1.0 %columns.1 = (f32[1,2,8,128]{3,2,1,0:T(8,128)S(1)}, f32[1,2,4,128]{3,2,1,0:T(4,128)S(1)}, f32[1,2,4,128]{3,2,1,0:T(4,128)S(1)}) custom-call(s32[1]{0:T(128)} %bitcast.1.even_ref, f32[128,3,128]{2,1,0:T(4,128)S(1)} %all-to-all-done.received_ref, f32[8,2,8,128]{3,2,1,0:T(8,128)S(1)} %get-tuple-element.40.plan_ref), custom_call_target="tpu_custom_call" | custom-call | tf_op jit(solution)/shard_map/columns/pallas_call | solution.py:184
  29.6 0.1 collective-permute-start.5
  29.7 3.3 %collective-permute-start.6 = (f32[1,2,4,128]{3,2,1,0:T(4,128)S(1)}, f32[1,2,4,128]{3,2,1,0:T(4,128)S(1)}, u32[]{:S(2)}, u32[]{:S(2)}) collective-permute-start(f32[1,2,4,128]{3,2,1,0:T(4,128)S(1)} %get-tuple-element.48), channel_id=1, source_target_pairs={{0,31},{1,2},{2,1},{3,4},{4,3},{5,6},{6,5},{7,8},{8,7},{9,10},{10,... | collective-permute-start | bytes 12296 | tf_op jit(solution)/shard_map/ppermute | solution.py:641
  33.0 0.6 %collective-permute-done.3.swap2_ref = f32[5,2,16,128]{3,2,1,0:T(8,128)S(1)} collective-permute-done((f32[5,2,16,128]{3,2,1,0:T(8,128)S(1)}, f32[5,2,16,128]{3,2,1,0:T(8,128)S(1)}, u32[]{:S(2)}, u32[]{:S(2)}) %collective-permute-start.3) | collective-permute-done | bytes 81952 | tf_op jit(solution)/shard_map/ppermute | solution.py:641
  33.6 0.0 collective-permute-done.2.swap1_ref
  33.6 0.6 %setup.1 = (f32[5,16,8,128]{3,2,1,0:T(8,128)S(1)}, f32[17,6,8,128]{3,2,1,0:T(8,128)S(1)}) custom-call(s32[1]{0:T(128)} %bitcast.odd_ref, f32[5,2,16,128]{3,2,1,0:T(8,128)S(1)} %get-tuple-element.38.own_ref, f32[5,2,16,128]{3,2,1,0:T(8,128)S(1)} %collective-permute-done.2.swap1_ref, f32[5,2,16,128]{3,2,1,0:T(8,128)S(1)} %collective-permute-done.3.swap2_ref, ...), custom_call_target="tpu_custom_call" | custom-call | flops 20000000 | bytes 1000000 | tf_op jit(solution)/shard_map/setup/pallas_call | solution.py:445
  34.2 3.0 %assemble.2 = (f32[9,27,6,8,128]{4,3,2,1,0:T(8,128)S(1)}, f32[9,3,8,128]{3,2,1,0:T(8,128)S(1)}) custom-call(f32[5,16,8,128]{3,2,1,0:T(8,128)S(1)} %get-tuple-element.54.field_ref, f32[17,6,8,128]{3,2,1,0:T(8,128)S(1)} %get-tuple-element.55.side_ref), custom_call_target="tpu_custom_call" | custom-call | flops 160000000 | bytes 1000000 | tf_op jit(solution)/shard_map/assemble/pallas_call | solution.py:544
  37.2 0.0 collective-permute-done.6.next_ref
  37.2 2.2 %collective-permute-start.9 = (f32[4,2,16,128]{3,2,1,0:T(8,128)S(1)}, f32[4,2,16,128]{3,2,1,0:T(8,128)S(1)}, u32[]{:S(2)}, u32[]{:S(2)}) collective-permute-start(f32[4,2,16,128]{3,2,1,0:T(8,128)S(1)} %widen_wall.1.refs_0_), channel_id=1, source_target_pairs={{0,96},{1,97},{2,98},{3,99},{4,100},{5,101},{6,102},{7,103},{8,104... | collective-permute-start | bytes 196616 | tf_op jit(solution)/shard_map/ppermute | solution.py:641
  39.4 0.9 %collective-permute-start.8 = (f32[4,2,16,128]{3,2,1,0:T(8,128)S(1)}, f32[4,2,16,128]{3,2,1,0:T(8,128)S(1)}, u32[]{:S(2)}, u32[]{:S(2)}) collective-permute-start(f32[4,2,16,128]{3,2,1,0:T(8,128)S(1)} %widen_wall.1.refs_0_), channel_id=1, source_target_pairs={{0,64},{1,65},{2,66},{3,67},{4,68},{5,69},{6,70},{7,71},{8,72},{9,... | collective-permute-start | bytes 196616 | tf_op jit(solution)/shard_map/ppermute | solution.py:641
  40.3 1.1 %collective-permute-start.7 = (f32[4,2,16,128]{3,2,1,0:T(8,128)S(1)}, f32[4,2,16,128]{3,2,1,0:T(8,128)S(1)}, u32[]{:S(2)}, u32[]{:S(2)}) collective-permute-start(f32[4,2,16,128]{3,2,1,0:T(8,128)S(1)} %widen_wall.1.refs_0_), channel_id=1, source_target_pairs={{0,32},{1,33},{2,34},{3,35},{4,36},{5,37},{6,38},{7,39},{8,40},{9,... | collective-permute-start | bytes 196616 | tf_op jit(solution)/shard_map/ppermute | solution.py:641
  41.4 2.1 %gather.1.refs_8_ = f32[3,2,8,128]{3,2,1,0:T(8,128)S(1)} custom-call(f32[128,3,128]{2,1,0:T(4,128)S(1)} %all-to-all-done.received_ref, f32[8,2,8,128]{3,2,1,0:T(8,128)S(1)} %get-tuple-element.40.plan_ref), custom_call_target="tpu_custom_call" | custom-call | flops 60000000 | bytes 1000000 | tf_op jit(solution)/shard_map/gather/pallas_call | solution.py:230
  43.5 3.1 %assemble.3 = (f32[9,27,6,8,128]{4,3,2,1,0:T(8,128)S(1)}, f32[9,3,8,128]{3,2,1,0:T(8,128)S(1)}) custom-call(f32[5,16,8,128]{3,2,1,0:T(8,128)S(1)} %get-tuple-element.54.field_ref, f32[17,6,8,128]{3,2,1,0:T(8,128)S(1)} %get-tuple-element.55.side_ref), custom_call_target="tpu_custom_call" | custom-call | flops 160000000 | bytes 1000000 | tf_op jit(solution)/shard_map/assemble/pallas_call | solution.py:544
  46.6 4.2 %sweeps.1 = f32[3,2,8,256]{3,2,1,0:T(8,128)} custom-call(s32[1]{0:T(128)} %bitcast.odd_ref, f32[4,2,16,128]{3,2,1,0:T(8,128)S(1)} %widen_wall.1.refs_0_, f32[4,2,16,128]{3,2,1,0:T(8,128)S(1)} %collective-permute-done.7.refs_1_, f32[4,2,16,128]{3,2,1,0:T(8,128)S(1)} %collective-permute-done.8.refs_2_, f32[4,2,16,128]{3,2,1,0:T(8,128)S(1)} %collective-permute-done.9.refs_3_, ...), custom_call_target="tpu_custom_call" | custom-call | tf_op jit(solution)/shard_map/sweeps/pallas_call | solution.py:620
  (10 shorter events, 0.1 us)
Async XLA Ops:
  5.1 23.5 %all-to-all-start = ((f32[128,3,128]{2,1,0:T(4,128)}), f32[128,3,128]{2,1,0:T(4,128)S(1)}, u32[]{:S(2)}, u32[]{:S(2)}) async-start(f32[128,3,128]{2,1,0:T(4,128)} %get-tuple-element.39), calls=%async_computation | async-start | bytes 524288 | tf_op jit(solution)/shard_map/all_to_all | solution.py:730
  16.3 6.3 %collective-permute-start = (f32[8,2,4,128]{3,2,1,0:T(4,128)}, f32[8,2,4,128]{3,2,1,0:T(4,128)S(1)}, u32[]{:S(2)}, u32[]{:S(2)}) collective-permute-start(f32[8,2,4,128]{3,2,1,0:T(4,128)} %get-tuple-element.33), channel_id=1, source_target_pairs={{0,1},{1,0},{2,3},{3,2},{4,5},{5,4},{6,7},{7,6},{8,9},{9,8},{10,11... | collective-permute-start | bytes 98312 | tf_op jit(solution)/shard_map/ppermute | solution.py:641
  16.4 7.3 %collective-permute-start.1 = (f32[8,2,4,128]{3,2,1,0:T(4,128)}, f32[8,2,4,128]{3,2,1,0:T(4,128)S(1)}, u32[]{:S(2)}, u32[]{:S(2)}) collective-permute-start(f32[8,2,4,128]{3,2,1,0:T(4,128)} %get-tuple-element.34), channel_id=1, source_target_pairs={{0,31},{1,2},{2,1},{3,4},{4,3},{5,6},{6,5},{7,8},{8,7},{9,10},{10,... | collective-permute-start | bytes 98312 | tf_op jit(solution)/shard_map/ppermute | solution.py:641
  21.6 0.9 %copy-start = (f32[16,2,8,128]{3,2,1,0:T(8,128)S(1)}, f32[16,2,8,128]{3,2,1,0:T(8,128)}, u32[]{:S(2)}) copy-start(f32[16,2,8,128]{3,2,1,0:T(8,128)} %get-tuple-element.32.whole_ref) | copy-start | bytes 393220
  23.7 9.3 %collective-permute-start.4 = (f32[5,2,16,128]{3,2,1,0:T(8,128)S(1)}, f32[5,2,16,128]{3,2,1,0:T(8,128)S(1)}, u32[]{:S(2)}, u32[]{:S(2)}) collective-permute-start(f32[5,2,16,128]{3,2,1,0:T(8,128)S(1)} %get-tuple-element.38.own_ref), channel_id=1, source_target_pairs={{0,96},{1,97},{2,98},{3,99},{4,100},{5,101},{6,102},{7,103},{8,104... | collective-permute-start | bytes 245768 | tf_op jit(solution)/shard_map/ppermute | solution.py:641
  27.7 5.9 %collective-permute-start.3 = (f32[5,2,16,128]{3,2,1,0:T(8,128)S(1)}, f32[5,2,16,128]{3,2,1,0:T(8,128)S(1)}, u32[]{:S(2)}, u32[]{:S(2)}) collective-permute-start(f32[5,2,16,128]{3,2,1,0:T(8,128)S(1)} %get-tuple-element.38.own_ref), channel_id=1, source_target_pairs={{0,64},{1,65},{2,66},{3,67},{4,68},{5,69},{6,70},{7,71},{8,72},{9,... | collective-permute-start | bytes 245768 | tf_op jit(solution)/shard_map/ppermute | solution.py:641
  28.6 5.0 %collective-permute-start.2 = (f32[5,2,16,128]{3,2,1,0:T(8,128)S(1)}, f32[5,2,16,128]{3,2,1,0:T(8,128)S(1)}, u32[]{:S(2)}, u32[]{:S(2)}) collective-permute-start(f32[5,2,16,128]{3,2,1,0:T(8,128)S(1)} %get-tuple-element.38.own_ref), channel_id=1, source_target_pairs={{0,32},{1,33},{2,34},{3,35},{4,36},{5,37},{6,38},{7,39},{8,40},{9,... | collective-permute-start | bytes 245768 | tf_op jit(solution)/shard_map/ppermute | solution.py:641
  29.6 7.6 %collective-permute-start.5 = (f32[1,2,4,128]{3,2,1,0:T(4,128)S(1)}, f32[1,2,4,128]{3,2,1,0:T(4,128)S(1)}, u32[]{:S(2)}, u32[]{:S(2)}) collective-permute-start(f32[1,2,4,128]{3,2,1,0:T(4,128)S(1)} %get-tuple-element.47), channel_id=1, source_target_pairs={{0,1},{1,0},{2,3},{3,2},{4,5},{5,4},{6,7},{7,6},{8,9},{9,8},{10,11... | collective-permute-start | bytes 12296 | tf_op jit(solution)/shard_map/ppermute | solution.py:641
  29.7 7.5 %collective-permute-start.6 = (f32[1,2,4,128]{3,2,1,0:T(4,128)S(1)}, f32[1,2,4,128]{3,2,1,0:T(4,128)S(1)}, u32[]{:S(2)}, u32[]{:S(2)}) collective-permute-start(f32[1,2,4,128]{3,2,1,0:T(4,128)S(1)} %get-tuple-element.48), channel_id=1, source_target_pairs={{0,31},{1,2},{2,1},{3,4},{4,3},{5,6},{6,5},{7,8},{8,7},{9,10},{10,... | collective-permute-start | bytes 12296 | tf_op jit(solution)/shard_map/ppermute | solution.py:641
  37.2 9.3 %collective-permute-start.9 = (f32[4,2,16,128]{3,2,1,0:T(8,128)S(1)}, f32[4,2,16,128]{3,2,1,0:T(8,128)S(1)}, u32[]{:S(2)}, u32[]{:S(2)}) collective-permute-start(f32[4,2,16,128]{3,2,1,0:T(8,128)S(1)} %widen_wall.1.refs_0_), channel_id=1, source_target_pairs={{0,96},{1,97},{2,98},{3,99},{4,100},{5,101},{6,102},{7,103},{8,104... | collective-permute-start | bytes 196616 | tf_op jit(solution)/shard_map/ppermute | solution.py:641
  39.4 7.2 %collective-permute-start.8 = (f32[4,2,16,128]{3,2,1,0:T(8,128)S(1)}, f32[4,2,16,128]{3,2,1,0:T(8,128)S(1)}, u32[]{:S(2)}, u32[]{:S(2)}) collective-permute-start(f32[4,2,16,128]{3,2,1,0:T(8,128)S(1)} %widen_wall.1.refs_0_), channel_id=1, source_target_pairs={{0,64},{1,65},{2,66},{3,67},{4,68},{5,69},{6,70},{7,71},{8,72},{9,... | collective-permute-start | bytes 196616 | tf_op jit(solution)/shard_map/ppermute | solution.py:641
  40.3 6.3 %collective-permute-start.7 = (f32[4,2,16,128]{3,2,1,0:T(8,128)S(1)}, f32[4,2,16,128]{3,2,1,0:T(8,128)S(1)}, u32[]{:S(2)}, u32[]{:S(2)}) collective-permute-start(f32[4,2,16,128]{3,2,1,0:T(8,128)S(1)} %widen_wall.1.refs_0_), channel_id=1, source_target_pairs={{0,32},{1,33},{2,34},{3,35},{4,36},{5,37},{6,38},{7,39},{8,40},{9,... | collective-permute-start | bytes 196616 | tf_op jit(solution)/shard_map/ppermute | solution.py:641
